TPU v7x, 32 devices: a whole 2x2x4 slice. The times are simulated.
32 devices in a mesh: groups: 2 (over x), wide: 16 (over z, y, core).
Axes of the slice: x: 2, y: 2, z: 4, core: 2. Of those that a mesh axis runs over, the one named last changes fastest.
Arguments:
- residual: bfloat16 [4096, 2048], P(('groups', 'wide')), parts along dimension 0, may hold values from -6 to 6
- queries: bfloat16 [4096, 2048], P(('groups', 'wide')), parts along dimension 0, may hold values from -160 to 160
- new_keys: bfloat16 [4096, 256], P(('groups', 'wide')), parts along dimension 0, may hold values from -6 to 6
- new_values: bfloat16 [4096, 256], P(('groups', 'wide')), parts along dimension 0, may hold values from -6 to 6
- cache_keys: bfloat16 [32, 2048, 256], P(('groups', 'wide')), parts along dimension 0, may hold values from -6 to 6
- cache_values: bfloat16 [32, 2048, 256], P(('groups', 'wide')), parts along dimension 0, may hold values from -6 to 6
- cache_len: int32 [32], P('groups'), parts along dimension 0, may hold values from 1 to 2048, 16384 in all
- o_weight: bfloat16 [2048, 2048], P('wide'), may hold values from -0.75 to 0.75
- norm_gain: float32 [2048], replicated, may hold values from 0.5 to 2
- expert_ids: int32 [4096, 8], P(('groups', 'wide')), parts along dimension 0, may hold values from 0 to 15, all different within a row; in each aligned block of 128 rows (0 to 127, 128 to 255, ...) at most 72 rows name the same one
- gate_raw: float32 [4096, 8], P(('groups', 'wide')), parts along dimension 0, may hold values from 0.1 to 1
- w_gate: bfloat16 [16, 2048, 768], P('wide'), may hold values from -0.125 to 0.125
- w_up: bfloat16 [16, 2048, 768], P('wide'), may hold values from -0.125 to 0.125
- w_down: bfloat16 [16, 768, 2048], P('wide'), may hold values from -0.4375 to 0.4375
Outputs:
- layer_out: bfloat16 [4096, 2048], P(('groups', 'wide')), parts along dimension 0
There are 2 independent parts, one for each index of `groups`. A program takes and returns all parts, laid end to end along the dimension named above; an argument that names none is the same for every part. Nothing has to cross between parts.
Inputs may be any that keep to these rules, and one draw needn't show every extreme that they name: `cache_len`: each span's cache holds 1 or more positions; in every part some span has a full cache of 2048 positions and the lengths sum to 16384. `expert_ids`: each token names 8 different experts; among the 128 tokens of one span no expert is named more than 72 times, and in every draw some span names some expert exactly 72 times.
All inputs are finite; a program needn't handle non-finite values.
Results may differ from a plain program's by a relative error of at most 0.01.
Values may be sent and summed in bfloat16 or wider, within the bound.
No kernel may reach another device: no remote copies, remote signals or barrier semaphores. Data moves between devices by JAX's collectives and lax.ppermute only.
A program may use at most 128 MiB of HBM per device.

v0:
```python
import jax
import jax.numpy as jnp
from jax import lax
from jax.sharding import PartitionSpec as P

D = 2048
HEADS = 16
KV_HEADS = 2
HEAD = 128
TOPK = 8
KEY_BLOCK = 512
SPAN = 128


def group_queries(query_rows):
    return query_rows.reshape(query_rows.shape[0], KV_HEADS, HEADS // KV_HEADS, HEAD)


def empty_state(token_count):
    shape = (KV_HEADS, HEADS // KV_HEADS, token_count)
    return (
        jnp.full(shape, -1e30, jnp.float32),
        jnp.zeros(shape, jnp.float32),
        jnp.zeros(shape + (HEAD,), jnp.float32),
    )


def update(state, query_four, key_block, value_block, visible):
    run_max, run_total, run_acc = state
    key_three = key_block.reshape(-1, KV_HEADS, HEAD)
    value_three = value_block.reshape(-1, KV_HEADS, HEAD)
    scores = jnp.einsum(
        "tgrd,kgd->grtk", query_four, key_three, preferred_element_type=jnp.float32
    ) * HEAD ** (-0.5)
    scores = jnp.where(visible[None, None], scores, jnp.float32(-1e30))
    new_max = jnp.maximum(run_max, jnp.max(scores, axis=-1))
    rescale = jnp.exp(run_max - new_max)
    weights = jnp.exp(scores - new_max[..., None])
    run_total = run_total * rescale + jnp.sum(weights, axis=-1)
    run_acc = run_acc * rescale[..., None] + jnp.einsum(
        "grtk,kgd->grtd",
        weights.astype(jnp.bfloat16),
        value_three,
        preferred_element_type=jnp.float32,
    )
    return (new_max, run_total, run_acc)


def cache_pass(state, query_four, key_rows, value_rows, length, offset, block_count):
    token_count = query_four.shape[0]

    def block_step(block, carried):
        first_row = block * KEY_BLOCK
        key_block = lax.dynamic_slice_in_dim(key_rows, first_row, KEY_BLOCK, 0)
        value_block = lax.dynamic_slice_in_dim(value_rows, first_row, KEY_BLOCK, 0)
        positions = offset + first_row + jnp.arange(KEY_BLOCK, dtype=jnp.int32)
        visible = jnp.broadcast_to((positions < length)[None, :], (token_count, KEY_BLOCK))
        return update(carried, query_four, key_block, value_block, visible)

    return lax.fori_loop(0, block_count, block_step, state)


def run_expert(rows_in, gate_w, up_w, down_w):
    flat_rows = rows_in.reshape(-1, rows_in.shape[-1])
    gate_part = jnp.dot(flat_rows, gate_w, preferred_element_type=jnp.float32)
    up_part = jnp.dot(flat_rows, up_w, preferred_element_type=jnp.float32)
    activated = (jax.nn.silu(gate_part) * up_part).astype(jnp.bfloat16)
    expert_rows = jnp.dot(activated, down_w, preferred_element_type=jnp.float32).astype(
        jnp.bfloat16
    )
    return expert_rows.reshape(rows_in.shape)


def per_device(
    residual,
    queries,
    new_keys,
    new_values,
    cache_keys,
    cache_values,
    cache_len,
    o_weight,
    norm_gain,
    expert_ids,
    gate_raw,
    w_gate,
    w_up,
    w_down,
):
    devices = lax.axis_size("wide")
    my_index = lax.axis_index("wide")
    token_count = queries.shape[0]
    query_four = group_queries(queries)
    key_cache = cache_keys[0]
    value_cache = cache_values[0]
    length = cache_len[my_index]
    own_blocks = (length + KEY_BLOCK - 1) // KEY_BLOCK
    token_rows = jnp.arange(token_count, dtype=jnp.int32)
    causal = token_rows[None, :] <= token_rows[:, None]
    state = update(empty_state(token_count), query_four, new_keys, new_values, causal)
    state = cache_pass(state, query_four, key_cache, value_cache, length, 0, own_blocks)
    attn_four = state[2] / state[1][..., None]
    attn = (
        jnp.transpose(attn_four, (2, 0, 1, 3))
        .reshape(token_count, HEADS * HEAD)
        .astype(jnp.bfloat16)
    )
    projected = jnp.dot(
        attn,
        lax.all_gather(o_weight, "wide", axis=0, tiled=True),
        preferred_element_type=jnp.float32,
    )
    mixed = residual.astype(jnp.float32) + projected
    normed = (
        mixed * lax.rsqrt(jnp.mean(mixed * mixed, axis=-1, keepdims=True) + 1e-06) * norm_gain
    ).astype(jnp.bfloat16)
    capacity = SPAN * TOPK // devices + max(2, SPAN * TOPK // (8 * devices))
    flat_ids = expert_ids.reshape(-1)
    one_hot = (flat_ids[:, None] == jnp.arange(devices, dtype=jnp.int32)[None, :]).astype(jnp.int32)
    ranks = jnp.sum(jnp.cumsum(one_hot, axis=0) * one_hot, axis=1) - 1
    slot_index = flat_ids * capacity + ranks
    token_of = jnp.arange(flat_ids.shape[0], dtype=jnp.int32) // TOPK
    slot_token = (
        jnp.full((devices * capacity,), token_count, jnp.int32).at[slot_index].set(token_of)
    )
    padded = jnp.concatenate([normed, jnp.zeros((1, D), jnp.bfloat16)], axis=0)
    outgoing = padded[slot_token].reshape(devices, capacity, D)
    arrived = lax.all_to_all(outgoing, "wide", split_axis=0, concat_axis=0, tiled=True)
    served = run_expert(arrived, w_gate[0], w_up[0], w_down[0])
    returned_rows = lax.all_to_all(served, "wide", split_axis=0, concat_axis=0, tiled=True)
    picked = returned_rows.reshape(devices * capacity, D)[slot_index].reshape(token_count, TOPK, D)
    shares = gate_raw / jnp.sum(gate_raw, axis=-1, keepdims=True)
    routed = jnp.sum(picked.astype(jnp.float32) * shares[..., None], axis=1)
    return (mixed + routed).astype(jnp.bfloat16)


def solution(mesh):
    placed = (
        P(("groups", "wide"), None),
        P(("groups", "wide"), None),
        P(("groups", "wide"), None),
        P(("groups", "wide"), None),
        P(("groups", "wide"), None, None),
        P(("groups", "wide"), None, None),
        P("groups"),
        P("wide", None),
        P(),
        P(("groups", "wide"), None),
        P(("groups", "wide"), None),
        P("wide", None, None),
        P("wide", None, None),
        P("wide", None, None),
    )
    return jax.shard_map(
        per_device,
        mesh=mesh,
        in_specs=placed,
        out_specs=P(("groups", "wide"), None),
        check_vma=False,
    )
```

profile of v0, /device:TPU:13, one launch (start us, length us, event | category | flops | bytes accessed | tf_op | source)
XLA Modules:
  0.0 361.1 jit_solution(6615246310391238780)
XLA Ops:
  7.3 1.5 dynamic_slice.9
  10.5 2.0 copy.25
  13.4 0.9 reshape.118
  14.2 2.0 copy.32
  16.3 2.3 copy.30
  18.6 2.3 copy.31
  20.9 1.3 fusion.37
  22.5 1.5 convolution_add_fusion.1
  24.0 7.5 %while.14 = (s32[]{:T(128)}, f32[2,8,128]{2,1,0:T(8,128)S(1)}, f32[2,8,128]{2,1,0:T(8,128)S(1)}, f32[2,8,128,128]{3,2,1,0:T(8,128)}, s32[]{:T(128)}, /*index=5*/...) while((s32[]{:T(128)}, f32[2,8,128]{2,1,0:T(8,128)S(1)}, ...), condition=%wide.region_5.6_spmd, body=%wide.region_2.5_spmd.sunk | while | flops 548934656 | bytes 25299184 | solution.py:60
  24.0 1.1 constant_dynamic-slice_fusion.3
  25.7 2.2 bitcast_reduce_fusion.2
  28.0 0.9 fusion.57
  28.9 1.6 fusion.58
  30.5 1.0 copy-done.4
  31.5 2.6 copy.33
  34.1 4.5 %reduce-window.6 = s32[16,8,128]{2,1,0:T(8,128)S(1)} reduce-window(s32[16,8,128]{2,1,0:T(8,128)S(1)} %fusion.30, s32[]{:T(128)} %constant.46.clone.1), window={size=1x1x128 pad=0_0x0_0x127_0}, to_apply=%region_7.8 | reduce-window | flops 2080768 | bytes 131076 | tf_op jit(solution)/shard_map/reduce-window
  39.3 4.3 %scatter_custom_fusion = s32[1152]{0:T(1024)S(1)} fusion(s32[1024]{0:T(1024)S(1)} %bitcast.107, s32[1024]{0:T(1024)S(1)} %add_select_fusion, s32[]{:T(128)} %constant.87.clone.1), kind=kCustom, calls=%fused_computation.64 | custom fusion | bytes 4612 | tf_op jit(solution)/shard_map/scatter | solution.py:124
  43.7 2.2 divide_convert_fusion
  45.8 38.6 %all-gather.2.cloned.1.call-done = bf16[2048,2048]{1,0:T(8,128)(2,1)} async-done(((bf16[128,2048]{1,0:T(8,128)(2,1)}), bf16[2048,2048]{1,0:T(8,128)(2,1)}) %all-gather.2.cloned.1.call-update) | async-done | bytes 8388624 | tf_op jit(solution)/shard_map/all_gather | solution.py:110
  84.5 4.9 %multiply_reduce_fusion = (f32[128]{0:T(128)S(1)}, f32[128,2048]{1,0:T(8,128)S(1)}) fusion(bf16[128,2048]{0,1:T(8,128)(2,1)} %bitcast.102, bf16[2048,2048]{1,0:T(8,128)(2,1)} %all-gather.2.cloned.1.call-done, bf16[128,2048]{1,0:T(8,128)(2,1)} %param.16), kind=kOutput, calls=%fused_computation.38 | convolution fusion | flops 1074790272 | bytes 10486272 | tf_op jit(solution)/shard_map/dot_general | solution.py:108
  89.4 1.0 copy-done.1
  90.6 0.9 concatenate.3
  91.4 11.8 %gather_fusion = bf16[1152,2048]{1,0:T(8,128)(2,1)} fusion(bf16[129,2048]{1,0:T(8,128)(2,1)} %concatenate.3, s32[2048]{0:T(1024)S(1)} %pad_clamp_fusion), kind=kCustom, calls=%fused_computation | custom fusion | bytes 9441792 | tf_op jit(solution)/shard_map/gather | solution.py:127
  103.2 109.3 %all_to_all.10 = bf16[16,72,2048]{2,1,0:T(8,128)(2,1)S(1)} all-to-all(bf16[16,72,2048]{2,1,0:T(8,128)(2,1)} %bitcast.93), channel_id=1, replica_groups=mesh['groups'=2,'wide'=16] {'wide'}, dimensions={0} | all-to-all | bytes 9437184 | tf_op jit(solution)/shard_map/all_to_all | solution.py:128
  212.5 3.9 %fusion.18 = f32[1152,768]{1,0:T(8,128)S(1)} fusion(bf16[1152,2048]{1,0:T(8,128)(2,1)S(1)} %bitcast.100, bf16[1,2048,768]{2,1,0:T(8,128)(2,1)S(1)} %copy-done.8), kind=kOutput, calls=%fused_computation.29 | convolution fusion | flops 3623878656 | bytes 11403264 | tf_op jit(solution)/shard_map/dot_general | solution.py:65
  216.4 4.2 %fusion.15 = bf16[1152,768]{1,0:T(8,128)(2,1)S(1)} fusion(bf16[1152,2048]{1,0:T(8,128)(2,1)S(1)} %bitcast.101, f32[1152,768]{1,0:T(8,128)S(1)} %fusion.18, bf16[1,2048,768]{2,1,0:T(8,128)(2,1)S(1)} %copy-done.9), kind=kOutput, calls=%fused_computation.26 | convolution fusion | flops 3629187072 | bytes 13172736 | tf_op jit(solution)/shard_map/dot_general | solution.py:66
  220.6 5.5 %convolution_convert_fusion = bf16[1152,2048]{1,0:T(8,128)(2,1)} fusion(bf16[1152,768]{1,0:T(8,128)(2,1)S(1)} %fusion.15, bf16[1,768,2048]{2,1,0:T(8,128)(2,1)S(1)} %copy-done), kind=kOutput, calls=%fused_computation.24 | convolution fusion | flops 3626237952 | bytes 9633792 | tf_op jit(solution)/shard_map/dot_general | solution.py:68
  226.1 5.0 %all-to-all-start.1 = ((bf16[16,72,2048]{2,1,0:T(8,128)(2,1)}), bf16[16,72,2048]{2,1,0:T(8,128)(2,1)}, u32[]{:S(2)}, u32[]{:S(2)}) async-start(bf16[16,72,2048]{2,1,0:T(8,128)(2,1)} %bitcast.99), calls=%async_computation.1 | async-start | bytes 9437184 | tf_op jit(solution)/shard_map/all_to_all | solution.py:130
  231.3 103.6 %all-to-all-done.1 = bf16[16,72,2048]{2,1,0:T(8,128)(2,1)} async-done(((bf16[16,72,2048]{2,1,0:T(8,128)(2,1)}), bf16[16,72,2048]{2,1,0:T(8,128)(2,1)}, u32[]{:S(2)}, u32[]{:S(2)}) %all-to-all-start.1) | async-done | bytes 4718624 | tf_op jit(solution)/shard_map/all_to_all | solution.py:130
  334.9 11.8 %gather_fusion.1 = bf16[1024,2048]{1,0:T(8,128)(2,1)} fusion(bf16[1152,2048]{1,0:T(8,128)(2,1)} %bitcast.24, s32[1024]{0:T(1024)S(1)} %broadcast_clamp_fusion), kind=kCustom, calls=%fused_computation.1 | custom fusion | bytes 8392704 | tf_op jit(solution)/shard_map/gather | solution.py:131
  346.7 6.6 %fusion.14 = f32[128,2048]{1,0:T(8,128)S(1)} fusion(bf16[1024,2048]{1,0:T(8,128)(2,1)} %gather_fusion.1, f32[128,8]{1,0:T(8,128)S(1)} %copy.39), kind=kLoop, calls=%fused_computation.23 | loop fusion | flops 6029312 | bytes 5246976 | tf_op jit(solution)/shard_map/reduce_sum | solution.py:133
  353.3 0.9 add_convert_fusion
  (54 shorter events, 4.4 us)
Async XLA Ops:
  6.5 214.0 %copy-start = (bf16[1,768,2048]{2,1,0:T(8,128)(2,1)S(1)}, bf16[1,768,2048]{2,1,0:T(8,128)(2,1)}, u32[]{:S(2)}) copy-start(bf16[1,768,2048]{2,1,0:T(8,128)(2,1)} %param.29) | copy-start | bytes 9437188
  6.5 77.9 %all-gather.2.cloned.1.call-start = ((), (), s32[]{:S(2)}) async-start(), calls=%async_computation.2 | async-start | bytes 8912896 | tf_op jit(solution)/shard_map/all_gather | solution.py:110
  24.0 15.0 %copy-start.5 = (s32[128,8]{0,1:T(8,128)S(1)}, s32[128,8]{0,1:T(8,128)}, u32[]{:S(2)}) copy-start(s32[128,8]{0,1:T(8,128)} %param.25) | copy-start | bytes 12292
  25.7 3.2 copy-start.3
  30.5 1.0 copy-start.4
  84.5 5.9 %copy-start.7 = (f32[2048]{0:T(1024)S(1)}, f32[2048]{0:T(1024)}, u32[]{:S(2)}) copy-start(f32[2048]{0:T(1024)} %param.24) | copy-start | bytes 24580
  89.4 1.0 copy-start.1
  103.2 109.3 %copy-start.8 = (bf16[1,2048,768]{2,1,0:T(8,128)(2,1)S(1)}, bf16[1,2048,768]{2,1,0:T(8,128)(2,1)}, u32[]{:S(2)}) copy-start(bf16[1,2048,768]{2,1,0:T(8,128)(2,1)} %param.27) | copy-start | bytes 9437188
  212.5 3.9 %copy-start.9 = (bf16[1,2048,768]{2,1,0:T(8,128)(2,1)S(1)}, bf16[1,2048,768]{2,1,0:T(8,128)(2,1)}, u32[]{:S(2)}) copy-start(bf16[1,2048,768]{2,1,0:T(8,128)(2,1)} %param.28) | copy-start | bytes 9437188
  226.1 5.0 %copy-start.6 = (f32[128,8]{0,1:T(8,128)S(1)}, f32[128,8]{0,1:T(8,128)}, u32[]{:S(2)}) copy-start(f32[128,8]{0,1:T(8,128)} %param.26) | copy-start | bytes 12292
  226.1 108.7 %all-to-all-start.1 = ((bf16[16,72,2048]{2,1,0:T(8,128)(2,1)}), bf16[16,72,2048]{2,1,0:T(8,128)(2,1)}, u32[]{:S(2)}, u32[]{:S(2)}) async-start(bf16[16,72,2048]{2,1,0:T(8,128)(2,1)} %bitcast.99), calls=%async_computation.1 | async-start | bytes 9437184 | tf_op jit(solution)/shard_map/all_to_all | solution.py:130
  346.7 6.6 %copy-start.2 = (f32[128,2048]{1,0:T(8,128)S(1)}, f32[128,2048]{1,0:T(8,128)}, u32[]{:S(2)}) copy-start(f32[128,2048]{1,0:T(8,128)} %copy-done.1) | copy-start | bytes 3145732
Sparse Core Ops, SparseCore 0:
  9.5 74.9 all-gather.1
where the time goes:
time: 362 us; the launch traced here: 361 us
  waiting for transfers between devices  143 us (40%)
  blocking collectives  109 us (30%)
  local copies, waits for them, and re-layouts  48 us (13%)
  matrix products  25.2 us (7%)
  other arithmetic  16.3 us (5%)
  between operations  14.3 us (4%)
  starting transfers between devices  5.04 us (1%)
    all_to_all x1, blocking collectives, per_device(): lax.all_to_all(outgoing, 'wide', split_axis=0, concat_axis=0, tiled=True)  109 us
    all_to_all x1, waiting for transfers between devices, per_device(): lax.all_to_all(served, 'wide', split_axis=0, concat_axis=0, tiled=True)  104 us
    all_gather x1, waiting for transfers between devices, per_device(): lax.all_gather(o_weight, 'wide', axis=0, tiled=True)  38.6 us
    gather x1, local copies, waits for them, and re-layouts, per_device(): returned_rows.reshape(devices * capacity, D)[slot_index]  11.8 us
    gather x1, local copies, waits for them, and re-layouts, per_device(): outgoing = padded[slot_token].reshape(devices, capacity, D)  11.8 us
    unnamed x20, local copies, waits for them, and re-layouts  8.47 us
  transfers between devices with their start and end apart: 2, of which 2 were waited for; matrix products, arithmetic and copies ran while one was open for 10% of the time, Pallas kernels for 0%

commit v1 on v0

v1 whole, which is shorter than its diff:
```python
import functools

import jax
import jax.numpy as jnp
from jax import lax
from jax.experimental import pallas as pl
from jax.experimental.pallas import tpu as pltpu
from jax.sharding import PartitionSpec as P

HEAD = 128
KEY_BLOCK = 512
ROW_BLOCK = 256
LOG2E = 1.4426950408889634
NEG = -1e30
MIB = 1 << 20

VMEM = pl.BlockSpec(memory_space=pltpu.VMEM)
SMEM = pl.BlockSpec(memory_space=pltpu.SMEM)
ANY = pl.BlockSpec(memory_space=pl.ANY)


def dot(a, b):
    return jnp.dot(a, b, preferred_element_type=jnp.float32)


def attention_kernel(len_ref, q_ref, nk_ref, nv_ref, k_ref, v_ref, o_ref):
    tokens = q_ref.shape[0]
    heads = q_ref.shape[1] // HEAD
    per_chunk = ROW_BLOCK // tokens
    length = len_ref[0]
    blocks = (length + KEY_BLOCK - 1) // KEY_BLOCK
    scale = jnp.float32(HEAD**-0.5 * LOG2E)

    def scores_of(q, k):
        return lax.dot_general(q, k, (((1,), (1,)), ((), ())), preferred_element_type=jnp.float32)

    for chunk in range(heads // per_chunk):
        cols = [pl.ds((chunk * per_chunk + i) * HEAD, HEAD) for i in range(per_chunk)]
        q = jnp.concatenate([q_ref[:, c] for c in cols], axis=0)

        def step(s, state, v):
            m, l, acc = state
            new_m = jnp.maximum(m, jnp.max(s, axis=1, keepdims=True))
            w = jnp.exp2((s - new_m) * scale)
            fade = jnp.exp2((m - new_m) * scale)
            l = l * fade + jnp.sum(w, axis=1, keepdims=True)
            acc = acc * fade + dot(w.astype(jnp.bfloat16), v)
            return new_m, l, acc

        s = scores_of(q, nk_ref[...])
        row = lax.broadcasted_iota(jnp.int32, s.shape, 0) % tokens
        col = lax.broadcasted_iota(jnp.int32, s.shape, 1)
        s = jnp.where(col <= row, s, NEG)
        m = jnp.max(s, axis=1, keepdims=True)
        w = jnp.exp2((s - m) * scale)
        state = (m, jnp.sum(w, axis=1, keepdims=True), dot(w.astype(jnp.bfloat16), nv_ref[...]))

        def body(i, state):
            rows = pl.ds(pl.multiple_of(i * KEY_BLOCK, KEY_BLOCK), KEY_BLOCK)
            s = scores_of(q, k_ref[rows, :])
            pos = i * KEY_BLOCK + lax.broadcasted_iota(jnp.int32, s.shape, 1)
            s = jnp.where(pos < length, s, NEG)
            return step(s, state, v_ref[rows, :])

        m, l, acc = lax.fori_loop(0, blocks, body, state)
        out = (acc / l).astype(jnp.bfloat16)
        for i in range(per_chunk):
            o_ref[:, cols[i]] = out[i * tokens : (i + 1) * tokens, :]


def attention(length, queries, new_keys, new_values, keys, values):
    tokens, width = queries.shape
    kv_heads = new_keys.shape[1] // HEAD
    group = width // kv_heads
    cache = keys.shape[0]
    return pl.pallas_call(
        attention_kernel,
        grid=(kv_heads,),
        in_specs=[
            SMEM,
            pl.BlockSpec((tokens, group), lambda g: (0, g)),
            pl.BlockSpec((tokens, HEAD), lambda g: (0, g)),
            pl.BlockSpec((tokens, HEAD), lambda g: (0, g)),
            pl.BlockSpec((cache, HEAD), lambda g: (0, g)),
            pl.BlockSpec((cache, HEAD), lambda g: (0, g)),
        ],
        out_specs=pl.BlockSpec((tokens, group), lambda g: (0, g)),
        out_shape=jax.ShapeDtypeStruct((tokens, width), jnp.bfloat16),
        compiler_params=pltpu.CompilerParams(vmem_limit_bytes=40 * MIB),
        cost_estimate=pl.CostEstimate(
            flops=4 * tokens * width * cache,
            bytes_accessed=4 * cache * HEAD * kv_heads,
            transcendentals=tokens * width // HEAD * cache,
        ),
        name="attention",
    )(length, queries, new_keys, new_values, keys, values)


def projection_kernel(n_blocks, base_ref, mine_ref, peer_ref, *refs):
    w_refs = refs[: n_blocks + 1]
    own_ref, other_ref, left, weight, sems = refs[n_blocks + 1 :]
    tokens = mine_ref.shape[0]
    rows = weight.shape[0] // n_blocks // 2
    half = weight.shape[1] // 2
    copies = []
    for b in range(n_blocks + 1):
        for part in range(2):
            at = pl.multiple_of(base_ref[2 * min(b, n_blocks - 1) + part], rows)
            src = w_refs[b].at[pl.ds(part * rows, rows)]
            if b < n_blocks - 1:
                dst = weight.at[pl.ds(at, rows)]
            else:
                dst = weight.at[pl.ds(at, rows), pl.ds((b - n_blocks + 1) * half, half)]
            copies.append(pltpu.make_async_copy(src, dst, sems.at[2 * b + part]))
            copies[-1].start()
    left[0:tokens] = mine_ref[...]
    left[tokens : 2 * tokens] = peer_ref[...]
    for copy in copies:
        copy.wait()
    step = 256

    def body(i, carry):
        cols = pl.ds(pl.multiple_of(i * step, step), step)
        both = dot(left[...], weight[:, cols])
        own_ref[:, cols] = both[:tokens]
        other_ref[:, cols] = both[tokens:]
        return carry

    lax.fori_loop(0, weight.shape[1] // step, body, 0)


def projection(bases, mine, peer, blocks):
    tokens, width = mine.shape
    n_blocks = len(blocks) - 1
    cols = blocks[0].shape[1]
    out = jax.ShapeDtypeStruct((tokens, cols), jnp.float32)
    return pl.pallas_call(
        functools.partial(projection_kernel, n_blocks),
        in_specs=[SMEM, VMEM, VMEM] + [ANY] * len(blocks),
        out_specs=[VMEM, VMEM],
        out_shape=[out, out],
        scratch_shapes=[
            pltpu.VMEM((2 * tokens, width), jnp.bfloat16),
            pltpu.VMEM((width, cols), jnp.bfloat16),
            pltpu.SemaphoreType.DMA((2 * n_blocks + 2,)),
        ],
        compiler_params=pltpu.CompilerParams(vmem_limit_bytes=40 * MIB),
        cost_estimate=pl.CostEstimate(
            flops=4 * tokens * width * cols, bytes_accessed=2 * width * cols, transcendentals=0
        ),
        name="projection",
    )(bases, mine, peer, *blocks)


def norm_kernel(core_ref, residual_ref, gain_ref, own_ref, recv_ref, mixed_ref, normed_ref):
    half = own_ref.shape[1]
    width = residual_ref.shape[1]
    core = core_ref[0]
    own_cols = pl.ds(pl.multiple_of(core * half, half), half)
    recv_cols = pl.ds(pl.multiple_of((1 - core) * half, half), half)
    a = residual_ref[:, own_cols].astype(jnp.float32) + own_ref[...]
    b = residual_ref[:, recv_cols].astype(jnp.float32) + recv_ref[...]
    mixed_ref[:, own_cols] = a
    mixed_ref[:, recv_cols] = b
    total = jnp.sum(a * a, axis=1, keepdims=True) + jnp.sum(b * b, axis=1, keepdims=True)
    factor = lax.rsqrt(total / width + 1e-06)
    normed_ref[:, own_cols] = (a * factor * gain_ref[:, own_cols]).astype(jnp.bfloat16)
    normed_ref[:, recv_cols] = (b * factor * gain_ref[:, recv_cols]).astype(jnp.bfloat16)


def mix_and_norm(core, residual, gain, own, recv):
    return pl.pallas_call(
        norm_kernel,
        in_specs=[SMEM, VMEM, VMEM, VMEM, VMEM],
        out_specs=[VMEM, VMEM],
        out_shape=[
            jax.ShapeDtypeStruct(residual.shape, jnp.float32),
            jax.ShapeDtypeStruct(residual.shape, jnp.bfloat16),
        ],
        compiler_params=pltpu.CompilerParams(vmem_limit_bytes=32 * MIB),
        name="mix_and_norm",
    )(core, residual, gain, own, recv)


def experts_kernel(pairs, n_in, n_out, slots, slot_rows, slot_cols, share_rows, *refs):
    x_refs = refs[:n_in]
    w_refs = refs[n_in : n_in + 6]
    out_refs = refs[n_in + 6 : n_in + 6 + n_out]
    xs, wg, wu, wd, rows_in, acc, scaled, x_sem, w_sem = refs[n_in + 6 + n_out :]
    depth = xs.shape[1]
    pair_tokens = xs.shape[0] // pairs
    block = pair_tokens // 2
    steps = wg.shape[0]
    ff = wg.shape[2]
    chunks = steps // 2

    x_copies = []
    at, col = 0, 0
    for i in range(n_in):
        wide = x_refs[i].shape[1]
        dst = xs.at[pl.ds(at, block), pl.ds(col, wide)]
        x_copies.append(pltpu.make_async_copy(x_refs[i], dst, x_sem.at[i]))
        x_copies[-1].start()
        col += wide
        if col == depth:
            at, col = at + block, 0
    for s in range(steps):
        e, f = s // chunks, s % chunks
        cut = pl.ds(f * ff, ff)
        pltpu.make_async_copy(w_refs[3 * e].at[:, cut], wg.at[s], w_sem.at[s, 0]).start()
        pltpu.make_async_copy(w_refs[3 * e + 1].at[:, cut], wu.at[s], w_sem.at[s, 1]).start()
        pltpu.make_async_copy(w_refs[3 * e + 2].at[cut, :], wd.at[s], w_sem.at[s, 2]).start()
    for copy in x_copies:
        copy.wait()

    step_cols = 512
    shares = []
    for p in range(pairs):
        row = lax.broadcasted_iota(jnp.int32, (2 * slots, pair_tokens), 0)
        first = row == slot_rows[p, 0:1, :]
        second = row - slots == slot_rows[p, 1:2, :]
        pick = jnp.where(first | second, 1.0, 0.0).astype(jnp.bfloat16)
        weight = jnp.where(first, share_rows[p, 0:1, :], 0.0) + jnp.where(
            second, share_rows[p, 1:2, :], 0.0
        )
        shares.append(jnp.sum(weight, axis=1, keepdims=True))

        def gather(i, carry, p=p, pick=pick):
            cols = pl.ds(pl.multiple_of(i * step_cols, step_cols), step_cols)
            got = dot(pick, xs[p * pair_tokens : (p + 1) * pair_tokens, cols]).astype(jnp.bfloat16)
            rows_in[0, p * slots : (p + 1) * slots, cols] = got[:slots]
            rows_in[1, p * slots : (p + 1) * slots, cols] = got[slots:]
            return carry

        lax.fori_loop(0, depth // step_cols, gather, 0)

    def expert(s, carry):
        e = s // chunks
        for k, ref in enumerate((wg, wu, wd)):
            pltpu.make_async_copy(ref.at[s], ref.at[s], w_sem.at[s, k]).wait()
        x = rows_in[e]
        gate = dot(x, wg[s])
        up = dot(x, wu[s])
        act = (gate / (1.0 + jnp.exp(-gate)) * up).astype(jnp.bfloat16)

        @pl.when(s % chunks == 0)
        def _():
            acc[e] = dot(act, wd[s])

        @pl.when(s % chunks != 0)
        def _():
            acc[e] += dot(act, wd[s])

        return carry

    lax.fori_loop(0, steps, expert, 0)

    at, col, o = 0, 0, 0
    for p in range(pairs):
        for e in range(2):
            part = shares[p][e * slots : (e + 1) * slots]
            scaled[e * slots : (e + 1) * slots, :] = (
                acc[e, p * slots : (p + 1) * slots, :] * part
            ).astype(jnp.bfloat16)
        lane = lax.broadcasted_iota(jnp.int32, (pair_tokens, 2 * slots), 1)
        back = (lane == slot_cols[p, :, 0:1]) | (lane - slots == slot_cols[p, :, 1:2])
        back = jnp.where(back, 1.0, 0.0).astype(jnp.bfloat16)
        for b in range(2):
            start = 0
            while start < depth:
                wide = out_refs[o].shape[1]

                def combine(i, carry, o=o, start=start, b=b, back=back):
                    src = pl.ds(pl.multiple_of(start + i * step_cols, step_cols), step_cols)
                    dst = pl.ds(pl.multiple_of(i * step_cols, step_cols), step_cols)
                    out_refs[o][:, dst] = dot(
                        back[b * block : (b + 1) * block], scaled[:, src]
                    ).astype(jnp.bfloat16)
                    return carry

                lax.fori_loop(0, wide // step_cols, combine, 0)
                start += wide
                o += 1


def experts(slots, slot_rows, slot_cols, share_rows, x_parts, weights, out_widths):
    pairs = slot_rows.shape[0]
    pair_tokens = slot_rows.shape[2]
    block = pair_tokens // 2
    depth, hidden = weights[0].shape
    ff = 256 if hidden % 256 == 0 else hidden
    chunks = hidden // ff
    n_in, n_out = len(x_parts), len(out_widths)
    return pl.pallas_call(
        functools.partial(experts_kernel, pairs, n_in, n_out, slots),
        in_specs=[VMEM, VMEM, VMEM] + [ANY] * (n_in + 6),
        out_specs=[VMEM] * n_out,
        out_shape=[jax.ShapeDtypeStruct((block, w), jnp.bfloat16) for w in out_widths],
        scratch_shapes=[
            pltpu.VMEM((pairs * pair_tokens, depth), jnp.bfloat16),
            pltpu.VMEM((2 * chunks, depth, ff), jnp.bfloat16),
            pltpu.VMEM((2 * chunks, depth, ff), jnp.bfloat16),
            pltpu.VMEM((2 * chunks, ff, depth), jnp.bfloat16),
            pltpu.VMEM((2, pairs * slots, depth), jnp.bfloat16),
            pltpu.VMEM((2, pairs * slots, depth), jnp.float32),
            pltpu.VMEM((2 * slots, depth), jnp.bfloat16),
            pltpu.SemaphoreType.DMA((n_in,)),
            pltpu.SemaphoreType.DMA((2 * chunks, 3)),
        ],
        compiler_params=pltpu.CompilerParams(vmem_limit_bytes=56 * MIB),
        cost_estimate=pl.CostEstimate(
            flops=12 * pairs * slots * depth * hidden,
            bytes_accessed=12 * depth * hidden,
            transcendentals=0,
        ),
        name="experts",
    )(slot_rows, slot_cols, share_rows, *x_parts, *weights)


def permutations(devices):
    cores = 2
    rows = 2
    ring = devices // (cores * rows)

    def index(z, y, c):
        return (z % ring * rows + y) * cores + c

    places = [(z, y, c) for z in range(ring) for y in range(rows) for c in range(cores)]
    forward = [(index(z, y, c), index(z + 1, y, c)) for z, y, c in places]
    backward = [(index(z, y, c), index(z + ring - 1, y, c)) for z, y, c in places]
    across = [(index(z, y, c), index(z, 1 - y, c)) for z, y, c in places]
    cores_swap = [(index(z, y, c), index(z, y, 1 - c)) for z, y, c in places]
    return ring, forward, backward, across, cores_swap


def per_device(
    residual,
    queries,
    new_keys,
    new_values,
    cache_keys,
    cache_values,
    cache_len,
    o_weight,
    norm_gain,
    expert_ids,
    gate_raw,
    w_gate,
    w_up,
    w_down,
):
    devices = lax.axis_size("wide")
    me = lax.axis_index("wide")
    tokens, depth = residual.shape
    top = expert_ids.shape[1]
    half = depth // 2
    ring, forward, backward, across, cores_swap = permutations(devices)
    core = me % 2
    row = me // 2 % 2
    place = me // 4

    send_forward = functools.partial(lax.ppermute, axis_name="wide", perm=forward)
    send_backward = functools.partial(lax.ppermute, axis_name="wide", perm=backward)
    send_across = functools.partial(lax.ppermute, axis_name="wide", perm=across)
    send_core = functools.partial(lax.ppermute, axis_name="wide", perm=cores_swap)

    def gather_blocks(own):
        same, other = [own], []
        for r in range(1, ring):
            same.append(send_forward(same[-1]))
        for r in range(ring - 1):
            other.append(send_across(same[r]))
        cut = own.shape[1] // 2
        if ring > 1:
            last = [send_across(same[-1][:, :cut]), send_forward(other[-1][:, cut:])]
        else:
            last = [send_across(own[:, :cut]), send_across(own[:, cut:])]
        return same, other, last

    mine_w = [w_gate[0], w_up[0], w_down[0]]

    keep = lax.dynamic_slice_in_dim(o_weight, core * half, half, 1)
    give = lax.dynamic_slice_in_dim(o_weight, (1 - core) * half, half, 1)
    own_block = jnp.concatenate([keep, send_core(give)], axis=0)
    w_same, w_other, w_last = gather_blocks(own_block)
    peer_w = [send_core(w) for w in mine_w]

    shares = gate_raw / jnp.sum(gate_raw, axis=-1, keepdims=True)
    table = jnp.concatenate([expert_ids.astype(jnp.float32).T, shares.T], axis=0)
    tables = lax.all_gather(table, "wide", axis=0, tiled=False)
    offsets = jnp.arange(ring, dtype=jnp.int32)
    rings = (place - offsets) % ring
    same_src = rings * 2 + row
    other_src = rings * 2 + 1 - row
    cap = tokens * top // devices + max(2, tokens * top // (8 * devices))
    slots = -(-2 * cap // 16) * 16

    order = jnp.stack([same_src, other_src], axis=0).reshape(2, ring // 2, 2).transpose(1, 0, 2)
    picked = tables[(order * 2 + core).reshape(-1)]
    ids = picked[:, :top]
    served = jnp.stack([me, me ^ 1]).astype(jnp.float32)
    hit = ids[:, None] == served[None, :, None, None]
    share_te = jnp.sum(jnp.where(hit, picked[:, None, top:], 0.0), axis=2)
    mask = jnp.any(hit, axis=2)
    before = (jnp.arange(tokens)[:, None] < jnp.arange(tokens)[None, :]).astype(jnp.bfloat16)
    rank = dot(mask.astype(jnp.bfloat16).reshape(-1, tokens), before).reshape(mask.shape)
    base = (jnp.arange(mask.shape[0], dtype=jnp.int32) % 2 * cap)[:, None, None]
    slot = jnp.where(mask, rank.astype(jnp.int32) + base, -(1 << 20))

    def by_pair(a):
        return a.reshape(ring, 2, 2, tokens).transpose(0, 2, 1, 3).reshape(ring, 2, 2 * tokens)

    slot_rows = by_pair(slot)
    share_rows = by_pair(share_te)
    slot_cols = slot_rows.transpose(0, 2, 1)

    length = lax.dynamic_slice_in_dim(cache_len, me, 1, 0)
    attn = attention(length, queries, new_keys, new_values, cache_keys[0], cache_values[0])
    attn_peer = send_core(attn)

    first_of = jnp.concatenate([same_src, other_src]) * 2
    bases = jnp.stack([first_of + core, first_of + 1 - core], axis=1).reshape(-1)
    own_part, other_part = projection(
        bases * o_weight.shape[0], attn, attn_peer, w_same + w_other + w_last
    )
    mixed, normed = mix_and_norm(
        core.astype(jnp.int32).reshape(1),
        residual,
        norm_gain.reshape(1, -1),
        own_part,
        send_core(other_part),
    )

    x_same, x_other, x_last = gather_blocks(normed)

    p_parts, q_parts, q_last = [], [], None
    for r in range(0, ring, 2):
        final = r + 2 == ring
        second = x_last if final else [x_other[r + 1]]
        x_parts = [x_same[r], x_same[r + 1], x_other[r]] + second
        widths = [depth] * 3 + ([half, half] if final else [depth])
        outs = experts(
            slots,
            slot_rows[r : r + 2],
            slot_cols[r : r + 2],
            share_rows[r : r + 2],
            x_parts,
            mine_w + peer_w,
            widths,
        )
        p_parts += [outs[0], outs[1]]
        q_parts += [outs[2]]
        if final:
            q_last = [outs[3], outs[4]]
        else:
            q_parts += [outs[3]]

    def add(*terms):
        total = terms[0].astype(jnp.float32)
        for term in terms[1:]:
            total = total + term.astype(jnp.float32)
        return total.astype(jnp.bfloat16)

    from_row = send_across(q_last[0])
    from_ring = send_backward(q_last[1])
    moving = jnp.concatenate(
        [add(p_parts[-1][:, :half], from_row), p_parts[-1][:, half:]], axis=1
    )
    for r in range(ring - 2, -1, -1):
        q = q_parts[r]
        if r == ring - 2:
            q = jnp.concatenate([q[:, :half], add(q[:, half:], from_ring)], axis=1)
        from_row = send_across(q)
        came = send_backward(moving)
        if r > 0:
            moving = add(p_parts[r], from_row, came)
    total = (
        mixed
        + p_parts[0].astype(jnp.float32)
        + from_row.astype(jnp.float32)
        + came.astype(jnp.float32)
    )
    return total.astype(jnp.bfloat16)


def solution(mesh):
    placed = (
        P(("groups", "wide"), None),
        P(("groups", "wide"), None),
        P(("groups", "wide"), None),
        P(("groups", "wide"), None),
        P(("groups", "wide"), None, None),
        P(("groups", "wide"), None, None),
        P("groups"),
        P("wide", None),
        P(),
        P(("groups", "wide"), None),
        P(("groups", "wide"), None),
        P("wide", None, None),
        P("wide", None, None),
        P("wide", None, None),
    )
    return jax.shard_map(
        per_device,
        mesh=mesh,
        in_specs=placed,
        out_specs=P(("groups", "wide"), None),
        check_vma=False,
    )
```

time: 362 us -> 284 us (0.78)
  the two profiles are of different devices: /device:TPU:13 before, /device:TPU:0 now
where the time goes in v1:
time: 284 us; the launch traced here: 282 us
  waiting for transfers between devices  137 us (48%)
  Pallas kernels  61.4 us (22%)
  blocking collectives  27.6 us (10%)
  starting transfers between devices  26.9 us (9%)
  local copies, waits for them, and re-layouts  20.1 us (7%)
  other arithmetic  8.08 us (3%)
    ppermute x6, waiting for transfers between devices, gather_blocks(): same.append(send_forward(same[-1]))  57 us
    pallas_call x2, Pallas kernels, experts(): pl.pallas_call(functools.partial(experts_kernel, pairs, n_in, n_out, slot...  47.3 us
    ppermute x6, waiting for transfers between devices, gather_blocks(): other.append(send_across(same[r]))  34.1 us
    all_gather x1, blocking collectives, per_device(): tables = lax.all_gather(table, 'wide', axis=0, tiled=False)  27.6 us
    ppermute x4, waiting for transfers between devices, gather_blocks(): last = [send_across(same[-1][:, :cut]), send_forward(other[-1][:, cut:])]  14.6 us
    ppermute x3, waiting for transfers between devices, per_device(): came = send_backward(moving)  13.1 us
    ppermute x6, starting transfers between devices, gather_blocks(): other.append(send_across(same[r]))  12.7 us
    pallas_call x1, Pallas kernels, attention(): pl.pallas_call(attention_kernel, grid=(kv_heads,), in_specs=[SMEM, pl.Blo...  9.14 us
  transfers between devices with their start and end apart: 30, of which 20 were waited for; matrix products, arithmetic and copies ran while one was open for 7% of the time, Pallas kernels for 13%

profile of v1, /device:TPU:0, one launch (start us, length us, event | category | flops | bytes accessed | tf_op | source)
XLA Modules:
  0.0 281.8 jit_solution(10635536991695815222)
XLA Ops:
  2.8 3.0 %collective-permute-start.2 = (bf16[256,1024]{1,0:T(8,128)(2,1)S(1)}, bf16[256,1024]{1,0:T(8,128)(2,1)S(1)}, u32[]{:S(2)}, u32[]{:S(2)}) collective-permute-start(bf16[256,1024]{1,0:T(8,128)(2,1)S(1)} %pad_maximum_fusion.refs_0_), channel_id=1, source_target_pairs={{0,4},{1,5},{2,6},{3,7},{4,8},{5,9},{6,10},{7,11},{8,12},{9,13},{1... | collective-permute-start | bytes 1572872 | tf_op jit(solution)/shard_map/ppermute | solution.py:370
  5.8 14.2 %collective-permute-done.2.refs_1_ = bf16[256,1024]{1,0:T(8,128)(2,1)S(1)} collective-permute-done((bf16[256,1024]{1,0:T(8,128)(2,1)S(1)}, bf16[256,1024]{1,0:T(8,128)(2,1)S(1)}, u32[]{:S(2)}, u32[]{:S(2)}) %collective-permute-start.2) | collective-permute-done | bytes 524320 | tf_op jit(solution)/shard_map/ppermute | solution.py:370
  21.3 14.0 %collective-permute-done.3.refs_2_ = bf16[256,1024]{1,0:T(8,128)(2,1)S(1)} collective-permute-done((bf16[256,1024]{1,0:T(8,128)(2,1)S(1)}, bf16[256,1024]{1,0:T(8,128)(2,1)S(1)}, u32[]{:S(2)}, u32[]{:S(2)}) %collective-permute-start.3) | collective-permute-done | bytes 524320 | tf_op jit(solution)/shard_map/ppermute | solution.py:370
  41.7 9.1 %attention.1.mine_ref = bf16[128,2048]{1,0:T(8,128)(2,1)} custom-call(s32[1]{0:T(128)} %dynamic_slice.9.len_ref, bf16[128,2048]{1,0:T(8,128)(2,1)S(1)} %copy-done.5, bf16[128,256]{1,0:T(8,128)(2,1)S(1)} %copy-done.6, bf16[128,256]{1,0:T(8,128)(2,1)S(1)} %copy-done.7, bf16[2048,256]{1,0:T(8,128)(2,1)S(1)} %bitcast.41, bf16[2048,256]{1,0:T(8,128)(2,1)S(1)} %bitcast.42), custom_call_target="tpu_custom_call" | custom-call | flops 2147483648 | bytes 2097152 | tf_op jit(solution)/shard_map/attention/pallas_call | solution.py:76
  50.9 8.6 %collective-permute-start.5 = (bf16[256,1024]{1,0:T(8,128)(2,1)S(1)}, bf16[256,1024]{1,0:T(8,128)(2,1)}, u32[]{:S(2)}, u32[]{:S(2)}) collective-permute-start(bf16[256,1024]{1,0:T(8,128)(2,1)S(1)} %pad_maximum_fusion.refs_0_), channel_id=1, source_target_pairs={{0,2},{1,3},{2,0},{3,1},{4,6},{5,7},{6,4},{7,5},{8,10},{9,11},{10,... | collective-permute-start | bytes 1572872 | tf_op jit(solution)/shard_map/ppermute | solution.py:372
  61.8 10.6 %collective-permute-done.5.refs_4_ = bf16[256,1024]{1,0:T(8,128)(2,1)} collective-permute-done((bf16[256,1024]{1,0:T(8,128)(2,1)S(1)}, bf16[256,1024]{1,0:T(8,128)(2,1)}, u32[]{:S(2)}, u32[]{:S(2)}) %collective-permute-start.5) | collective-permute-done | bytes 524320 | tf_op jit(solution)/shard_map/ppermute | solution.py:372
  72.4 1.9 collective-permute-start.8
  74.3 9.3 %collective-permute-done.6.refs_5_ = bf16[256,1024]{1,0:T(8,128)(2,1)} collective-permute-done((bf16[256,1024]{1,0:T(8,128)(2,1)S(1)}, bf16[256,1024]{1,0:T(8,128)(2,1)}, u32[]{:S(2)}, u32[]{:S(2)}) %collective-permute-start.6) | collective-permute-done | bytes 524320 | tf_op jit(solution)/shard_map/ppermute | solution.py:372
  83.6 2.5 collective-permute-start.9
  86.4 2.6 collective-permute-done.8.refs_7_
  89.0 6.6 %collective-permute-done.9.refs_8_ = bf16[256,512]{1,0:T(8,128)(2,1)} collective-permute-done((bf16[256,512]{1,0:T(8,128)(2,1)}, bf16[256,512]{1,0:T(8,128)(2,1)}, u32[]{:S(2)}, u32[]{:S(2)}) %collective-permute-start.9) | collective-permute-done | bytes 262176 | tf_op jit(solution)/shard_map/ppermute | solution.py:375
  95.5 4.7 %projection.1 = (f32[128,1024]{1,0:T(8,128)S(1)}, f32[128,1024]{1,0:T(8,128)S(1)}) custom-call(s32[16]{0:T(128)S(1)} %mul.70.base_ref, bf16[128,2048]{1,0:T(8,128)(2,1)} %attention.1.mine_ref, bf16[128,2048]{1,0:T(8,128)(2,1)} %collective-permute-done.peer_ref, bf16[256,1024]{1,0:T(8,128)(2,1)S(1)} %pad_maximum_fusion.refs_0_, ...), custom_call_target="tpu_custom_call" | custom-call | flops 1073741824 | bytes 4194304 | tf_op jit(solution)/shard_map/projection/pallas_call | solution.py:137
  100.4 1.8 collective-permute-done.10.recv_ref
  102.7 27.6 %all-gather = f32[256,128]{1,0:T(8,128)S(1)} all-gather(f32[16,128]{1,0:T(8,128)S(1)} %pad_maximum_fusion.3), channel_id=2, replica_groups=mesh['groups'=2,'wide'=16] {'wide'}, dimensions={0}, use_global_device_ids=true | all-gather | bytes 139264 | tf_op jit(solution)/shard_map/all_gather | solution.py:390
  131.6 15.3 %collective-permute-done.19.refs_0_ = bf16[128,2048]{1,0:T(8,128)(2,1)} collective-permute-done((bf16[128,2048]{1,0:T(8,128)(2,1)S(1)}, bf16[128,2048]{1,0:T(8,128)(2,1)}, u32[]{:S(2)}, u32[]{:S(2)}) %collective-permute-start.19) | collective-permute-done | bytes 524320 | tf_op jit(solution)/shard_map/ppermute | solution.py:370
  149.0 13.4 %collective-permute-done.20.refs_1_ = bf16[128,2048]{1,0:T(8,128)(2,1)S(1)} collective-permute-done((bf16[128,2048]{1,0:T(8,128)(2,1)}, bf16[128,2048]{1,0:T(8,128)(2,1)S(1)}, u32[]{:S(2)}, u32[]{:S(2)}) %collective-permute-start.20) | collective-permute-done | bytes 524320 | tf_op jit(solution)/shard_map/ppermute | solution.py:370
  164.7 1.7 copy.36.slot_rows
  167.8 2.4 collective-permute-done.22.refs_3_
  170.3 3.1 %collective-permute-done.23.refs_4_ = bf16[128,1024]{1,0:T(8,128)(2,1)} collective-permute-done((bf16[128,1024]{1,0:T(8,128)(2,1)}, bf16[128,1024]{1,0:T(8,128)(2,1)}, u32[]{:S(2)}, u32[]{:S(2)}) %collective-permute-start.23) | collective-permute-done | bytes 262176 | tf_op jit(solution)/shard_map/ppermute | solution.py:375
  173.3 23.7 %experts.3 = (bf16[128,2048]{1,0:T(8,128)(2,1)}, bf16[128,2048]{1,0:T(8,128)(2,1)}, bf16[128,2048]{1,0:T(8,128)(2,1)}, bf16[128,1024]{1,0:T(8,128)(2,1)}, bf16[128,1024]{1,0:T(8,128)(2,1)}) custom-call(s32[2,2,256]{2,1,0:T(2,128)} %copy.36.slot_rows, s32[2,256,2]{2,1,0:T(8,128)} %get-tuple-element.32.slot_cols, f32[2,2,256]{2,1,0:T(2,128)} %copy.37.share_rows, ...), custom_call_target="tpu_custom_call" | custom-call | flops 5435817984 | bytes 18874368 | tf_op jit(solution)/shard_map/experts/pallas_call | solution.py:294
  197.0 1.3 collective-permute-start.26
  202.4 4.2 %collective-permute-done.26 = bf16[128,1024]{1,0:T(8,128)(2,1)S(1)} collective-permute-done((bf16[128,1024]{1,0:T(8,128)(2,1)}, bf16[128,1024]{1,0:T(8,128)(2,1)S(1)}, u32[]{:S(2)}, u32[]{:S(2)}) %collective-permute-start.26) | collective-permute-done | bytes 262176 | tf_op jit(solution)/shard_map/ppermute | solution.py:464
  208.4 2.3 collective-permute-done.24
  214.8 3.0 %collective-permute-done.12.refs_2_ = bf16[128,2048]{1,0:T(8,128)(2,1)S(1)} collective-permute-done((bf16[128,2048]{1,0:T(8,128)(2,1)S(1)}, bf16[128,2048]{1,0:T(8,128)(2,1)S(1)}, u32[]{:S(2)}, u32[]{:S(2)}) %collective-permute-start.12) | collective-permute-done | bytes 524320 | tf_op jit(solution)/shard_map/ppermute | solution.py:372
  217.8 11.2 %collective-permute-done.13.refs_3_ = bf16[128,2048]{1,0:T(8,128)(2,1)S(1)} collective-permute-done((bf16[128,2048]{1,0:T(8,128)(2,1)S(1)}, bf16[128,2048]{1,0:T(8,128)(2,1)S(1)}, u32[]{:S(2)}, u32[]{:S(2)}) %collective-permute-start.13) | collective-permute-done | bytes 524320 | tf_op jit(solution)/shard_map/ppermute | solution.py:372
  229.8 23.6 %experts.2 = (bf16[128,2048]{1,0:T(8,128)(2,1)}, bf16[128,2048]{1,0:T(8,128)(2,1)}, bf16[128,2048]{1,0:T(8,128)(2,1)}, bf16[128,2048]{1,0:T(8,128)(2,1)}) custom-call(s32[2,2,256]{2,1,0:T(2,128)} %copy.34.slot_rows, s32[2,256,2]{2,1,0:T(8,128)} %get-tuple-element.31.slot_cols, f32[2,2,256]{2,1,0:T(2,128)} %copy.35.share_rows, bf16[128,2048]{1,0:T(8,128)(2,1)} %copy-done, ...), custom_call_target="tpu_custom_call" | custom-call | flops 5435817984 | bytes 18874368 | tf_op jit(solution)/shard_map/experts/pallas_call | solution.py:294
  253.5 1.3 collective-permute-start.18
  254.8 1.4 add_convert_fusion.2
  257.1 8.9 %collective-permute-done.18 = bf16[128,2048]{1,0:T(8,128)(2,1)S(1)} collective-permute-done((bf16[128,2048]{1,0:T(8,128)(2,1)}, bf16[128,2048]{1,0:T(8,128)(2,1)S(1)}, u32[]{:S(2)}, u32[]{:S(2)}) %collective-permute-start.18) | collective-permute-done | bytes 524320 | tf_op jit(solution)/shard_map/ppermute | solution.py:473
  266.0 4.1 %collective-permute-done.28 = bf16[128,2048]{1,0:T(8,128)(2,1)S(1)} collective-permute-done((bf16[128,2048]{1,0:T(8,128)(2,1)S(1)}, bf16[128,2048]{1,0:T(8,128)(2,1)S(1)}, u32[]{:S(2)}, u32[]{:S(2)}) %collective-permute-start.28) | collective-permute-done | bytes 524320 | tf_op jit(solution)/shard_map/ppermute | solution.py:474
  270.1 1.3 add_convert_fusion.1
  271.6 9.0 %collective-permute-done.29 = bf16[128,2048]{1,0:T(8,128)(2,1)S(1)} collective-permute-done((bf16[128,2048]{1,0:T(8,128)(2,1)S(1)}, bf16[128,2048]{1,0:T(8,128)(2,1)S(1)}, u32[]{:S(2)}, u32[]{:S(2)}) %collective-permute-start.29) | collective-permute-done | bytes 524320 | tf_op jit(solution)/shard_map/ppermute | solution.py:474
  (118 shorter events, 33.8 us)
Async XLA Ops:
  1.1 1.7 collective-permute-start.1
  2.8 17.2 %collective-permute-start.2 = (bf16[256,1024]{1,0:T(8,128)(2,1)S(1)}, bf16[256,1024]{1,0:T(8,128)(2,1)S(1)}, u32[]{:S(2)}, u32[]{:S(2)}) collective-permute-start(bf16[256,1024]{1,0:T(8,128)(2,1)S(1)} %pad_maximum_fusion.refs_0_), channel_id=1, source_target_pairs={{0,4},{1,5},{2,6},{3,7},{4,8},{5,9},{6,10},{7,11},{8,12},{9,13},{1... | collective-permute-start | bytes 1572872 | tf_op jit(solution)/shard_map/ppermute | solution.py:370
  20.0 15.3 %collective-permute-start.3 = (bf16[256,1024]{1,0:T(8,128)(2,1)S(1)}, bf16[256,1024]{1,0:T(8,128)(2,1)S(1)}, u32[]{:S(2)}, u32[]{:S(2)}) collective-permute-start(bf16[256,1024]{1,0:T(8,128)(2,1)S(1)} %collective-permute-done.2.refs_1_), channel_id=1, source_target_pairs={{0,4},{1,5},{2,6},{3,7},{4,8},{5,9},{6,10},{7,11},{8,12},{9,13},{1... | collective-permute-start | bytes 1572872 | tf_op jit(solution)/shard_map/ppermute | solution.py:370
  35.3 24.3 %collective-permute-start.4 = (bf16[256,1024]{1,0:T(8,128)(2,1)S(1)}, bf16[256,1024]{1,0:T(8,128)(2,1)S(1)}, u32[]{:S(2)}, u32[]{:S(2)}) collective-permute-start(bf16[256,1024]{1,0:T(8,128)(2,1)S(1)} %collective-permute-done.3.refs_2_), channel_id=1, source_target_pairs={{0,4},{1,5},{2,6},{3,7},{4,8},{5,9},{6,10},{7,11},{8,12},{9,13},{1... | collective-permute-start | bytes 1572872 | tf_op jit(solution)/shard_map/ppermute | solution.py:370
  35.3 25.3 %collective-permute-start.7 = (bf16[256,1024]{1,0:T(8,128)(2,1)S(1)}, bf16[256,1024]{1,0:T(8,128)(2,1)S(1)}, u32[]{:S(2)}, u32[]{:S(2)}) collective-permute-start(bf16[256,1024]{1,0:T(8,128)(2,1)S(1)} %collective-permute-done.3.refs_2_), channel_id=1, source_target_pairs={{0,2},{1,3},{2,0},{3,1},{4,6},{5,7},{6,4},{7,5},{8,10},{9,11},{10,... | collective-permute-start | bytes 1572872 | tf_op jit(solution)/shard_map/ppermute | solution.py:372
  41.7 44.6 %copy-start.16 = (f32[128,8]{0,1:T(8,128)S(1)}, f32[128,8]{0,1:T(8,128)}, u32[]{:S(2)}) copy-start(f32[128,8]{0,1:T(8,128)} %param.24) | copy-start | bytes 12292
  50.9 10.7 %collective-permute-start = (bf16[128,2048]{1,0:T(8,128)(2,1)}, bf16[128,2048]{1,0:T(8,128)(2,1)}, u32[]{:S(2)}, u32[]{:S(2)}) collective-permute-start(bf16[128,2048]{1,0:T(8,128)(2,1)} %attention.1.mine_ref), channel_id=1, source_target_pairs={{0,1},{1,0},{2,3},{3,2},{4,5},{5,4},{6,7},{7,6},{8,9},{9,8},{10,11... | collective-permute-start | bytes 1572872 | tf_op jit(solution)/shard_map/ppermute | solution.py:419
  50.9 21.5 %collective-permute-start.5 = (bf16[256,1024]{1,0:T(8,128)(2,1)S(1)}, bf16[256,1024]{1,0:T(8,128)(2,1)}, u32[]{:S(2)}, u32[]{:S(2)}) collective-permute-start(bf16[256,1024]{1,0:T(8,128)(2,1)S(1)} %pad_maximum_fusion.refs_0_), channel_id=1, source_target_pairs={{0,2},{1,3},{2,0},{3,1},{4,6},{5,7},{6,4},{7,5},{8,10},{9,11},{10,... | collective-permute-start | bytes 1572872 | tf_op jit(solution)/shard_map/ppermute | solution.py:372
  59.5 24.1 %collective-permute-start.6 = (bf16[256,1024]{1,0:T(8,128)(2,1)S(1)}, bf16[256,1024]{1,0:T(8,128)(2,1)}, u32[]{:S(2)}, u32[]{:S(2)}) collective-permute-start(bf16[256,1024]{1,0:T(8,128)(2,1)S(1)} %collective-permute-done.2.refs_1_), channel_id=1, source_target_pairs={{0,2},{1,3},{2,0},{3,1},{4,6},{5,7},{6,4},{7,5},{8,10},{9,11},{10,... | collective-permute-start | bytes 1572872 | tf_op jit(solution)/shard_map/ppermute | solution.py:372
  59.6 108.3 %collective-permute-start.14 = (bf16[2048,768]{1,0:T(8,128)(2,1)}, bf16[2048,768]{1,0:T(8,128)(2,1)}, u32[]{:S(2)}, u32[]{:S(2)}) collective-permute-start(bf16[2048,768]{1,0:T(8,128)(2,1)} %bitcast.43), channel_id=1, source_target_pairs={{0,1},{1,0},{2,3},{3,2},{4,5},{5,4},{6,7},{7,6},{8,9},{9,8},{10,11... | collective-permute-start | bytes 9437192 | tf_op jit(solution)/shard_map/ppermute | solution.py:386
  60.6 107.2 %collective-permute-start.15 = (bf16[2048,768]{1,0:T(8,128)(2,1)}, bf16[2048,768]{1,0:T(8,128)(2,1)}, u32[]{:S(2)}, u32[]{:S(2)}) collective-permute-start(bf16[2048,768]{1,0:T(8,128)(2,1)} %bitcast.46), channel_id=1, source_target_pairs={{0,1},{1,0},{2,3},{3,2},{4,5},{5,4},{6,7},{7,6},{8,9},{9,8},{10,11... | collective-permute-start | bytes 9437192 | tf_op jit(solution)/shard_map/ppermute | solution.py:386
  61.6 106.3 %collective-permute-start.16 = (bf16[768,2048]{1,0:T(8,128)(2,1)}, bf16[768,2048]{1,0:T(8,128)(2,1)}, u32[]{:S(2)}, u32[]{:S(2)}) collective-permute-start(bf16[768,2048]{1,0:T(8,128)(2,1)} %bitcast.49), channel_id=1, source_target_pairs={{0,1},{1,0},{2,3},{3,2},{4,5},{5,4},{6,7},{7,6},{8,9},{9,8},{10,11... | collective-permute-start | bytes 9437192 | tf_op jit(solution)/shard_map/ppermute | solution.py:386
  72.4 16.6 %collective-permute-start.8 = (bf16[256,512]{1,0:T(8,128)(2,1)}, bf16[256,512]{1,0:T(8,128)(2,1)S(1)}, u32[]{:S(2)}, u32[]{:S(2)}) collective-permute-start(bf16[256,512]{1,0:T(8,128)(2,1)} %slice.82), channel_id=1, source_target_pairs={{0,2},{1,3},{2,0},{3,1},{4,6},{5,7},{6,4},{7,5},{8,10},{9,11},{10,... | collective-permute-start | bytes 786440 | tf_op jit(solution)/shard_map/ppermute | solution.py:375
  83.6 11.9 %collective-permute-start.9 = (bf16[256,512]{1,0:T(8,128)(2,1)}, bf16[256,512]{1,0:T(8,128)(2,1)}, u32[]{:S(2)}, u32[]{:S(2)}) collective-permute-start(bf16[256,512]{1,0:T(8,128)(2,1)} %slice.83), channel_id=1, source_target_pairs={{0,4},{1,5},{2,6},{3,7},{4,8},{5,9},{6,10},{7,11},{8,12},{9,13},{1... | collective-permute-start | bytes 786440 | tf_op jit(solution)/shard_map/ppermute | solution.py:375
  100.2 2.0 collective-permute-start.10
  102.5 95.8 %copy-start = (bf16[128,2048]{1,0:T(8,128)(2,1)}, bf16[128,2048]{1,0:T(8,128)(2,1)S(1)}, u32[]{:S(2)}) copy-start(bf16[128,2048]{1,0:T(8,128)(2,1)S(1)} %get-tuple-element.21.refs_0_) | copy-start | bytes 1572868
  102.5 28.3 %collective-permute-start.11 = (bf16[128,2048]{1,0:T(8,128)(2,1)S(1)}, bf16[128,2048]{1,0:T(8,128)(2,1)S(1)}, u32[]{:S(2)}, u32[]{:S(2)}) collective-permute-start(bf16[128,2048]{1,0:T(8,128)(2,1)S(1)} %get-tuple-element.21.refs_0_), channel_id=1, source_target_pairs={{0,4},{1,5},{2,6},{3,7},{4,8},{5,9},{6,10},{7,11},{8,12},{9,13},{1... | collective-permute-start | bytes 1572872 | tf_op jit(solution)/shard_map/ppermute | solution.py:370
  130.8 16.1 %collective-permute-start.19 = (bf16[128,2048]{1,0:T(8,128)(2,1)S(1)}, bf16[128,2048]{1,0:T(8,128)(2,1)}, u32[]{:S(2)}, u32[]{:S(2)}) collective-permute-start(bf16[128,2048]{1,0:T(8,128)(2,1)S(1)} %collective-permute-done.11.refs_1_), channel_id=1, source_target_pairs={{0,4},{1,5},{2,6},{3,7},{4,8},{5,9},{6,10},{7,11},{8,12},{9,13},{1... | collective-permute-start | bytes 1572872 | tf_op jit(solution)/shard_map/ppermute | solution.py:370
  147.0 15.4 %collective-permute-start.20 = (bf16[128,2048]{1,0:T(8,128)(2,1)}, bf16[128,2048]{1,0:T(8,128)(2,1)S(1)}, u32[]{:S(2)}, u32[]{:S(2)}) collective-permute-start(bf16[128,2048]{1,0:T(8,128)(2,1)} %collective-permute-done.19.refs_0_), channel_id=1, source_target_pairs={{0,4},{1,5},{2,6},{3,7},{4,8},{5,9},{6,10},{7,11},{8,12},{9,13},{1... | collective-permute-start | bytes 1572872 | tf_op jit(solution)/shard_map/ppermute | solution.py:370
  147.0 16.9 %collective-permute-start.21 = (bf16[128,2048]{1,0:T(8,128)(2,1)}, bf16[128,2048]{1,0:T(8,128)(2,1)S(1)}, u32[]{:S(2)}, u32[]{:S(2)}) collective-permute-start(bf16[128,2048]{1,0:T(8,128)(2,1)} %collective-permute-done.19.refs_0_), channel_id=1, source_target_pairs={{0,2},{1,3},{2,0},{3,1},{4,6},{5,7},{6,4},{7,5},{8,10},{9,11},{10,... | collective-permute-start | bytes 1572872 | tf_op jit(solution)/shard_map/ppermute | solution.py:372
  163.1 7.2 %collective-permute-start.22 = (bf16[128,1024]{1,0:T(8,128)(2,1)}, bf16[128,1024]{1,0:T(8,128)(2,1)}, u32[]{:S(2)}, u32[]{:S(2)}) collective-permute-start(bf16[128,1024]{1,0:T(8,128)(2,1)} %slice.92), channel_id=1, source_target_pairs={{0,2},{1,3},{2,0},{3,1},{4,6},{5,7},{6,4},{7,5},{8,10},{9,11},{10,... | collective-permute-start | bytes 786440 | tf_op jit(solution)/shard_map/ppermute | solution.py:375
  164.7 8.7 %collective-permute-start.23 = (bf16[128,1024]{1,0:T(8,128)(2,1)}, bf16[128,1024]{1,0:T(8,128)(2,1)}, u32[]{:S(2)}, u32[]{:S(2)}) collective-permute-start(bf16[128,1024]{1,0:T(8,128)(2,1)} %slice.93), channel_id=1, source_target_pairs={{0,4},{1,5},{2,6},{3,7},{4,8},{5,9},{6,10},{7,11},{8,12},{9,13},{1... | collective-permute-start | bytes 786440 | tf_op jit(solution)/shard_map/ppermute | solution.py:375
  197.0 9.5 %collective-permute-start.26 = (bf16[128,1024]{1,0:T(8,128)(2,1)}, bf16[128,1024]{1,0:T(8,128)(2,1)S(1)}, u32[]{:S(2)}, u32[]{:S(2)}) collective-permute-start(bf16[128,1024]{1,0:T(8,128)(2,1)} %get-tuple-element.30), channel_id=1, source_target_pairs={{0,2},{1,3},{2,0},{3,1},{4,6},{5,7},{6,4},{7,5},{8,10},{9,11},{10,... | collective-permute-start | bytes 786440 | tf_op jit(solution)/shard_map/ppermute | solution.py:464
  198.3 19.4 %collective-permute-start.12 = (bf16[128,2048]{1,0:T(8,128)(2,1)S(1)}, bf16[128,2048]{1,0:T(8,128)(2,1)S(1)}, u32[]{:S(2)}, u32[]{:S(2)}) collective-permute-start(bf16[128,2048]{1,0:T(8,128)(2,1)S(1)} %get-tuple-element.21.refs_0_), channel_id=1, source_target_pairs={{0,2},{1,3},{2,0},{3,1},{4,6},{5,7},{6,4},{7,5},{8,10},{9,11},{10,... | collective-permute-start | bytes 1572872 | tf_op jit(solution)/shard_map/ppermute | solution.py:372
  199.1 29.9 %collective-permute-start.13 = (bf16[128,2048]{1,0:T(8,128)(2,1)S(1)}, bf16[128,2048]{1,0:T(8,128)(2,1)S(1)}, u32[]{:S(2)}, u32[]{:S(2)}) collective-permute-start(bf16[128,2048]{1,0:T(8,128)(2,1)S(1)} %copy-done.11), channel_id=1, source_target_pairs={{0,2},{1,3},{2,0},{3,1},{4,6},{5,7},{6,4},{7,5},{8,10},{9,11},{10,... | collective-permute-start | bytes 1572872 | tf_op jit(solution)/shard_map/ppermute | solution.py:372
  201.3 9.4 %collective-permute-start.24 = (bf16[128,1024]{1,0:T(8,128)(2,1)}, bf16[128,1024]{1,0:T(8,128)(2,1)S(1)}, u32[]{:S(2)}, u32[]{:S(2)}) collective-permute-start(bf16[128,1024]{1,0:T(8,128)(2,1)} %get-tuple-element.28), channel_id=1, source_target_pairs={{0,12},{1,13},{2,14},{3,15},{4,0},{5,1},{6,2},{7,3},{8,4},{9,5},{1... | collective-permute-start | bytes 786440 | tf_op jit(solution)/shard_map/ppermute | solution.py:465
  208.4 46.4 %collective-permute-start.27 = (bf16[128,2048]{1,0:T(8,128)(2,1)}, bf16[128,2048]{1,0:T(8,128)(2,1)}, u32[]{:S(2)}, u32[]{:S(2)}) collective-permute-start(bf16[128,2048]{1,0:T(8,128)(2,1)} %pad_maximum_fusion.2), channel_id=1, source_target_pairs={{0,12},{1,13},{2,14},{3,15},{4,0},{5,1},{6,2},{7,3},{8,4},{9,5},{1... | collective-permute-start | bytes 1572872 | tf_op jit(solution)/shard_map/ppermute | solution.py:474
  212.7 42.1 %collective-permute-start.25 = (bf16[128,2048]{1,0:T(8,128)(2,1)}, bf16[128,2048]{1,0:T(8,128)(2,1)}, u32[]{:S(2)}, u32[]{:S(2)}) collective-permute-start(bf16[128,2048]{1,0:T(8,128)(2,1)} %pad_maximum_fusion.1), channel_id=1, source_target_pairs={{0,2},{1,3},{2,0},{3,1},{4,6},{5,7},{6,4},{7,5},{8,10},{9,11},{10,... | collective-permute-start | bytes 1572872 | tf_op jit(solution)/shard_map/ppermute | solution.py:473
  253.5 12.6 %collective-permute-start.18 = (bf16[128,2048]{1,0:T(8,128)(2,1)}, bf16[128,2048]{1,0:T(8,128)(2,1)S(1)}, u32[]{:S(2)}, u32[]{:S(2)}) collective-permute-start(bf16[128,2048]{1,0:T(8,128)(2,1)} %get-tuple-element.25), channel_id=1, source_target_pairs={{0,2},{1,3},{2,0},{3,1},{4,6},{5,7},{6,4},{7,5},{8,10},{9,11},{10,... | collective-permute-start | bytes 1572872 | tf_op jit(solution)/shard_map/ppermute | solution.py:473
  256.2 13.9 %collective-permute-start.28 = (bf16[128,2048]{1,0:T(8,128)(2,1)S(1)}, bf16[128,2048]{1,0:T(8,128)(2,1)S(1)}, u32[]{:S(2)}, u32[]{:S(2)}) collective-permute-start(bf16[128,2048]{1,0:T(8,128)(2,1)S(1)} %add_convert_fusion.2), channel_id=1, source_target_pairs={{0,12},{1,13},{2,14},{3,15},{4,0},{5,1},{6,2},{7,3},{8,4},{9,5},{1... | collective-permute-start | bytes 1572872 | tf_op jit(solution)/shard_map/ppermute | solution.py:474
  256.3 15.4 %collective-permute-start.17 = (bf16[128,2048]{1,0:T(8,128)(2,1)}, bf16[128,2048]{1,0:T(8,128)(2,1)S(1)}, u32[]{:S(2)}, u32[]{:S(2)}) collective-permute-start(bf16[128,2048]{1,0:T(8,128)(2,1)} %get-tuple-element.23), channel_id=1, source_target_pairs={{0,2},{1,3},{2,0},{3,1},{4,6},{5,7},{6,4},{7,5},{8,10},{9,11},{10,... | collective-permute-start | bytes 1572872 | tf_op jit(solution)/shard_map/ppermute | solution.py:473
  271.4 9.2 %collective-permute-start.29 = (bf16[128,2048]{1,0:T(8,128)(2,1)S(1)}, bf16[128,2048]{1,0:T(8,128)(2,1)S(1)}, u32[]{:S(2)}, u32[]{:S(2)}) collective-permute-start(bf16[128,2048]{1,0:T(8,128)(2,1)S(1)} %add_convert_fusion.1), channel_id=1, source_target_pairs={{0,12},{1,13},{2,14},{3,15},{4,0},{5,1},{6,2},{7,3},{8,4},{9,5},{1... | collective-permute-start | bytes 1572872 | tf_op jit(solution)/shard_map/ppermute | solution.py:474
  (16 other events, 242.5 us)

commit v2 on v0

v2 whole, which is shorter than its diff:
```python
import functools

import jax
import jax.numpy as jnp
from jax import lax
from jax.experimental import pallas as pl
from jax.experimental.pallas import tpu as pltpu
from jax.sharding import PartitionSpec as P

HEAD = 128
KEY_BLOCK = 1024
LOG2E = 1.4426950408889634
NEG = -1e30
MIB = 1 << 20

VMEM = pl.BlockSpec(memory_space=pltpu.VMEM)
SMEM = pl.BlockSpec(memory_space=pltpu.SMEM)
ANY = pl.BlockSpec(memory_space=pl.ANY)


def dot(a, b):
    return jnp.dot(a, b, preferred_element_type=jnp.float32)


def attention_kernel(len_ref, q_ref, nk_ref, nv_ref, k_ref, v_ref, o_ref, q_all, scores, top, acc, total):
    tokens = q_ref.shape[0]
    heads = q_ref.shape[1] // HEAD
    cache = k_ref.shape[0]
    length = len_ref[0]
    blocks = (length + KEY_BLOCK - 1) // KEY_BLOCK
    scale = jnp.float32(HEAD**-0.5 * LOG2E)
    rows = heads * tokens

    for h in range(heads):
        q_all[h * tokens : (h + 1) * tokens, :] = q_ref[:, h * HEAD : (h + 1) * HEAD]

    def scores_of(k):
        return lax.dot_general(
            q_all[...], k, (((1,), (1,)), ((), ())), preferred_element_type=jnp.float32
        )

    def fold(x, op):
        parts = [x[:, i : i + HEAD] for i in range(0, x.shape[1], HEAD)]
        while len(parts) > 1:
            parts = [op(*parts[i : i + 2]) if i + 1 < len(parts) else parts[i] for i in range(0, len(parts), 2)]
        return parts[0]

    s = scores_of(nk_ref[...])
    row = lax.broadcasted_iota(jnp.int32, s.shape, 0) % tokens
    col = lax.broadcasted_iota(jnp.int32, s.shape, 1)
    s = jnp.where(col <= row, s, NEG)
    scores[:, cache:] = s
    top[...] = fold(s, jnp.maximum)

    def score(i, carry):
        at = pl.ds(pl.multiple_of(i * KEY_BLOCK, KEY_BLOCK), KEY_BLOCK)
        s = scores_of(k_ref[at, :])
        pos = lax.broadcasted_iota(jnp.int32, s.shape, 1)
        s = jnp.where(pos < length - i * KEY_BLOCK, s, NEG)
        scores[:, at] = s
        top[...] = jnp.maximum(top[...], fold(s, jnp.maximum))
        return carry

    lax.fori_loop(0, blocks, score, 0)
    best = jnp.max(top[...], axis=1, keepdims=True) * scale
    top[...] = jnp.broadcast_to(best, top.shape)

    def weigh(s):
        shift = jnp.concatenate([top[...]] * (s.shape[1] // HEAD), axis=1)
        return jnp.exp2(s * scale - shift)

    w = weigh(scores[:, cache:])
    total[...] = fold(w, jnp.add)
    acc[...] = dot(w.astype(jnp.bfloat16), nv_ref[...])

    def add_block(i, carry):
        at = pl.ds(pl.multiple_of(i * KEY_BLOCK, KEY_BLOCK), KEY_BLOCK)
        w = weigh(scores[:, at])
        total[...] += fold(w, jnp.add)
        acc[...] += dot(w.astype(jnp.bfloat16), v_ref[at, :])
        return carry

    lax.fori_loop(0, blocks, add_block, 0)
    out = (acc[...] / jnp.sum(total[...], axis=1, keepdims=True)).astype(jnp.bfloat16)
    for h in range(heads):
        o_ref[:, h * HEAD : (h + 1) * HEAD] = out[h * tokens : (h + 1) * tokens, :]


def attention(part, parts, length, queries, new_keys, new_values, keys, values):
    tokens, width = queries.shape
    kv_heads = new_keys.shape[1] // HEAD
    g = part * kv_heads // parts
    group = width // parts
    cache = keys.shape[0]
    rows = group // HEAD * tokens
    return pl.pallas_call(
        attention_kernel,
        grid=(1,),
        in_specs=[
            SMEM,
            pl.BlockSpec((tokens, group), lambda i: (0, part)),
            pl.BlockSpec((tokens, HEAD), lambda i: (0, g)),
            pl.BlockSpec((tokens, HEAD), lambda i: (0, g)),
            pl.BlockSpec((cache, HEAD), lambda i: (0, g)),
            pl.BlockSpec((cache, HEAD), lambda i: (0, g)),
        ],
        out_specs=pl.BlockSpec((tokens, group), lambda i: (0, 0)),
        out_shape=jax.ShapeDtypeStruct((tokens, group), jnp.bfloat16),
        scratch_shapes=[
            pltpu.VMEM((rows, HEAD), jnp.bfloat16),
            pltpu.VMEM((rows, cache + tokens), jnp.float32),
            pltpu.VMEM((rows, HEAD), jnp.float32),
            pltpu.VMEM((rows, HEAD), jnp.float32),
            pltpu.VMEM((rows, HEAD), jnp.float32),
        ],
        compiler_params=pltpu.CompilerParams(vmem_limit_bytes=58 * MIB),
        cost_estimate=pl.CostEstimate(
            flops=20 * tokens * group * cache,
            bytes_accessed=4 * cache * HEAD,
            transcendentals=tokens * group // HEAD * cache,
        ),
        name="attention",
    )(length, queries, new_keys, new_values, keys, values)


def projection_kernel(n_pieces, n_blocks, base_ref, *refs):
    pieces, w_refs = refs[:n_pieces], refs[n_pieces : n_pieces + n_blocks + 1]
    outs = refs[n_pieces + n_blocks + 1 : -3]
    left, weight, sems = refs[-3:]
    tokens, group = pieces[0].shape
    rows = weight.shape[0] // n_blocks // 2
    half = weight.shape[1] // 2
    copies = []
    for b in range(n_blocks + 1):
        for part in range(2):
            at = pl.multiple_of(base_ref[2 * min(b, n_blocks - 1) + part], rows)
            src = w_refs[b].at[pl.ds(part * rows, rows)]
            if b < n_blocks - 1:
                dst = weight.at[pl.ds(at, rows)]
            else:
                dst = weight.at[pl.ds(at, rows), pl.ds((b - n_blocks + 1) * half, half)]
            copies.append(pltpu.make_async_copy(src, dst, sems.at[2 * b + part]))
            copies[-1].start()
    each = n_pieces // len(outs)
    for i in range(n_pieces):
        at = (i // each) * tokens
        left[at : at + tokens, (i % each) * group : (i % each + 1) * group] = pieces[i][...]
    for copy in copies:
        copy.wait()
    whole = dot(left[...], weight[...])
    for i, out in enumerate(outs):
        out[...] = whole[i * tokens : (i + 1) * tokens].astype(out.dtype)


def projection(bases, pieces, blocks, types):
    tokens, group = pieces[0].shape
    width = len(pieces) // len(types) * group
    n_blocks = len(blocks) - 1
    cols = blocks[0].shape[1]
    return pl.pallas_call(
        functools.partial(projection_kernel, len(pieces), n_blocks),
        in_specs=[SMEM] + [VMEM] * len(pieces) + [ANY] * len(blocks),
        out_specs=[VMEM] * len(types),
        out_shape=[jax.ShapeDtypeStruct((tokens, cols), t) for t in types],
        scratch_shapes=[
            pltpu.VMEM((len(types) * tokens, width), jnp.bfloat16),
            pltpu.VMEM((width, cols), jnp.bfloat16),
            pltpu.SemaphoreType.DMA((2 * n_blocks + 2,)),
        ],
        compiler_params=pltpu.CompilerParams(vmem_limit_bytes=58 * MIB),
        cost_estimate=pl.CostEstimate(
            flops=8 * tokens * width * cols, bytes_accessed=2 * width * cols, transcendentals=0
        ),
        name="projection",
    )(bases, *pieces, *blocks)


def norm_kernel(place_ref, residual_ref, gain_ref, *refs):
    parts, mixed_ref, normed_refs = refs[:-3], refs[-3], refs[-2:]
    cols, width = parts[0].shape[1], residual_ref.shape[1]
    total = 0.0
    for i, part in enumerate(parts):
        at = pl.ds(pl.multiple_of(place_ref[i], HEAD), cols)
        mixed = residual_ref[:, at].astype(jnp.float32) + part[...].astype(jnp.float32)
        mixed_ref[:, at] = mixed
        total = total + jnp.sum(mixed * mixed, axis=1, keepdims=True)
    factor = lax.rsqrt(total / width + 1e-06)
    half = width // 2
    for h, normed_ref in enumerate(normed_refs):
        at = slice(h * half, (h + 1) * half)
        normed_ref[...] = (mixed_ref[:, at] * factor * gain_ref[:, at]).astype(jnp.bfloat16)


def mix_and_norm(places, residual, gain, parts):
    return pl.pallas_call(
        norm_kernel,
        in_specs=[SMEM] + [VMEM] * (2 + len(parts)),
        out_specs=[VMEM] * 3,
        out_shape=[jax.ShapeDtypeStruct(residual.shape, jnp.float32)]
        + [jax.ShapeDtypeStruct((residual.shape[0], residual.shape[1] // 2), jnp.bfloat16)] * 2,
        compiler_params=pltpu.CompilerParams(vmem_limit_bytes=58 * MIB),
        name="mix_and_norm",
    )(places, residual, gain, *parts)


def finish_kernel(mixed_ref, *refs):
    out_ref = refs[-1]
    terms = (len(refs) - 1) // 2
    half = refs[0].shape[1]
    for h in range(2):
        cols = slice(h * half, (h + 1) * half)
        total = mixed_ref[:, cols]
        for ref in refs[h * terms : (h + 1) * terms]:
            total = total + ref[...].astype(jnp.float32)
        out_ref[:, cols] = total.astype(out_ref.dtype)


def finish(mixed, first, second):
    return pl.pallas_call(
        finish_kernel,
        in_specs=[VMEM] * (1 + len(first) + len(second)),
        out_specs=VMEM,
        out_shape=jax.ShapeDtypeStruct(mixed.shape, jnp.bfloat16),
        name="finish",
    )(mixed, *first, *second)


def routing_kernel(cap, served_ref, table_ref, rows_ref, cols_ref, shares_ref, mask):
    blocks, _, _, tokens = table_ref.shape
    for b in range(blocks):
        ids = table_ref[b, 0].astype(jnp.float32)
        share = table_ref[b, 1].astype(jnp.float32) + table_ref[b, 2].astype(jnp.float32)
        at = slice(b % 2 * tokens, (b % 2 + 1) * tokens)
        for e in range(2):
            hit = ids == served_ref[e].astype(jnp.float32)
            mask[2 * b + e : 2 * b + e + 1, :] = jnp.max(
                jnp.where(hit, 1.0, 0.0), axis=0, keepdims=True
            )
            shares_ref[b // 2, e : e + 1, at] = jnp.sum(
                jnp.where(hit, share, 0.0), axis=0, keepdims=True
            )
    first = lax.broadcasted_iota(jnp.int32, (tokens, tokens), 0)
    second = lax.broadcasted_iota(jnp.int32, (tokens, tokens), 1)
    before = jnp.where(first < second, 1.0, 0.0).astype(jnp.bfloat16)
    same = jnp.where(first == second, 1.0, 0.0).astype(jnp.bfloat16)
    there = mask[...]
    rank = dot(there.astype(jnp.bfloat16), before)
    line = lax.broadcasted_iota(jnp.int32, rank.shape, 0)
    slot = jnp.where(there > 0.5, rank + jnp.where(line // 2 % 2 == 1, float(cap), 0.0), -512.0)
    columns = lax.dot_general(
        same, slot.astype(jnp.bfloat16), (((1,), (1,)), ((), ())), preferred_element_type=jnp.float32
    )
    for b in range(blocks):
        at = slice(b % 2 * tokens, (b % 2 + 1) * tokens)
        lines = slice(2 * b, 2 * b + 2)
        rows_ref[b // 2, :, at] = slot[lines].astype(jnp.int32)
        cols_ref[b // 2, at, :] = columns[:, lines].astype(jnp.int32)


def routing(cap, served, table):
    blocks, _, _, tokens = table.shape
    pairs = blocks // 2
    rows = jax.ShapeDtypeStruct((pairs, 2, 2 * tokens), jnp.int32)
    return pl.pallas_call(
        functools.partial(routing_kernel, cap),
        in_specs=[SMEM, VMEM],
        out_specs=[VMEM] * 3,
        out_shape=[
            rows,
            jax.ShapeDtypeStruct((pairs, 2 * tokens, 2), jnp.int32),
            jax.ShapeDtypeStruct(rows.shape, jnp.float32),
        ],
        scratch_shapes=[pltpu.VMEM((2 * blocks, tokens), jnp.float32)],
        compiler_params=pltpu.CompilerParams(vmem_limit_bytes=16 * MIB),
        name="routing",
    )(served, table)


def fetch_kernel(*refs):
    count = (len(refs) - 2) // 2
    token, sems = refs[-2:]
    token[...] = jnp.zeros_like(token)
    copies = [
        pltpu.make_async_copy(refs[i], refs[count + i], sems.at[i]) for i in range(count)
    ]
    for copy in copies:
        copy.start()
    for copy in copies:
        copy.wait()


def fetch(arrays):
    arrays = [pltpu.with_memory_space_constraint(a, pltpu.HBM) for a in arrays]
    *there, token = pl.pallas_call(
        fetch_kernel,
        in_specs=[ANY] * len(arrays),
        out_specs=[VMEM] * (len(arrays) + 1),
        out_shape=[pltpu.VMEM(a.shape, a.dtype) for a in arrays]
        + [jax.ShapeDtypeStruct((8, HEAD), jnp.float32)],
        scratch_shapes=[pltpu.SemaphoreType.DMA((len(arrays),))],
        compiler_params=pltpu.CompilerParams(vmem_limit_bytes=24 * MIB),
        name="fetch",
    )(*arrays)
    return there, token


def experts_kernel(first_pair, pairs, n_in, n_out, slots, slot_rows, slot_cols, share_rows, *refs):
    x_refs = refs[:n_in]
    w_refs = refs[n_in : n_in + 6]
    out_refs = refs[n_in + 7 : n_in + 7 + n_out]
    xs, rows_in, act, scaled, x_sem = refs[n_in + 7 + n_out :]
    depth = xs.shape[1]
    pair_tokens = xs.shape[0] // pairs
    block = pair_tokens // 2
    hidden = act.shape[1]

    x_copies = []
    at, col = 0, 0
    for i in range(n_in):
        wide = x_refs[i].shape[1]
        dst = xs.at[pl.ds(at, block), pl.ds(col, wide)]
        x_copies.append(pltpu.make_async_copy(x_refs[i], dst, x_sem.at[i]))
        x_copies[-1].start()
        col += wide
        if col == depth:
            at, col = at + block, 0
    for copy in x_copies:
        copy.wait()

    shares = []
    for p in range(pairs):
        row = lax.broadcasted_iota(jnp.int32, (2 * slots, pair_tokens), 0)
        first = row == slot_rows[first_pair + p, 0:1, :]
        second = row - slots == slot_rows[first_pair + p, 1:2, :]
        pick = jnp.where(first | second, 1.0, 0.0).astype(jnp.bfloat16)
        weight = jnp.where(first, share_rows[first_pair + p, 0:1, :], 0.0) + jnp.where(
            second, share_rows[first_pair + p, 1:2, :], 0.0
        )
        shares.append(jnp.sum(weight, axis=1, keepdims=True))
        step = min(1024, depth)
        for c in range(0, depth, step):
            got = dot(pick, xs[p * pair_tokens : (p + 1) * pair_tokens, c : c + step])
            got = got.astype(jnp.bfloat16)
            rows_in[0, p * slots : (p + 1) * slots, c : c + step] = got[:slots]
            rows_in[1, p * slots : (p + 1) * slots, c : c + step] = got[slots:]

    for e in range(2):
        x = rows_in[e]
        gate = dot(x, w_refs[3 * e][...])
        up = dot(x, w_refs[3 * e + 1][...])
        act[...] = (gate / (1.0 + jnp.exp(-gate)) * up).astype(jnp.bfloat16)
        share = jnp.concatenate([s[e * slots : (e + 1) * slots] for s in shares], axis=0)
        y = (dot(act[...], w_refs[3 * e + 2][...]) * share).astype(jnp.bfloat16)
        for p in range(pairs):
            scaled[p, e * slots : (e + 1) * slots, :] = y[p * slots : (p + 1) * slots]

    o = 0
    for p in range(pairs):
        lane = lax.broadcasted_iota(jnp.int32, (pair_tokens, 2 * slots), 1)
        back = lane == slot_cols[first_pair + p, :, 0:1]
        back = back | (lane - slots == slot_cols[first_pair + p, :, 1:2])
        back = jnp.where(back, 1.0, 0.0).astype(jnp.bfloat16)
        place = []
        for b in range(2):
            start = 0
            while start < depth:
                place.append((b, start, out_refs[o]))
                start += out_refs[o].shape[1]
                o += 1
        step = min(1024, depth)
        for c in range(0, depth, step):
            got = dot(back, scaled[p, :, c : c + step]).astype(jnp.bfloat16)
            for b, start, ref in place:
                if start <= c < start + ref.shape[1]:
                    ref[:, c - start : c - start + step] = got[b * block : (b + 1) * block]


def experts(slots, first_pair, pairs, slot_rows, slot_cols, share_rows, x_parts, weights, out_widths):
    pair_tokens = slot_rows.shape[2]
    block = pair_tokens // 2
    depth, hidden = weights[0].shape
    n_in, n_out = len(x_parts), len(out_widths)
    return pl.pallas_call(
        functools.partial(experts_kernel, first_pair, pairs, n_in, n_out, slots),
        in_specs=[VMEM, VMEM, VMEM] + [ANY] * n_in + [VMEM] * 6 + [ANY],
        out_specs=[VMEM] * n_out,
        out_shape=[jax.ShapeDtypeStruct((block, w), jnp.bfloat16) for w in out_widths],
        scratch_shapes=[
            pltpu.VMEM((pairs * pair_tokens, depth), jnp.bfloat16),
            pltpu.VMEM((2, pairs * slots, depth), jnp.bfloat16),
            pltpu.VMEM((pairs * slots, hidden), jnp.bfloat16),
            pltpu.VMEM((pairs, 2 * slots, depth), jnp.bfloat16),
            pltpu.SemaphoreType.DMA((n_in,)),
        ],
        compiler_params=pltpu.CompilerParams(vmem_limit_bytes=32 * MIB),
        cost_estimate=pl.CostEstimate(
            flops=12 * pairs * slots * depth * hidden,
            bytes_accessed=12 * depth * hidden,
            transcendentals=0,
        ),
        name="experts",
    )(slot_rows, slot_cols, share_rows, *x_parts, *weights)


def permutations(devices):
    cores, rows = 2, 2
    ring = devices // (cores * rows)

    def index(z, y, c):
        return (z % ring * rows + y % rows) * cores + c % cores

    def shift(dz, dy=0, dc=0):
        return [
            (index(z, y, c), index(z + dz + ring, y + dy, c + dc))
            for z in range(ring)
            for y in range(rows)
            for c in range(cores)
        ]

    return ring, shift


def per_device(
    residual,
    queries,
    new_keys,
    new_values,
    cache_keys,
    cache_values,
    cache_len,
    o_weight,
    norm_gain,
    expert_ids,
    gate_raw,
    w_gate,
    w_up,
    w_down,
):
    devices = lax.axis_size("wide")
    replicas = lax.axis_size("groups")
    me = lax.axis_index("wide")
    tokens, depth = residual.shape
    top = expert_ids.shape[1]
    half = depth // 2
    ring, shift = permutations(devices)
    core = me % 2
    row = me // 2 % 2
    place = me // 4
    side = lax.axis_index("groups") % 2

    def sender(*by):
        return lambda x: lax.ppermute(x, "wide", shift(*by))

    def side_sender(*by):
        pairs = [
            (g * devices + a, (g ^ 1) * devices + b)
            for g in range(replicas)
            for a, b in shift(*by)
        ]
        return lambda x: lax.ppermute(x, ("groups", "wide"), pairs)

    send_forward, send_backward = sender(1), sender(-1)
    send_across, send_core = sender(0, 1), sender(0, 0, 1)
    send_side, send_corner = side_sender(0), side_sender(0, 0, 1)
    barrier = lax.optimization_barrier

    def gather_whole(own, beside):
        same, other = [own], []
        for r in range(1, ring):
            moved, crossed = send_forward(same[-1]), send_across(same[-1])
            new = beside[r - 1](same, other) if r <= len(beside) else {}
            moved, crossed, new = barrier((moved, crossed, new))
            kept.update(new)
            same.append(moved)
            other.append(crossed)
        cut = own.shape[1] // 2
        last = [send_across(same[-1][:, :cut]), send_forward(other[-1][:, cut:])]
        for step in beside[ring - 1 :]:
            last, new = barrier((last, step(same, other)))
            kept.update(new)
        return same, other, last

    def gather_halves(own, beside):
        same, other = [list(own)], []
        for r in range(1, ring):
            moved = [send_forward(h) for h in same[-1]]
            crossed = [send_across(h) for h in same[-1]]
            new = beside[r - 1](same, other) if r <= len(beside) else {}
            moved[0], crossed[0] = barrier((moved[0], crossed[0]))
            moved[1], crossed[1], new = barrier((moved[1], crossed[1], new))
            kept.update(new)
            same.append(moved)
            other.append(crossed)
        last = [send_across(same[-1][0]), send_forward(other[-1][1])]
        for step in beside[ring - 1 :]:
            last, new = barrier((last, step(same, other)))
            kept.update(new)
        other.append(last)
        return same, other

    kept = {}

    cols = depth // 4
    quarter = 2 * side + core
    keep = lax.dynamic_slice_in_dim(o_weight, quarter * cols, cols, 1)
    give = lax.dynamic_slice_in_dim(o_weight, (quarter ^ 1) * cols, cols, 1)
    shares = gate_raw / jnp.sum(gate_raw, axis=-1, keepdims=True)
    high = shares.astype(jnp.bfloat16)
    low = (shares - high.astype(jnp.float32)).astype(jnp.bfloat16)
    table = jnp.stack([expert_ids.astype(jnp.bfloat16), high, low]).transpose(0, 2, 1)
    table = table.reshape(-1, cols)
    table_rows = table.shape[0]
    table = jnp.pad(table, ((0, -table_rows % 16), (0, 0)))
    own_block = jnp.concatenate([keep, send_core(give), table], axis=0)
    length = lax.dynamic_slice_in_dim(cache_len, me, 1, 0)
    mine = [w_gate[0], w_up[0], w_down[0]]
    length, own_block, mine = barrier((length, own_block, mine))
    operands = (queries, new_keys, new_values, cache_keys[0], cache_values[0])

    def attend_first(same, other):
        return {"a0": attention(0, 2, length, *operands), "w0": send_core(mine[0])}

    def attend_second(same, other):
        begin, kept["a0"] = barrier((length, kept["a0"]))
        return {
            "a1": attention(1, 2, begin, *operands),
            "side0": send_side(kept["a0"]),
            "w1": send_core(mine[1]),
        }

    def swap_first(same, other):
        return {
            "side1": send_side(kept["a1"]),
            "core0": send_core(kept["a0"]),
            "w2": send_core(mine[2]),
        }

    def swap_second(same, other):
        return {
            "core1": send_core(kept["a1"]),
            "corner0": send_core(kept["side0"]),
            "corner1": send_core(kept["side1"]),
        }

    w_same, w_other, w_last = gather_whole(
        own_block, [attend_first, attend_second, swap_first, swap_second]
    )
    offsets = jnp.arange(ring, dtype=jnp.int32)
    rings = (place - offsets) % ring
    first_of = jnp.concatenate([rings * 2 + row, rings * 2 + 1 - row]) * 2
    bases = jnp.stack([first_of + core, first_of + 1 - core], axis=1).reshape(-1)
    pieces = [kept[name + str(g)] for name in ("a", "core", "side", "corner") for g in range(2)]
    own_part, core_part, side_part, corner_part = projection(
        bases * o_weight.shape[0],
        pieces,
        w_same + w_other + w_last,
        [jnp.float32, jnp.float32, jnp.bfloat16, jnp.bfloat16],
    )
    parts = [own_part, send_core(core_part), send_side(side_part), send_corner(corner_part)]
    places = jnp.stack([quarter, quarter ^ 1, quarter ^ 2, quarter ^ 3]).astype(jnp.int32) * cols
    mixed, *normed = mix_and_norm(places, residual, norm_gain.reshape(1, -1), parts)

    cap = tokens * top // devices + max(2, tokens * top // (8 * devices))
    slots = -(-2 * cap // 16) * 16

    def make_tables(same, other):
        rows = slice(own_block.shape[0] - table.shape[0], own_block.shape[0] - table.shape[0] + table_rows)
        blocks, same[0] = barrier((w_same + w_other + w_last, same[0]))
        tables = [b[rows] for b in blocks[:-2]]
        tables.append(jnp.concatenate([h[rows] for h in blocks[-2:]], axis=1))
        picked = jnp.stack(tables).reshape(2, ring // 2, 2, 3, top, tokens).transpose(1, 0, 2, 3, 4, 5)
        picked = picked.reshape(2 * ring, 3, top, tokens)
        names = ("slot_rows", "slot_cols", "share_rows")
        return dict(zip(names, routing(cap, jnp.stack([me, me ^ 1]), picked)))

    def load_weights(same, other):
        arrays = mine + [kept["w0"], kept["w1"], kept["w2"]]
        arrays, kept["slot_rows"], kept["slot_cols"] = barrier(
            (arrays, kept["slot_rows"], kept["slot_cols"])
        )
        weights, token = fetch(arrays)
        beside_weights.extend(weights)
        return {"token": token}

    beside_weights = []

    def serve(first, count, blocks):
        tables = [kept[name] for name in ("slot_rows", "slot_cols", "share_rows")]
        halves = [h for block in blocks for h in block]
        outs = experts(
            slots, first, count, *tables, halves, beside_weights + [kept["token"]], [half] * len(halves)
        )
        return [outs[i : i + 2] for i in range(0, len(outs), 2)]

    def nothing(same, other):
        return {}

    def serve_four(r):
        def step(same, other):
            p0, p1, q0, q1 = serve(r, 2, same[r : r + 2] + other[r : r + 2])
            return {("p", r): p0, ("p", r + 1): p1, ("q", r): q0, ("q", r + 1): q1}

        return step

    def serve_two(same, other):
        p0, p1 = serve(ring - 2, 1, same[-2:])
        return {("p", ring - 2): p0, ("p", ring - 1): p1}

    beside = [make_tables, load_weights]
    for r in range(0, ring - 2, 2):
        beside += [serve_four(r), nothing]
    beside[ring - 1 :] = [serve_two]
    x_same, x_other = gather_halves(normed, beside)
    q = [kept["q", r] for r in range(ring - 2)] + serve(ring - 1, 1, x_other[-2:])
    p = [kept["p", r] for r in range(ring)]

    def add(*terms):
        return sum(t.astype(jnp.float32) for t in terms).astype(jnp.bfloat16)

    r = ring - 1
    came = [None, send_backward(p[r][1])]
    extra = send_backward(q[r][1])
    crossed = [send_across(q[r][0]), None]
    later = [send_across(q[r - 1][0]), None]
    crossed[1] = send_across(add(q[r - 1][1], extra))
    came[0] = send_backward(add(p[r][0], crossed[0]))
    crossed[0] = later[0]
    for r in range(ring - 2, 0, -1):
        moving = [None, None]
        for h in (1, 0):
            total = add(p[r][h], came[h], crossed[h])
            total, behind = barrier((total, q[r - 1][h]))
            came[h] = send_backward(total)
            crossed[h] = send_across(behind)
    return finish(mixed, *[[p[0][h], came[h], crossed[h]] for h in range(2)])


def solution(mesh):
    placed = (
        P(("groups", "wide"), None),
        P(("groups", "wide"), None),
        P(("groups", "wide"), None),
        P(("groups", "wide"), None),
        P(("groups", "wide"), None, None),
        P(("groups", "wide"), None, None),
        P("groups"),
        P("wide", None),
        P(),
        P(("groups", "wide"), None),
        P(("groups", "wide"), None),
        P("wide", None, None),
        P("wide", None, None),
        P("wide", None, None),
    )
    return jax.shard_map(
        per_device,
        mesh=mesh,
        in_specs=placed,
        out_specs=P(("groups", "wide"), None),
        check_vma=False,
    )
```

time: 362 us -> 169 us (0.47)
  the two profiles are of different devices: /device:TPU:13 before, /device:TPU:0 now
where the time goes in v2:
time: 169 us; the launch traced here: 168 us
  starting transfers between devices  52.8 us (31%)
  Pallas kernels  49.2 us (29%)
  waiting for transfers between devices  45.4 us (27%)
  local copies, waits for them, and re-layouts  16.4 us (10%)
  other arithmetic  3.58 us (2%)
    ppermute x45, starting transfers between devices, sender(): return lambda x: lax.ppermute(x, 'wide', shift(*by))  48 us
    ppermute x45, waiting for transfers between devices, sender(): return lambda x: lax.ppermute(x, 'wide', shift(*by))  32.7 us
    pallas_call x3, Pallas kernels, experts(): pl.pallas_call(functools.partial(experts_kernel, first_pair, pairs, n_in,...  18 us
    pallas_call x2, Pallas kernels, attention(): pl.pallas_call(attention_kernel, grid=(1,), in_specs=[SMEM, pl.BlockSpec(...  13.2 us
    ppermute x4, waiting for transfers between devices, side_sender(): return lambda x: lax.ppermute(x, ('groups', 'wide'), pairs)  12.8 us
    unnamed x71, local copies, waits for them, and re-layouts  11.9 us
    pallas_call x1, Pallas kernels, fetch(): pl.pallas_call(fetch_kernel, in_specs=[ANY] * len(arrays), out_specs=[VME...  6.5 us
    pallas_call x1, Pallas kernels, projection(): pl.pallas_call(functools.partial(projection_kernel, len(pieces), n_blocks...  5.24 us
  transfers between devices with their start and end apart: 49, of which 17 were waited for; matrix products, arithmetic and copies ran while one was open for 7% of the time, Pallas kernels for 21%

profile of v2, /device:TPU:0, one launch (start us, length us, event | category | flops | bytes accessed | tf_op | source)
XLA Modules:
  0.0 167.9 jit_solution(2293895261256981631)
XLA Ops:
  5.6 3.0 %collective-permute-start.1 = (bf16[272,512]{1,0:T(8,128)(2,1)S(1)}, bf16[272,512]{1,0:T(8,128)(2,1)S(1)}, u32[]{:S(2)}, u32[]{:S(2)}) collective-permute-start(bf16[272,512]{1,0:T(8,128)(2,1)S(1)} %fusion.1.refs_8_), channel_id=1, source_target_pairs={{0,4},{1,5},{2,6},{3,7},{4,8},{5,9},{6,10},{7,11},{8,12},{9,13},{1... | collective-permute-start | bytes 835592 | tf_op jit(solution)/shard_map/ppermute | solution.py:452
  10.2 6.6 %attention.2.refs_0_ = bf16[128,1024]{1,0:T(8,128)(2,1)} custom-call(s32[1]{0:T(128)} %dynamic_slice.9.len_ref, bf16[128,2048]{1,0:T(8,128)(2,1)} %q_ref.3, bf16[128,256]{1,0:T(8,128)(2,1)} %nk_ref.3, bf16[128,256]{1,0:T(8,128)(2,1)} %nv_ref.3, bf16[2048,256]{1,0:T(8,128)(2,1)} %bitcast.53, bf16[2048,256]{1,0:T(8,128)(2,1)} %bitcast.55), custom_call_target="tpu_custom_call" | custom-call | flops 5368709120 | bytes 1048576 | tf_op jit(solution)/shard_map/attention/pallas_call | solution.py:96
  21.6 6.6 %attention.3.refs_1_ = bf16[128,1024]{1,0:T(8,128)(2,1)} custom-call(s32[1]{0:T(128)} %dynamic_slice.9.len_ref, bf16[128,2048]{1,0:T(8,128)(2,1)} %q_ref.3, bf16[128,256]{1,0:T(8,128)(2,1)} %nk_ref.3, bf16[128,256]{1,0:T(8,128)(2,1)} %nv_ref.3, bf16[2048,256]{1,0:T(8,128)(2,1)} %bitcast.54, bf16[2048,256]{1,0:T(8,128)(2,1)} %bitcast.56), custom_call_target="tpu_custom_call" | custom-call | flops 5368709120 | bytes 1048576 | tf_op jit(solution)/shard_map/attention/pallas_call | solution.py:96
  31.5 6.9 %collective-permute-done.11.refs_5_ = bf16[128,1024]{1,0:T(8,128)(2,1)S(1)} collective-permute-done((bf16[128,1024]{1,0:T(8,128)(2,1)}, bf16[128,1024]{1,0:T(8,128)(2,1)S(1)}, u32[]{:S(2)}, u32[]{:S(2)}) %collective-permute-start.11) | collective-permute-done | bytes 262176 | tf_op jit(solution)/shard_map/ppermute | solution.py:460
  42.4 2.3 %collective-permute-done.13.refs_15_ = bf16[272,256]{1,0:T(8,128)(2,1)S(1)} collective-permute-done((bf16[272,256]{1,0:T(8,128)(2,1)S(1)}, bf16[272,256]{1,0:T(8,128)(2,1)S(1)}, u32[]{:S(2)}, u32[]{:S(2)}) %collective-permute-start.13) | collective-permute-done | bytes 139296 | tf_op jit(solution)/shard_map/ppermute | solution.py:452
  44.7 2.8 %collective-permute-done.14.refs_16_ = bf16[272,256]{1,0:T(8,128)(2,1)S(1)} collective-permute-done((bf16[272,256]{1,0:T(8,128)(2,1)S(1)}, bf16[272,256]{1,0:T(8,128)(2,1)S(1)}, u32[]{:S(2)}, u32[]{:S(2)}) %collective-permute-start.14) | collective-permute-done | bytes 139296 | tf_op jit(solution)/shard_map/ppermute | solution.py:452
  48.9 5.2 %projection.1 = (f32[128,512]{1,0:T(8,128)}, f32[128,512]{1,0:T(8,128)}, bf16[128,512]{1,0:T(8,128)(2,1)}, bf16[128,512]{1,0:T(8,128)(2,1)}) custom-call(s32[16]{0:T(128)} %mul.52.base_ref, bf16[128,1024]{1,0:T(8,128)(2,1)} %attention.2.refs_0_, bf16[128,1024]{1,0:T(8,128)(2,1)} %attention.3.refs_1_, bf16[128,1024]{1,0:T(8,128)(2,1)} %copy-done.18, ...), custom_call_target="tpu_custom_call" | custom-call | flops 1073741824 | bytes 2097152 | tf_op jit(solution)/shard_map/projection/pallas_call | solution.py:160
  54.3 1.8 %collective-permute-start.19 = (bf16[128,512]{1,0:T(8,128)(2,1)}, bf16[128,512]{1,0:T(8,128)(2,1)S(1)}, u32[]{:S(2)}, u32[]{:S(2)}) collective-permute-start(bf16[128,512]{1,0:T(8,128)(2,1)} %get-tuple-element.146), channel_id=1, source_target_pairs={{0,16},{1,17},{2,18},{3,19},{4,20},{5,21},{6,22},{7,23},{8,24},{9,... | collective-permute-start | bytes 393224 | tf_op jit(solution)/shard_map/ppermute | solution.py:460
  56.9 4.0 %collective-permute-done.19.refs_2_ = bf16[128,512]{1,0:T(8,128)(2,1)S(1)} collective-permute-done((bf16[128,512]{1,0:T(8,128)(2,1)}, bf16[128,512]{1,0:T(8,128)(2,1)S(1)}, u32[]{:S(2)}, u32[]{:S(2)}) %collective-permute-start.19) | collective-permute-done | bytes 131104 | tf_op jit(solution)/shard_map/ppermute | solution.py:460
  60.9 1.9 %collective-permute-done.20.refs_3_ = bf16[128,512]{1,0:T(8,128)(2,1)S(1)} collective-permute-done((bf16[128,512]{1,0:T(8,128)(2,1)}, bf16[128,512]{1,0:T(8,128)(2,1)S(1)}, u32[]{:S(2)}, u32[]{:S(2)}) %collective-permute-start.20) | collective-permute-done | bytes 131104 | tf_op jit(solution)/shard_map/ppermute | solution.py:460
  63.5 2.6 %mix_and_norm.1 = (f32[128,2048]{1,0:T(8,128)}, bf16[128,1024]{1,0:T(8,128)(2,1)}, bf16[128,1024]{1,0:T(8,128)(2,1)}) custom-call(s32[4]{0:T(128)} %add_multiply_fusion.1.place_ref, bf16[128,2048]{1,0:T(8,128)(2,1)} %residual_ref.1, f32[1,2048]{1,0:T(1,128)} %bitcast.52, f32[128,512]{1,0:T(8,128)} %get-tuple-element.144.refs_0_, f32[128,512]{1,0:T(8,128)} %copy-done.25, ...), custom_call_target="tpu_custom_call" | custom-call | tf_op jit(solution)/shard_map/mix_and_norm/pallas_call | solution.py:195
  78.8 4.0 %collective-permute-done.27.refs_2_ = bf16[128,1024]{1,0:T(8,128)(2,1)S(1)} collective-permute-done((bf16[128,1024]{1,0:T(8,128)(2,1)}, bf16[128,1024]{1,0:T(8,128)(2,1)S(1)}, u32[]{:S(2)}, u32[]{:S(2)}) %collective-permute-start.27) | collective-permute-done | bytes 262176 | tf_op jit(solution)/shard_map/ppermute | solution.py:452
  83.6 6.5 %fetch.1 = (bf16[2048,768]{1,0:T(8,128)(2,1)S(1)}, bf16[2048,768]{1,0:T(8,128)(2,1)S(1)}, bf16[768,2048]{1,0:T(8,128)(2,1)S(1)}, bf16[2048,768]{1,0:T(8,128)(2,1...) custom-call(bf16[2048,768]{1,0:T(8,128)(2,1)} %bitcast.46, ...), custom_call_target="tpu_custom_call" | custom-call | tf_op jit(solution)/shard_map/fetch/pallas_call | solution.py:294
  93.7 2.6 %collective-permute-start.31 = (bf16[128,1024]{1,0:T(8,128)(2,1)S(1)}, bf16[128,1024]{1,0:T(8,128)(2,1)S(1)}, u32[]{:S(2)}, u32[]{:S(2)}) collective-permute-start(bf16[128,1024]{1,0:T(8,128)(2,1)S(1)} %collective-permute-done.29.refs_0_), channel_id=1, source_target_pairs={{0,4},{1,5},{2,6},{3,7},{4,8},{5,9},{6,10},{7,11},{8,12},{9,13},{1... | collective-permute-start | bytes 786440 | tf_op jit(solution)/shard_map/ppermute | solution.py:452
  97.1 9.8 %experts.3 = (bf16[128,1024]{1,0:T(8,128)(2,1)S(1)}, bf16[128,1024]{1,0:T(8,128)(2,1)S(1)}, bf16[128,1024]{1,0:T(8,128)(2,1)S(1)}, bf16[128,1024]{1,0:T(8,128)(2...) custom-call(s32[4,2,256]{2,1,0:T(2,128)S(1)} %get-tuple-element.177., ...), custom_call_target="tpu_custom_call" | custom-call | flops 5435817984 | bytes 18874368 | tf_op jit(solution)/shard_map/experts/pallas_call | solution.py:383
  110.7 1.9 %copy-done.1 = bf16[2048,768]{1,0:T(8,128)(2,1)S(1)} copy-done((bf16[2048,768]{1,0:T(8,128)(2,1)S(1)}, bf16[2048,768]{1,0:T(8,128)(2,1)}, u32[]{:S(2)}) %copy-start.1) | copy-done | bytes 3145752
  112.6 4.1 %experts.4 = (bf16[128,1024]{1,0:T(8,128)(2,1)S(1)}, bf16[128,1024]{1,0:T(8,128)(2,1)S(1)}, bf16[128,1024]{1,0:T(8,128)(2,1)S(1)}, bf16[128,1024]{1,0:T(8,128)(2,1)S(1)}) custom-call(s32[4,2,256]{2,1,0:T(2,128)S(1)} %get-tuple-element.177.slot_rows, s32[4,256,2]{2,1,0:T(8,128)S(1)} %get-tuple-element.178.slot_cols, ...), custom_call_target="tpu_custom_call" | custom-call | flops 2717908992 | bytes 18874368 | tf_op jit(solution)/shard_map/experts/pallas_call | solution.py:383
  117.1 4.1 %experts.5 = (bf16[128,1024]{1,0:T(8,128)(2,1)S(1)}, bf16[128,1024]{1,0:T(8,128)(2,1)S(1)}, bf16[128,1024]{1,0:T(8,128)(2,1)S(1)}, bf16[128,1024]{1,0:T(8,128)(2,1)S(1)}) custom-call(s32[4,2,256]{2,1,0:T(2,128)S(1)} %get-tuple-element.177.slot_rows, s32[4,256,2]{2,1,0:T(8,128)S(1)} %get-tuple-element.178.slot_cols, ...), custom_call_target="tpu_custom_call" | custom-call | flops 2717908992 | bytes 18874368 | tf_op jit(solution)/shard_map/experts/pallas_call | solution.py:383
  125.0 4.0 %collective-permute-done.35 = bf16[128,1024]{1,0:T(8,128)(2,1)S(1)} collective-permute-done((bf16[128,1024]{1,0:T(8,128)(2,1)S(1)}, bf16[128,1024]{1,0:T(8,128)(2,1)S(1)}, u32[]{:S(2)}, u32[]{:S(2)}) %collective-permute-start.35) | collective-permute-done | bytes 262176 | tf_op jit(solution)/shard_map/ppermute | solution.py:452
  132.6 1.9 %collective-permute-done.37 = bf16[128,1024]{1,0:T(8,128)(2,1)S(1)} collective-permute-done((bf16[128,1024]{1,0:T(8,128)(2,1)S(1)}, bf16[128,1024]{1,0:T(8,128)(2,1)S(1)}, u32[]{:S(2)}, u32[]{:S(2)}) %collective-permute-start.37) | collective-permute-done | bytes 262176 | tf_op jit(solution)/shard_map/ppermute | solution.py:452
  134.4 3.9 %collective-permute-done.36 = bf16[128,1024]{1,0:T(8,128)(2,1)S(1)} collective-permute-done((bf16[128,1024]{1,0:T(8,128)(2,1)S(1)}, bf16[128,1024]{1,0:T(8,128)(2,1)S(1)}, u32[]{:S(2)}, u32[]{:S(2)}) %collective-permute-start.36) | collective-permute-done | bytes 262176 | tf_op jit(solution)/shard_map/ppermute | solution.py:452
  138.9 2.4 %collective-permute-start.38 = (bf16[128,1024]{1,0:T(8,128)(2,1)S(1)}, bf16[128,1024]{1,0:T(8,128)(2,1)S(1)}, u32[]{:S(2)}, u32[]{:S(2)}) collective-permute-start(bf16[128,1024]{1,0:T(8,128)(2,1)S(1)} %add_convert_fusion.4), channel_id=1, source_target_pairs={{0,12},{1,13},{2,14},{3,15},{4,0},{5,1},{6,2},{7,3},{8,4},{9,5},{1... | collective-permute-start | bytes 786440 | tf_op jit(solution)/shard_map/ppermute | solution.py:452
  141.3 2.6 %collective-permute-done.42 = bf16[128,1024]{1,0:T(8,128)(2,1)S(1)} collective-permute-done((bf16[128,1024]{1,0:T(8,128)(2,1)S(1)}, bf16[128,1024]{1,0:T(8,128)(2,1)S(1)}, u32[]{:S(2)}, u32[]{:S(2)}) %collective-permute-start.42) | collective-permute-done | bytes 262176 | tf_op jit(solution)/shard_map/ppermute | solution.py:452
  144.5 2.4 %collective-permute-start.45 = (bf16[128,1024]{1,0:T(8,128)(2,1)S(1)}, bf16[128,1024]{1,0:T(8,128)(2,1)S(1)}, u32[]{:S(2)}, u32[]{:S(2)}) collective-permute-start(bf16[128,1024]{1,0:T(8,128)(2,1)S(1)} %add_convert_fusion.1), channel_id=1, source_target_pairs={{0,12},{1,13},{2,14},{3,15},{4,0},{5,1},{6,2},{7,3},{8,4},{9,5},{1... | collective-permute-start | bytes 786440 | tf_op jit(solution)/shard_map/ppermute | solution.py:452
  146.9 2.6 %collective-permute-done.38 = bf16[128,1024]{1,0:T(8,128)(2,1)S(1)} collective-permute-done((bf16[128,1024]{1,0:T(8,128)(2,1)S(1)}, bf16[128,1024]{1,0:T(8,128)(2,1)S(1)}, u32[]{:S(2)}, u32[]{:S(2)}) %collective-permute-start.38) | collective-permute-done | bytes 262176 | tf_op jit(solution)/shard_map/ppermute | solution.py:452
  149.7 2.9 %collective-permute-start.40 = (bf16[128,1024]{1,0:T(8,128)(2,1)S(1)}, bf16[128,1024]{1,0:T(8,128)(2,1)S(1)}, u32[]{:S(2)}, u32[]{:S(2)}) collective-permute-start(bf16[128,1024]{1,0:T(8,128)(2,1)S(1)} %add_convert_fusion.3), channel_id=1, source_target_pairs={{0,12},{1,13},{2,14},{3,15},{4,0},{5,1},{6,2},{7,3},{8,4},{9,5},{1... | collective-permute-start | bytes 786440 | tf_op jit(solution)/shard_map/ppermute | solution.py:452
  153.2 2.0 %collective-permute-done.45 = bf16[128,1024]{1,0:T(8,128)(2,1)S(1)} collective-permute-done((bf16[128,1024]{1,0:T(8,128)(2,1)S(1)}, bf16[128,1024]{1,0:T(8,128)(2,1)S(1)}, u32[]{:S(2)}, u32[]{:S(2)}) %collective-permute-start.45) | collective-permute-done | bytes 262176 | tf_op jit(solution)/shard_map/ppermute | solution.py:452
  155.3 2.9 %collective-permute-start.47 = (bf16[128,1024]{1,0:T(8,128)(2,1)S(1)}, bf16[128,1024]{1,0:T(8,128)(2,1)S(1)}, u32[]{:S(2)}, u32[]{:S(2)}) collective-permute-start(bf16[128,1024]{1,0:T(8,128)(2,1)S(1)} %add_convert_fusion), channel_id=1, source_target_pairs={{0,12},{1,13},{2,14},{3,15},{4,0},{5,1},{6,2},{7,3},{8,4},{9,5},{1... | collective-permute-start | bytes 786440 | tf_op jit(solution)/shard_map/ppermute | solution.py:452
  158.2 2.0 %collective-permute-start.48 = (bf16[128,1024]{1,0:T(8,128)(2,1)S(1)}, bf16[128,1024]{1,0:T(8,128)(2,1)S(1)}, u32[]{:S(2)}, u32[]{:S(2)}) collective-permute-start(bf16[128,1024]{1,0:T(8,128)(2,1)S(1)} %get-tuple-element.236), channel_id=1, source_target_pairs={{0,2},{1,3},{2,0},{3,1},{4,6},{5,7},{6,4},{7,5},{8,10},{9,11},{10,... | collective-permute-start | bytes 786440 | tf_op jit(solution)/shard_map/ppermute | solution.py:452
  160.2 1.9 %collective-permute-done.47.refs_4_ = bf16[128,1024]{1,0:T(8,128)(2,1)S(1)} collective-permute-done((bf16[128,1024]{1,0:T(8,128)(2,1)S(1)}, bf16[128,1024]{1,0:T(8,128)(2,1)S(1)}, u32[]{:S(2)}, u32[]{:S(2)}) %collective-permute-start.47) | collective-permute-done | bytes 262176 | tf_op jit(solution)/shard_map/ppermute | solution.py:452
  162.1 2.5 %collective-permute-done.48.refs_5_ = bf16[128,1024]{1,0:T(8,128)(2,1)S(1)} collective-permute-done((bf16[128,1024]{1,0:T(8,128)(2,1)S(1)}, bf16[128,1024]{1,0:T(8,128)(2,1)S(1)}, u32[]{:S(2)}, u32[]{:S(2)}) %collective-permute-start.48) | collective-permute-done | bytes 262176 | tf_op jit(solution)/shard_map/ppermute | solution.py:452
  165.3 2.7 %finish.1 = bf16[128,2048]{1,0:T(8,128)(2,1)} custom-call(f32[128,2048]{1,0:T(8,128)} %get-tuple-element.148.mixed_ref, bf16[128,1024]{1,0:T(8,128)(2,1)} %copy-done.6, bf16[128,1024]{1,0:T(8,128)(2,1)} %copy-done.23, bf16[128,1024]{1,0:T(8,128)(2,1)} %copy-done.24, bf16[128,1024]{1,0:T(8,128)(2,1)} %copy-done.7, bf16[128,1024]{1,0:T(8,128)(2,1)} %copy-done.26, ...), custom_call_target="tpu_custom_call" | custom-call | tf_op jit(solution)/shard_map/finish/pallas_call | solution.py:219
  (175 shorter events, 54.3 us)
Async XLA Ops:
  5.0 12.6 %collective-permute-start.3 = (bf16[2048,768]{1,0:T(8,128)(2,1)}, bf16[2048,768]{1,0:T(8,128)(2,1)S(1)}, u32[]{:S(2)}, u32[]{:S(2)}) collective-permute-start(bf16[2048,768]{1,0:T(8,128)(2,1)} %bitcast.45), channel_id=1, source_target_pairs={{0,1},{1,0},{2,3},{3,2},{4,5},{5,4},{6,7},{7,6},{8,9},{9,8},{10,11... | collective-permute-start | bytes 9437192 | tf_op jit(solution)/shard_map/ppermute | solution.py:452
  5.1 23.1 %collective-permute-start.7 = (bf16[2048,768]{1,0:T(8,128)(2,1)}, bf16[2048,768]{1,0:T(8,128)(2,1)}, u32[]{:S(2)}, u32[]{:S(2)}) collective-permute-start(bf16[2048,768]{1,0:T(8,128)(2,1)} %bitcast.47), channel_id=1, source_target_pairs={{0,1},{1,0},{2,3},{3,2},{4,5},{5,4},{6,7},{7,6},{8,9},{9,8},{10,11... | collective-permute-start | bytes 9437192 | tf_op jit(solution)/shard_map/ppermute | solution.py:452
  5.6 25.4 %collective-permute-start.12 = (bf16[768,2048]{1,0:T(8,128)(2,1)}, bf16[768,2048]{1,0:T(8,128)(2,1)}, u32[]{:S(2)}, u32[]{:S(2)}) collective-permute-start(bf16[768,2048]{1,0:T(8,128)(2,1)} %bitcast.49), channel_id=1, source_target_pairs={{0,1},{1,0},{2,3},{3,2},{4,5},{5,4},{6,7},{7,6},{8,9},{9,8},{10,11... | collective-permute-start | bytes 9437192 | tf_op jit(solution)/shard_map/ppermute | solution.py:452
  5.6 11.9 %collective-permute-start.1 = (bf16[272,512]{1,0:T(8,128)(2,1)S(1)}, bf16[272,512]{1,0:T(8,128)(2,1)S(1)}, u32[]{:S(2)}, u32[]{:S(2)}) collective-permute-start(bf16[272,512]{1,0:T(8,128)(2,1)S(1)} %fusion.1.refs_8_), channel_id=1, source_target_pairs={{0,4},{1,5},{2,6},{3,7},{4,8},{5,9},{6,10},{7,11},{8,12},{9,13},{1... | collective-permute-start | bytes 835592 | tf_op jit(solution)/shard_map/ppermute | solution.py:452
  17.6 10.7 %collective-permute-start.4 = (bf16[272,512]{1,0:T(8,128)(2,1)S(1)}, bf16[272,512]{1,0:T(8,128)(2,1)S(1)}, u32[]{:S(2)}, u32[]{:S(2)}) collective-permute-start(bf16[272,512]{1,0:T(8,128)(2,1)S(1)} %collective-permute-done.1.refs_9_), channel_id=1, source_target_pairs={{0,4},{1,5},{2,6},{3,7},{4,8},{5,9},{6,10},{7,11},{8,12},{9,13},{1... | collective-permute-start | bytes 835592 | tf_op jit(solution)/shard_map/ppermute | solution.py:452
  18.6 9.7 %collective-permute-start.5 = (bf16[272,512]{1,0:T(8,128)(2,1)S(1)}, bf16[272,512]{1,0:T(8,128)(2,1)S(1)}, u32[]{:S(2)}, u32[]{:S(2)}) collective-permute-start(bf16[272,512]{1,0:T(8,128)(2,1)S(1)} %collective-permute-done.1.refs_9_), channel_id=1, source_target_pairs={{0,2},{1,3},{2,0},{3,1},{4,6},{5,7},{6,4},{7,5},{8,10},{9,11},{10,... | collective-permute-start | bytes 835592 | tf_op jit(solution)/shard_map/ppermute | solution.py:452
  28.3 10.1 %collective-permute-start.8 = (bf16[272,512]{1,0:T(8,128)(2,1)S(1)}, bf16[272,512]{1,0:T(8,128)(2,1)S(1)}, u32[]{:S(2)}, u32[]{:S(2)}) collective-permute-start(bf16[272,512]{1,0:T(8,128)(2,1)S(1)} %collective-permute-done.4.refs_10_), channel_id=1, source_target_pairs={{0,4},{1,5},{2,6},{3,7},{4,8},{5,9},{6,10},{7,11},{8,12},{9,13},{1... | collective-permute-start | bytes 835592 | tf_op jit(solution)/shard_map/ppermute | solution.py:452
  28.7 9.7 %collective-permute-start.9 = (bf16[272,512]{1,0:T(8,128)(2,1)S(1)}, bf16[272,512]{1,0:T(8,128)(2,1)S(1)}, u32[]{:S(2)}, u32[]{:S(2)}) collective-permute-start(bf16[272,512]{1,0:T(8,128)(2,1)S(1)} %collective-permute-done.4.refs_10_), channel_id=1, source_target_pairs={{0,2},{1,3},{2,0},{3,1},{4,6},{5,7},{6,4},{7,5},{8,10},{9,11},{10,... | collective-permute-start | bytes 835592 | tf_op jit(solution)/shard_map/ppermute | solution.py:452
  31.0 11.4 %collective-permute-start.15 = (bf16[128,1024]{1,0:T(8,128)(2,1)}, bf16[128,1024]{1,0:T(8,128)(2,1)S(1)}, u32[]{:S(2)}, u32[]{:S(2)}) collective-permute-start(bf16[128,1024]{1,0:T(8,128)(2,1)} %attention.3.refs_1_), channel_id=1, source_target_pairs={{0,1},{1,0},{2,3},{3,2},{4,5},{5,4},{6,7},{7,6},{8,9},{9,8},{10,11... | collective-permute-start | bytes 786440 | tf_op jit(solution)/shard_map/ppermute | solution.py:452
  31.2 11.1 %collective-permute-start.16 = (bf16[128,1024]{1,0:T(8,128)(2,1)S(1)}, bf16[128,1024]{1,0:T(8,128)(2,1)S(1)}, u32[]{:S(2)}, u32[]{:S(2)}) collective-permute-start(bf16[128,1024]{1,0:T(8,128)(2,1)S(1)} %collective-permute-done.6.refs_4_), channel_id=1, source_target_pairs={{0,1},{1,0},{2,3},{3,2},{4,5},{5,4},{6,7},{7,6},{8,9},{9,8},{10,11... | collective-permute-start | bytes 786440 | tf_op jit(solution)/shard_map/ppermute | solution.py:452
  38.5 9.1 %collective-permute-start.17 = (bf16[128,1024]{1,0:T(8,128)(2,1)S(1)}, bf16[128,1024]{1,0:T(8,128)(2,1)S(1)}, u32[]{:S(2)}, u32[]{:S(2)}) collective-permute-start(bf16[128,1024]{1,0:T(8,128)(2,1)S(1)} %collective-permute-done.11.refs_5_), channel_id=1, source_target_pairs={{0,1},{1,0},{2,3},{3,2},{4,5},{5,4},{6,7},{7,6},{8,9},{9,8},{10,11... | collective-permute-start | bytes 786440 | tf_op jit(solution)/shard_map/ppermute | solution.py:452
  66.1 11.1 %collective-permute-start.21 = (bf16[128,1024]{1,0:T(8,128)(2,1)}, bf16[128,1024]{1,0:T(8,128)(2,1)S(1)}, u32[]{:S(2)}, u32[]{:S(2)}) collective-permute-start(bf16[128,1024]{1,0:T(8,128)(2,1)} %get-tuple-element.181.refs_1_), channel_id=1, source_target_pairs={{0,4},{1,5},{2,6},{3,7},{4,8},{5,9},{6,10},{7,11},{8,12},{9,13},{1... | collective-permute-start | bytes 786440 | tf_op jit(solution)/shard_map/ppermute | solution.py:452
  66.1 11.1 %collective-permute-start.22 = (bf16[128,1024]{1,0:T(8,128)(2,1)}, bf16[128,1024]{1,0:T(8,128)(2,1)S(1)}, u32[]{:S(2)}, u32[]{:S(2)}) collective-permute-start(bf16[128,1024]{1,0:T(8,128)(2,1)} %get-tuple-element.181.refs_1_), channel_id=1, source_target_pairs={{0,2},{1,3},{2,0},{3,1},{4,6},{5,7},{6,4},{7,5},{8,10},{9,11},{10,... | collective-permute-start | bytes 786440 | tf_op jit(solution)/shard_map/ppermute | solution.py:452
  66.9 16.0 %collective-permute-start.27 = (bf16[128,1024]{1,0:T(8,128)(2,1)}, bf16[128,1024]{1,0:T(8,128)(2,1)S(1)}, u32[]{:S(2)}, u32[]{:S(2)}) collective-permute-start(bf16[128,1024]{1,0:T(8,128)(2,1)} %get-tuple-element.180.refs_0_), channel_id=1, source_target_pairs={{0,4},{1,5},{2,6},{3,7},{4,8},{5,9},{6,10},{7,11},{8,12},{9,13},{1... | collective-permute-start | bytes 786440 | tf_op jit(solution)/shard_map/ppermute | solution.py:452
  68.4 14.5 %collective-permute-start.28 = (bf16[128,1024]{1,0:T(8,128)(2,1)}, bf16[128,1024]{1,0:T(8,128)(2,1)S(1)}, u32[]{:S(2)}, u32[]{:S(2)}) collective-permute-start(bf16[128,1024]{1,0:T(8,128)(2,1)} %get-tuple-element.180.refs_0_), channel_id=1, source_target_pairs={{0,2},{1,3},{2,0},{3,1},{4,6},{5,7},{6,4},{7,5},{8,10},{9,11},{10,... | collective-permute-start | bytes 786440 | tf_op jit(solution)/shard_map/ppermute | solution.py:452
  77.2 14.5 %collective-permute-start.23 = (bf16[128,1024]{1,0:T(8,128)(2,1)S(1)}, bf16[128,1024]{1,0:T(8,128)(2,1)S(1)}, u32[]{:S(2)}, u32[]{:S(2)}) collective-permute-start(bf16[128,1024]{1,0:T(8,128)(2,1)S(1)} %collective-permute-done.21.refs_3_), channel_id=1, source_target_pairs={{0,4},{1,5},{2,6},{3,7},{4,8},{5,9},{6,10},{7,11},{8,12},{9,13},{1... | collective-permute-start | bytes 786440 | tf_op jit(solution)/shard_map/ppermute | solution.py:452
  78.3 13.5 %collective-permute-start.24 = (bf16[128,1024]{1,0:T(8,128)(2,1)S(1)}, bf16[128,1024]{1,0:T(8,128)(2,1)S(1)}, u32[]{:S(2)}, u32[]{:S(2)}) collective-permute-start(bf16[128,1024]{1,0:T(8,128)(2,1)S(1)} %collective-permute-done.21.refs_3_), channel_id=1, source_target_pairs={{0,2},{1,3},{2,0},{3,1},{4,6},{5,7},{6,4},{7,5},{8,10},{9,11},{10,... | collective-permute-start | bytes 786440 | tf_op jit(solution)/shard_map/ppermute | solution.py:452
  82.8 10.8 %collective-permute-start.29 = (bf16[128,1024]{1,0:T(8,128)(2,1)S(1)}, bf16[128,1024]{1,0:T(8,128)(2,1)S(1)}, u32[]{:S(2)}, u32[]{:S(2)}) collective-permute-start(bf16[128,1024]{1,0:T(8,128)(2,1)S(1)} %collective-permute-done.27.refs_2_), channel_id=1, source_target_pairs={{0,4},{1,5},{2,6},{3,7},{4,8},{5,9},{6,10},{7,11},{8,12},{9,13},{1... | collective-permute-start | bytes 786440 | tf_op jit(solution)/shard_map/ppermute | solution.py:452
  82.8 10.8 %collective-permute-start.30 = (bf16[128,1024]{1,0:T(8,128)(2,1)S(1)}, bf16[128,1024]{1,0:T(8,128)(2,1)S(1)}, u32[]{:S(2)}, u32[]{:S(2)}) collective-permute-start(bf16[128,1024]{1,0:T(8,128)(2,1)S(1)} %collective-permute-done.27.refs_2_), channel_id=1, source_target_pairs={{0,2},{1,3},{2,0},{3,1},{4,6},{5,7},{6,4},{7,5},{8,10},{9,11},{10,... | collective-permute-start | bytes 786440 | tf_op jit(solution)/shard_map/ppermute | solution.py:452
  91.8 15.8 %collective-permute-start.25 = (bf16[128,1024]{1,0:T(8,128)(2,1)S(1)}, bf16[128,1024]{1,0:T(8,128)(2,1)S(1)}, u32[]{:S(2)}, u32[]{:S(2)}) collective-permute-start(bf16[128,1024]{1,0:T(8,128)(2,1)S(1)} %collective-permute-done.23.refs_1_), channel_id=1, source_target_pairs={{0,4},{1,5},{2,6},{3,7},{4,8},{5,9},{6,10},{7,11},{8,12},{9,13},{1... | collective-permute-start | bytes 786440 | tf_op jit(solution)/shard_map/ppermute | solution.py:452
  91.9 15.7 %collective-permute-start.26 = (bf16[128,1024]{1,0:T(8,128)(2,1)S(1)}, bf16[128,1024]{1,0:T(8,128)(2,1)S(1)}, u32[]{:S(2)}, u32[]{:S(2)}) collective-permute-start(bf16[128,1024]{1,0:T(8,128)(2,1)S(1)} %collective-permute-done.23.refs_1_), channel_id=1, source_target_pairs={{0,2},{1,3},{2,0},{3,1},{4,6},{5,7},{6,4},{7,5},{8,10},{9,11},{10,... | collective-permute-start | bytes 786440 | tf_op jit(solution)/shard_map/ppermute | solution.py:452
  93.7 13.9 %collective-permute-start.31 = (bf16[128,1024]{1,0:T(8,128)(2,1)S(1)}, bf16[128,1024]{1,0:T(8,128)(2,1)S(1)}, u32[]{:S(2)}, u32[]{:S(2)}) collective-permute-start(bf16[128,1024]{1,0:T(8,128)(2,1)S(1)} %collective-permute-done.29.refs_0_), channel_id=1, source_target_pairs={{0,4},{1,5},{2,6},{3,7},{4,8},{5,9},{6,10},{7,11},{8,12},{9,13},{1... | collective-permute-start | bytes 786440 | tf_op jit(solution)/shard_map/ppermute | solution.py:452
  96.3 11.3 %collective-permute-start.32 = (bf16[128,1024]{1,0:T(8,128)(2,1)S(1)}, bf16[128,1024]{1,0:T(8,128)(2,1)S(1)}, u32[]{:S(2)}, u32[]{:S(2)}) collective-permute-start(bf16[128,1024]{1,0:T(8,128)(2,1)S(1)} %collective-permute-done.29.refs_0_), channel_id=1, source_target_pairs={{0,2},{1,3},{2,0},{3,1},{4,6},{5,7},{6,4},{7,5},{8,10},{9,11},{10,... | collective-permute-start | bytes 786440 | tf_op jit(solution)/shard_map/ppermute | solution.py:452
  122.1 9.7 %collective-permute-start.43 = (bf16[128,1024]{1,0:T(8,128)(2,1)S(1)}, bf16[128,1024]{1,0:T(8,128)(2,1)S(1)}, u32[]{:S(2)}, u32[]{:S(2)}) collective-permute-start(bf16[128,1024]{1,0:T(8,128)(2,1)S(1)} %get-tuple-element.230), channel_id=1, source_target_pairs={{0,12},{1,13},{2,14},{3,15},{4,0},{5,1},{6,2},{7,3},{8,4},{9,5},{1... | collective-permute-start | bytes 786440 | tf_op jit(solution)/shard_map/ppermute | solution.py:452
  123.8 10.7 %collective-permute-start.37 = (bf16[128,1024]{1,0:T(8,128)(2,1)S(1)}, bf16[128,1024]{1,0:T(8,128)(2,1)S(1)}, u32[]{:S(2)}, u32[]{:S(2)}) collective-permute-start(bf16[128,1024]{1,0:T(8,128)(2,1)S(1)} %get-tuple-element.218), channel_id=1, source_target_pairs={{0,2},{1,3},{2,0},{3,1},{4,6},{5,7},{6,4},{7,5},{8,10},{9,11},{10,... | collective-permute-start | bytes 786440 | tf_op jit(solution)/shard_map/ppermute | solution.py:452
  129.0 9.3 %collective-permute-start.36 = (bf16[128,1024]{1,0:T(8,128)(2,1)S(1)}, bf16[128,1024]{1,0:T(8,128)(2,1)S(1)}, u32[]{:S(2)}, u32[]{:S(2)}) collective-permute-start(bf16[128,1024]{1,0:T(8,128)(2,1)S(1)} %add_convert_fusion.5), channel_id=1, source_target_pairs={{0,12},{1,13},{2,14},{3,15},{4,0},{5,1},{6,2},{7,3},{8,4},{9,5},{1... | collective-permute-start | bytes 786440 | tf_op jit(solution)/shard_map/ppermute | solution.py:452
  130.8 13.1 %collective-permute-start.42 = (bf16[128,1024]{1,0:T(8,128)(2,1)S(1)}, bf16[128,1024]{1,0:T(8,128)(2,1)S(1)}, u32[]{:S(2)}, u32[]{:S(2)}) collective-permute-start(bf16[128,1024]{1,0:T(8,128)(2,1)S(1)} %get-tuple-element.228), channel_id=1, source_target_pairs={{0,12},{1,13},{2,14},{3,15},{4,0},{5,1},{6,2},{7,3},{8,4},{9,5},{1... | collective-permute-start | bytes 786440 | tf_op jit(solution)/shard_map/ppermute | solution.py:452
  131.8 12.1 %collective-permute-start.44 = (bf16[128,1024]{1,0:T(8,128)(2,1)S(1)}, bf16[128,1024]{1,0:T(8,128)(2,1)S(1)}, u32[]{:S(2)}, u32[]{:S(2)}) collective-permute-start(bf16[128,1024]{1,0:T(8,128)(2,1)S(1)} %add_convert_fusion.2), channel_id=1, source_target_pairs={{0,2},{1,3},{2,0},{3,1},{4,6},{5,7},{6,4},{7,5},{8,10},{9,11},{10,... | collective-permute-start | bytes 786440 | tf_op jit(solution)/shard_map/ppermute | solution.py:452
  138.9 10.6 %collective-permute-start.38 = (bf16[128,1024]{1,0:T(8,128)(2,1)S(1)}, bf16[128,1024]{1,0:T(8,128)(2,1)S(1)}, u32[]{:S(2)}, u32[]{:S(2)}) collective-permute-start(bf16[128,1024]{1,0:T(8,128)(2,1)S(1)} %add_convert_fusion.4), channel_id=1, source_target_pairs={{0,12},{1,13},{2,14},{3,15},{4,0},{5,1},{6,2},{7,3},{8,4},{9,5},{1... | collective-permute-start | bytes 786440 | tf_op jit(solution)/shard_map/ppermute | solution.py:452
  144.1 9.1 %collective-permute-start.46 = (bf16[128,1024]{1,0:T(8,128)(2,1)S(1)}, bf16[128,1024]{1,0:T(8,128)(2,1)S(1)}, u32[]{:S(2)}, u32[]{:S(2)}) collective-permute-start(bf16[128,1024]{1,0:T(8,128)(2,1)S(1)} %get-tuple-element.233), channel_id=1, source_target_pairs={{0,2},{1,3},{2,0},{3,1},{4,6},{5,7},{6,4},{7,5},{8,10},{9,11},{10,... | collective-permute-start | bytes 786440 | tf_op jit(solution)/shard_map/ppermute | solution.py:452
  144.5 10.6 %collective-permute-start.45 = (bf16[128,1024]{1,0:T(8,128)(2,1)S(1)}, bf16[128,1024]{1,0:T(8,128)(2,1)S(1)}, u32[]{:S(2)}, u32[]{:S(2)}) collective-permute-start(bf16[128,1024]{1,0:T(8,128)(2,1)S(1)} %add_convert_fusion.1), channel_id=1, source_target_pairs={{0,12},{1,13},{2,14},{3,15},{4,0},{5,1},{6,2},{7,3},{8,4},{9,5},{1... | collective-permute-start | bytes 786440 | tf_op jit(solution)/shard_map/ppermute | solution.py:452
  149.7 10.5 %collective-permute-start.40 = (bf16[128,1024]{1,0:T(8,128)(2,1)S(1)}, bf16[128,1024]{1,0:T(8,128)(2,1)S(1)}, u32[]{:S(2)}, u32[]{:S(2)}) collective-permute-start(bf16[128,1024]{1,0:T(8,128)(2,1)S(1)} %add_convert_fusion.3), channel_id=1, source_target_pairs={{0,12},{1,13},{2,14},{3,15},{4,0},{5,1},{6,2},{7,3},{8,4},{9,5},{1... | collective-permute-start | bytes 786440 | tf_op jit(solution)/shard_map/ppermute | solution.py:452
  (49 other events, 391.5 us)

commit v3 on v2

--- a/solution.py
+++ b/solution.py
@@ -124,50 +124,50 @@
 
 
 def projection_kernel(n_pieces, n_blocks, base_ref, *refs):
-    pieces, w_refs = refs[:n_pieces], refs[n_pieces : n_pieces + n_blocks + 1]
-    outs = refs[n_pieces + n_blocks + 1 : -3]
-    left, weight, sems = refs[-3:]
+    pieces, w_refs = refs[:n_pieces], refs[n_pieces : n_pieces + n_blocks - 1]
+    left_out, sum_out, weight, sems = refs[n_pieces + n_blocks - 1 :]
     tokens, group = pieces[0].shape
     rows = weight.shape[0] // n_blocks // 2
-    half = weight.shape[1] // 2
+    each = left_out.shape[1] // group
     copies = []
-    for b in range(n_blocks + 1):
+
+    def begin(src, dst):
+        copies.append(pltpu.make_async_copy(src, dst, sems.at[len(copies)]))
+        copies[-1].start()
+
+    for b in range(n_blocks - 1):
         for part in range(2):
-            at = pl.multiple_of(base_ref[2 * min(b, n_blocks - 1) + part], rows)
-            src = w_refs[b].at[pl.ds(part * rows, rows)]
-            if b < n_blocks - 1:
-                dst = weight.at[pl.ds(at, rows)]
-            else:
-                dst = weight.at[pl.ds(at, rows), pl.ds((b - n_blocks + 1) * half, half)]
-            copies.append(pltpu.make_async_copy(src, dst, sems.at[2 * b + part]))
-            copies[-1].start()
-    each = n_pieces // len(outs)
-    for i in range(n_pieces):
-        at = (i // each) * tokens
-        left[at : at + tokens, (i % each) * group : (i % each + 1) * group] = pieces[i][...]
+            at = pl.multiple_of(base_ref[2 * b + part], rows)
+            begin(w_refs[b].at[pl.ds(part * rows, rows)], weight.at[pl.ds(at, rows)])
+    for i, piece in enumerate(pieces):
+        dst = left_out.at[pl.ds(i // each * tokens, tokens), pl.ds(i % each * group, group)]
+        begin(piece, dst)
+    for part in range(2):
+        at = pl.multiple_of(base_ref[2 * n_blocks - 2 + part], rows)
+        weight[pl.ds(at, rows), :] = jnp.zeros((rows, weight.shape[1]), weight.dtype)
     for copy in copies:
         copy.wait()
-    whole = dot(left[...], weight[...])
-    for i, out in enumerate(outs):
-        out[...] = whole[i * tokens : (i + 1) * tokens].astype(out.dtype)
-
-
-def projection(bases, pieces, blocks, types):
+    sum_out[...] = dot(left_out[...], weight[...])
+
+
+def projection(bases, pieces, count, blocks):
     tokens, group = pieces[0].shape
-    width = len(pieces) // len(types) * group
-    n_blocks = len(blocks) - 1
+    width = len(pieces) // count * group
+    n_blocks = len(blocks) + 1
     cols = blocks[0].shape[1]
     return pl.pallas_call(
         functools.partial(projection_kernel, len(pieces), n_blocks),
-        in_specs=[SMEM] + [VMEM] * len(pieces) + [ANY] * len(blocks),
-        out_specs=[VMEM] * len(types),
-        out_shape=[jax.ShapeDtypeStruct((tokens, cols), t) for t in types],
+        in_specs=[SMEM] + [ANY] * (len(pieces) + len(blocks)),
+        out_specs=[VMEM] * 2,
+        out_shape=[
+            jax.ShapeDtypeStruct((count * tokens, width), jnp.bfloat16),
+            jax.ShapeDtypeStruct((count * tokens, cols), jnp.float32),
+        ],
         scratch_shapes=[
-            pltpu.VMEM((len(types) * tokens, width), jnp.bfloat16),
             pltpu.VMEM((width, cols), jnp.bfloat16),
-            pltpu.SemaphoreType.DMA((2 * n_blocks + 2,)),
-        ],
-        compiler_params=pltpu.CompilerParams(vmem_limit_bytes=58 * MIB),
+            pltpu.SemaphoreType.DMA((2 * n_blocks - 2 + len(pieces),)),
+        ],
+        compiler_params=pltpu.CompilerParams(vmem_limit_bytes=24 * MIB),
         cost_estimate=pl.CostEstimate(
             flops=8 * tokens * width * cols, bytes_accessed=2 * width * cols, transcendentals=0
         ),
@@ -175,61 +175,133 @@
     )(bases, *pieces, *blocks)
 
 
-def norm_kernel(place_ref, residual_ref, gain_ref, *refs):
-    parts, mixed_ref, normed_refs = refs[:-3], refs[-3], refs[-2:]
-    cols, width = parts[0].shape[1], residual_ref.shape[1]
-    total = 0.0
+def complete_kernel(whole_tiles, base_ref, left_ref, sum_ref, first_ref, second_ref, *refs):
+    outs, (piece, sems) = refs[:-2], refs[-2:]
+    tokens = outs[0].shape[0]
+    half = first_ref.shape[1]
+    copies = []
+    if whole_tiles:
+        rows = piece.shape[1] // 2
+        for part in range(2):
+            at = pl.multiple_of(base_ref[part], rows)
+            src = left_ref.at[:, pl.ds(at, rows)]
+            dst = piece.at[:, pl.ds(part * rows, rows)]
+            copies.append(pltpu.make_async_copy(src, dst, sems.at[part]))
+    else:
+        copies.append(pltpu.make_async_copy(left_ref, piece, sems.at[0]))
+    for copy in copies:
+        copy.start()
+    for copy in copies:
+        copy.wait()
+    for h, w_ref in enumerate((first_ref, second_ref)):
+        cols = slice(h * half, (h + 1) * half)
+        whole = sum_ref[:, cols] + dot(piece[...], w_ref[...])
+        for i, out in enumerate(outs):
+            out[:, cols] = whole[i * tokens : (i + 1) * tokens].astype(out.dtype)
+
+
+def complete(bases, rows, left, total, last, types):
+    tokens = left.shape[0] // len(types)
+    whole_tiles = rows % HEAD == 0
+    if not whole_tiles:
+        parts = [lax.dynamic_slice_in_dim(left, bases[i], rows, 1) for i in range(2)]
+        left = jnp.concatenate(parts, axis=1)
+    w_spec = pl.BlockSpec((2 * rows, last[0].shape[1]), lambda i: (0, 0))
+    full = pl.BlockSpec(total.shape, lambda i: (0, 0))
+    out = pl.BlockSpec((tokens, total.shape[1]), lambda i: (0, 0))
+    return pl.pallas_call(
+        functools.partial(complete_kernel, whole_tiles),
+        grid=(1,),
+        in_specs=[SMEM, ANY, full, w_spec, w_spec],
+        out_specs=[out] * len(types),
+        out_shape=[jax.ShapeDtypeStruct((tokens, total.shape[1]), t) for t in types],
+        scratch_shapes=[
+            pltpu.VMEM((left.shape[0], 2 * rows), jnp.bfloat16),
+            pltpu.SemaphoreType.DMA((2,)),
+        ],
+        compiler_params=pltpu.CompilerParams(vmem_limit_bytes=24 * MIB),
+        name="complete",
+    )(bases, left, total, *last)
+
+
+def mix_kernel(place_ref, residual_ref, gain_ref, *refs):
+    parts, (mixed_ref, sent_ref) = refs[:-2], refs[-2:]
+    cols = parts[0].shape[1]
     for i, part in enumerate(parts):
-        at = pl.ds(pl.multiple_of(place_ref[i], HEAD), cols)
-        mixed = residual_ref[:, at].astype(jnp.float32) + part[...].astype(jnp.float32)
-        mixed_ref[:, at] = mixed
-        total = total + jnp.sum(mixed * mixed, axis=1, keepdims=True)
-    factor = lax.rsqrt(total / width + 1e-06)
-    half = width // 2
-    for h, normed_ref in enumerate(normed_refs):
-        at = slice(h * half, (h + 1) * half)
-        normed_ref[...] = (mixed_ref[:, at] * factor * gain_ref[:, at]).astype(jnp.bfloat16)
-
-
-def mix_and_norm(places, residual, gain, parts):
+        here = pl.ds(pl.multiple_of(place_ref[i], cols), cols)
+        there = pl.ds(pl.multiple_of(place_ref[len(parts)] + place_ref[i], cols), cols)
+        mixed = residual_ref[:, there].astype(jnp.float32) + part[...].astype(jnp.float32)
+        mixed_ref[:, here] = mixed
+        sent_ref[:, here] = (mixed * gain_ref[:, there]).astype(jnp.bfloat16)
+
+
+def mix(places, residual, gain, parts):
+    shape = (residual.shape[0], residual.shape[1] // 2)
+    residual = pltpu.with_memory_space_constraint(residual, pltpu.HBM)
     return pl.pallas_call(
-        norm_kernel,
+        mix_kernel,
         in_specs=[SMEM] + [VMEM] * (2 + len(parts)),
-        out_specs=[VMEM] * 3,
-        out_shape=[jax.ShapeDtypeStruct(residual.shape, jnp.float32)]
-        + [jax.ShapeDtypeStruct((residual.shape[0], residual.shape[1] // 2), jnp.bfloat16)] * 2,
-        compiler_params=pltpu.CompilerParams(vmem_limit_bytes=58 * MIB),
-        name="mix_and_norm",
+        out_specs=[VMEM] * 2,
+        out_shape=[
+            jax.ShapeDtypeStruct(shape, jnp.float32),
+            jax.ShapeDtypeStruct(shape, jnp.bfloat16),
+        ],
+        compiler_params=pltpu.CompilerParams(vmem_limit_bytes=24 * MIB),
+        cost_estimate=pl.CostEstimate(flops=0, bytes_accessed=0, transcendentals=0),
+        name="mix",
     )(places, residual, gain, *parts)
 
 
-def finish_kernel(mixed_ref, *refs):
+def finish_kernel(side_ref, *refs):
     out_ref = refs[-1]
     terms = (len(refs) - 1) // 2
     half = refs[0].shape[1]
     for h in range(2):
-        cols = slice(h * half, (h + 1) * half)
-        total = mixed_ref[:, cols]
-        for ref in refs[h * terms : (h + 1) * terms]:
+        total = refs[h * terms][...]
+        for ref in refs[h * terms + 1 : (h + 1) * terms]:
             total = total + ref[...].astype(jnp.float32)
-        out_ref[:, cols] = total.astype(out_ref.dtype)
-
-
-def finish(mixed, first, second):
+        at = side_ref[0] if h == 0 else 1 - side_ref[0]
+        out_ref[:, pl.ds(pl.multiple_of(at * half, half), half)] = total.astype(out_ref.dtype)
+
+
+def finish(side, first, second):
+    tokens, half = first[0].shape
+    rows = max(16, tokens // 4)
+    part = pl.BlockSpec((rows, half), lambda i: (i, 0))
     return pl.pallas_call(
         finish_kernel,
-        in_specs=[VMEM] * (1 + len(first) + len(second)),
-        out_specs=VMEM,
-        out_shape=jax.ShapeDtypeStruct(mixed.shape, jnp.bfloat16),
+        grid=(tokens // rows,),
+        in_specs=[SMEM] + [part] * (len(first) + len(second)),
+        out_specs=pl.BlockSpec((rows, 2 * half), lambda i: (i, 0)),
+        out_shape=jax.ShapeDtypeStruct((tokens, 2 * half), jnp.bfloat16),
+        compiler_params=pltpu.CompilerParams(vmem_limit_bytes=24 * MIB),
         name="finish",
-    )(mixed, *first, *second)
-
-
-def routing_kernel(cap, served_ref, table_ref, rows_ref, cols_ref, shares_ref, mask):
-    blocks, _, _, tokens = table_ref.shape
-    for b in range(blocks):
-        ids = table_ref[b, 0].astype(jnp.float32)
-        share = table_ref[b, 1].astype(jnp.float32) + table_ref[b, 2].astype(jnp.float32)
+    )(side, *first, *second)
+
+
+def routing_kernel(cap, n_blocks, served_ref, *refs):
+    sources, refs = refs[: n_blocks + 1], refs[n_blocks + 1 :]
+    rows_ref, cols_ref, shares_ref, table_ref, mask, sems = refs
+    tokens = mask.shape[1]
+    top, lines, width = 8, table_ref.shape[1], table_ref.shape[2]
+    copies = []
+    for b, source in enumerate(sources):
+        src = source.at[pl.ds(source.shape[0] - lines, lines)]
+        if b < n_blocks - 1:
+            dst = table_ref.at[b]
+        else:
+            at = (b - n_blocks + 1) * (width // 2)
+            dst = table_ref.at[n_blocks - 1, :, pl.ds(at, width // 2)]
+        copies.append(pltpu.make_async_copy(src, dst, sems.at[b]))
+        copies[-1].start()
+    for copy in copies:
+        copy.wait()
+    for b in range(n_blocks):
+        parts = [
+            table_ref[b, :, i * tokens : (i + 1) * tokens].astype(jnp.float32)[:top]
+            for i in range(3)
+        ]
+        ids, share = parts[0], parts[1] + parts[2]
         at = slice(b % 2 * tokens, (b % 2 + 1) * tokens)
         for e in range(2):
             hit = ids == served_ref[e].astype(jnp.float32)
@@ -250,30 +322,36 @@
     columns = lax.dot_general(
         same, slot.astype(jnp.bfloat16), (((1,), (1,)), ((), ())), preferred_element_type=jnp.float32
     )
-    for b in range(blocks):
+    for b in range(n_blocks):
         at = slice(b % 2 * tokens, (b % 2 + 1) * tokens)
-        lines = slice(2 * b, 2 * b + 2)
-        rows_ref[b // 2, :, at] = slot[lines].astype(jnp.int32)
-        cols_ref[b // 2, at, :] = columns[:, lines].astype(jnp.int32)
-
-
-def routing(cap, served, table):
-    blocks, _, _, tokens = table.shape
-    pairs = blocks // 2
+        pair = slice(2 * b, 2 * b + 2)
+        rows_ref[b // 2, :, at] = slot[pair].astype(jnp.int32)
+        cols_ref[b // 2, at, :] = columns[:, pair].astype(jnp.int32)
+
+
+def routing(cap, tokens, lines, served, blocks):
+    blocks = [pltpu.with_memory_space_constraint(b, pltpu.HBM) for b in blocks]
+    n_blocks = len(blocks) - 1
+    pairs = n_blocks // 2
     rows = jax.ShapeDtypeStruct((pairs, 2, 2 * tokens), jnp.int32)
     return pl.pallas_call(
-        functools.partial(routing_kernel, cap),
-        in_specs=[SMEM, VMEM],
+        functools.partial(routing_kernel, cap, n_blocks),
+        in_specs=[SMEM] + [ANY] * len(blocks),
         out_specs=[VMEM] * 3,
         out_shape=[
             rows,
             jax.ShapeDtypeStruct((pairs, 2 * tokens, 2), jnp.int32),
             jax.ShapeDtypeStruct(rows.shape, jnp.float32),
         ],
-        scratch_shapes=[pltpu.VMEM((2 * blocks, tokens), jnp.float32)],
+        scratch_shapes=[
+            pltpu.VMEM((n_blocks, lines, blocks[0].shape[1]), jnp.bfloat16),
+            pltpu.VMEM((2 * n_blocks, tokens), jnp.float32),
+            pltpu.SemaphoreType.DMA((n_blocks + 1,)),
+        ],
         compiler_params=pltpu.CompilerParams(vmem_limit_bytes=16 * MIB),
+        cost_estimate=pl.CostEstimate(flops=0, bytes_accessed=0, transcendentals=0),
         name="routing",
-    )(served, table)
+    )(served, *blocks)
 
 
 def fetch_kernel(*refs):
@@ -299,12 +377,13 @@
         + [jax.ShapeDtypeStruct((8, HEAD), jnp.float32)],
         scratch_shapes=[pltpu.SemaphoreType.DMA((len(arrays),))],
         compiler_params=pltpu.CompilerParams(vmem_limit_bytes=24 * MIB),
+        cost_estimate=pl.CostEstimate(flops=0, bytes_accessed=0, transcendentals=0),
         name="fetch",
     )(*arrays)
     return there, token
 
 
-def experts_kernel(first_pair, pairs, n_in, n_out, slots, slot_rows, slot_cols, share_rows, *refs):
+def experts_kernel(first_pair, pairs, n_in, n_out, slots, side_ref, gain_ref, slot_rows, slot_cols, share_rows, *refs):
     x_refs = refs[:n_in]
     w_refs = refs[n_in : n_in + 6]
     out_refs = refs[n_in + 7 : n_in + 7 + n_out]
@@ -314,16 +393,13 @@
     block = pair_tokens // 2
     hidden = act.shape[1]
 
+    half = depth // 2
+    starts = [pl.multiple_of(side_ref[0] * half, half), pl.multiple_of((1 - side_ref[0]) * half, half)]
     x_copies = []
-    at, col = 0, 0
     for i in range(n_in):
-        wide = x_refs[i].shape[1]
-        dst = xs.at[pl.ds(at, block), pl.ds(col, wide)]
+        dst = xs.at[pl.ds(i // 2 * block, block), pl.ds(starts[i % 2], half)]
         x_copies.append(pltpu.make_async_copy(x_refs[i], dst, x_sem.at[i]))
         x_copies[-1].start()
-        col += wide
-        if col == depth:
-            at, col = at + block, 0
     for copy in x_copies:
         copy.wait()
 
@@ -344,47 +420,43 @@
             rows_in[0, p * slots : (p + 1) * slots, c : c + step] = got[:slots]
             rows_in[1, p * slots : (p + 1) * slots, c : c + step] = got[slots:]
 
+    inverse = 1.0 / gain_ref[...]
     for e in range(2):
         x = rows_in[e]
-        gate = dot(x, w_refs[3 * e][...])
-        up = dot(x, w_refs[3 * e + 1][...])
+        squares = 0.0
+        for c in range(0, depth, HEAD):
+            part = x[:, c : c + HEAD].astype(jnp.float32) * inverse[:, c : c + HEAD]
+            squares = squares + part * part
+        factor = lax.rsqrt(jnp.sum(squares, axis=1, keepdims=True) / depth + 1e-06)
+        gate = dot(x, w_refs[3 * e][...]) * factor
+        up = dot(x, w_refs[3 * e + 1][...]) * factor
         act[...] = (gate / (1.0 + jnp.exp(-gate)) * up).astype(jnp.bfloat16)
         share = jnp.concatenate([s[e * slots : (e + 1) * slots] for s in shares], axis=0)
         y = (dot(act[...], w_refs[3 * e + 2][...]) * share).astype(jnp.bfloat16)
         for p in range(pairs):
             scaled[p, e * slots : (e + 1) * slots, :] = y[p * slots : (p + 1) * slots]
 
-    o = 0
     for p in range(pairs):
         lane = lax.broadcasted_iota(jnp.int32, (pair_tokens, 2 * slots), 1)
         back = lane == slot_cols[first_pair + p, :, 0:1]
         back = back | (lane - slots == slot_cols[first_pair + p, :, 1:2])
         back = jnp.where(back, 1.0, 0.0).astype(jnp.bfloat16)
-        place = []
-        for b in range(2):
-            start = 0
-            while start < depth:
-                place.append((b, start, out_refs[o]))
-                start += out_refs[o].shape[1]
-                o += 1
-        step = min(1024, depth)
-        for c in range(0, depth, step):
-            got = dot(back, scaled[p, :, c : c + step]).astype(jnp.bfloat16)
-            for b, start, ref in place:
-                if start <= c < start + ref.shape[1]:
-                    ref[:, c - start : c - start + step] = got[b * block : (b + 1) * block]
-
-
-def experts(slots, first_pair, pairs, slot_rows, slot_cols, share_rows, x_parts, weights, out_widths):
+        for h in range(2):
+            got = dot(back, scaled[p, :, pl.ds(starts[h], half)]).astype(jnp.bfloat16)
+            for b in range(2):
+                out_refs[4 * p + 2 * b + h][...] = got[b * block : (b + 1) * block]
+
+
+def experts(slots, first_pair, pairs, side, gain, slot_rows, slot_cols, share_rows, x_parts, weights):
     pair_tokens = slot_rows.shape[2]
     block = pair_tokens // 2
     depth, hidden = weights[0].shape
-    n_in, n_out = len(x_parts), len(out_widths)
+    n_in = n_out = len(x_parts)
     return pl.pallas_call(
         functools.partial(experts_kernel, first_pair, pairs, n_in, n_out, slots),
-        in_specs=[VMEM, VMEM, VMEM] + [ANY] * n_in + [VMEM] * 6 + [ANY],
+        in_specs=[SMEM] + [VMEM] * 4 + [ANY] * n_in + [VMEM] * 6 + [ANY],
         out_specs=[VMEM] * n_out,
-        out_shape=[jax.ShapeDtypeStruct((block, w), jnp.bfloat16) for w in out_widths],
+        out_shape=[jax.ShapeDtypeStruct((block, depth // 2), jnp.bfloat16)] * n_out,
         scratch_shapes=[
             pltpu.VMEM((pairs * pair_tokens, depth), jnp.bfloat16),
             pltpu.VMEM((2, pairs * slots, depth), jnp.bfloat16),
@@ -392,14 +464,14 @@
             pltpu.VMEM((pairs, 2 * slots, depth), jnp.bfloat16),
             pltpu.SemaphoreType.DMA((n_in,)),
         ],
-        compiler_params=pltpu.CompilerParams(vmem_limit_bytes=32 * MIB),
+        compiler_params=pltpu.CompilerParams(vmem_limit_bytes=22 * MIB),
         cost_estimate=pl.CostEstimate(
             flops=12 * pairs * slots * depth * hidden,
             bytes_accessed=12 * depth * hidden,
             transcendentals=0,
         ),
         name="experts",
-    )(slot_rows, slot_cols, share_rows, *x_parts, *weights)
+    )(side, gain, slot_rows, slot_cols, share_rows, *x_parts, *weights)
 
 
 def permutations(devices):
@@ -480,11 +552,13 @@
             kept.update(new)
         return same, other, last
 
-    def gather_halves(own, beside):
+    def gather_halves(own, beside, held):
         same, other = [list(own)], []
         for r in range(1, ring):
             moved = [send_forward(h) for h in same[-1]]
             crossed = [send_across(h) for h in same[-1]]
+            if r == 1:
+                same[0] = list(held)
             new = beside[r - 1](same, other) if r <= len(beside) else {}
             moved[0], crossed[0] = barrier((moved[0], crossed[0]))
             moved[1], crossed[1], new = barrier((moved[1], crossed[1], new))
@@ -500,6 +574,9 @@
 
     kept = {}
 
+    def nothing(same, other):
+        return {}
+
     cols = depth // 4
     quarter = 2 * side + core
     keep = lax.dynamic_slice_in_dim(o_weight, quarter * cols, cols, 1)
@@ -507,15 +584,16 @@
     shares = gate_raw / jnp.sum(gate_raw, axis=-1, keepdims=True)
     high = shares.astype(jnp.bfloat16)
     low = (shares - high.astype(jnp.float32)).astype(jnp.bfloat16)
-    table = jnp.stack([expert_ids.astype(jnp.bfloat16), high, low]).transpose(0, 2, 1)
-    table = table.reshape(-1, cols)
-    table_rows = table.shape[0]
-    table = jnp.pad(table, ((0, -table_rows % 16), (0, 0)))
+    table = jnp.concatenate([expert_ids.astype(jnp.bfloat16).T, high.T, low.T], axis=1)
+    lines = 16
+    table = jnp.pad(table, ((0, lines - top), (0, cols - 3 * tokens)))
     own_block = jnp.concatenate([keep, send_core(give), table], axis=0)
     length = lax.dynamic_slice_in_dim(cache_len, me, 1, 0)
     mine = [w_gate[0], w_up[0], w_down[0]]
     length, own_block, mine = barrier((length, own_block, mine))
     operands = (queries, new_keys, new_values, cache_keys[0], cache_values[0])
+
+    late = {}
 
     def attend_first(same, other):
         return {"a0": attention(0, 2, length, *operands), "w0": send_core(mine[0])}
@@ -529,55 +607,54 @@
         }
 
     def swap_first(same, other):
-        return {
-            "side1": send_side(kept["a1"]),
-            "core0": send_core(kept["a0"]),
-            "w2": send_core(mine[2]),
-        }
-
-    def swap_second(same, other):
-        return {
-            "core1": send_core(kept["a1"]),
-            "corner0": send_core(kept["side0"]),
-            "corner1": send_core(kept["side1"]),
-        }
-
-    w_same, w_other, w_last = gather_whole(
-        own_block, [attend_first, attend_second, swap_first, swap_second]
-    )
+        late["side1"] = send_side(kept["a1"])
+        return {"core0": send_core(kept["a0"]), "w2": send_core(mine[2])}
+
     offsets = jnp.arange(ring, dtype=jnp.int32)
     rings = (place - offsets) % ring
     first_of = jnp.concatenate([rings * 2 + row, rings * 2 + 1 - row]) * 2
     bases = jnp.stack([first_of + core, first_of + 1 - core], axis=1).reshape(-1)
-    pieces = [kept[name + str(g)] for name in ("a", "core", "side", "corner") for g in range(2)]
-    own_part, core_part, side_part, corner_part = projection(
-        bases * o_weight.shape[0],
-        pieces,
-        w_same + w_other + w_last,
-        [jnp.float32, jnp.float32, jnp.bfloat16, jnp.bfloat16],
+    bases = bases * o_weight.shape[0]
+
+    def project(same, other):
+        kept["core1"] = send_core(kept["a1"])
+        kept["corner0"] = send_core(kept["side0"])
+        kept["corner1"] = send_core(late["side1"])
+        kept.update(late)
+        pieces = [kept[name + str(g)] for name in ("a", "core", "side", "corner") for g in range(2)]
+        left, total = projection(bases, pieces, 4, same + other)
+        return {"left": left, "sum": total}
+
+    w_same, w_other, w_last = gather_whole(
+        own_block, [attend_first, attend_second, swap_first] + [nothing] * (ring - 4) + [project]
     )
-    parts = [own_part, send_core(core_part), send_side(side_part), send_corner(corner_part)]
-    places = jnp.stack([quarter, quarter ^ 1, quarter ^ 2, quarter ^ 3]).astype(jnp.int32) * cols
-    mixed, *normed = mix_and_norm(places, residual, norm_gain.reshape(1, -1), parts)
-
+    types = [jnp.float32, jnp.float32, jnp.bfloat16, jnp.bfloat16]
+    own_part, core_part, side_part, corner_part = complete(
+        bases[-2:], o_weight.shape[0], kept["left"], kept["sum"], w_last, types
+    )
+
+    gain = norm_gain.reshape(1, -1)
+    near = [own_part, send_core(core_part)]
+    far = [send_side(side_part), send_corner(corner_part)]
+    here = [core * cols, (1 - core) * cols]
+    mixed_near, x_near = mix(jnp.stack(here + [side * half]).astype(jnp.int32), residual, gain, near)
+    far_places = jnp.stack(here + [(1 - side) * half]).astype(jnp.int32)
     cap = tokens * top // devices + max(2, tokens * top // (8 * devices))
     slots = -(-2 * cap // 16) * 16
-
-    def make_tables(same, other):
-        rows = slice(own_block.shape[0] - table.shape[0], own_block.shape[0] - table.shape[0] + table_rows)
-        blocks, same[0] = barrier((w_same + w_other + w_last, same[0]))
-        tables = [b[rows] for b in blocks[:-2]]
-        tables.append(jnp.concatenate([h[rows] for h in blocks[-2:]], axis=1))
-        picked = jnp.stack(tables).reshape(2, ring // 2, 2, 3, top, tokens).transpose(1, 0, 2, 3, 4, 5)
-        picked = picked.reshape(2 * ring, 3, top, tokens)
-        names = ("slot_rows", "slot_cols", "share_rows")
-        return dict(zip(names, routing(cap, jnp.stack([me, me ^ 1]), picked)))
+    served = jnp.stack([me, me ^ 1])
+    w_blocks, x_near_later = barrier((w_same + w_other + w_last, x_near))
+    order = []
+    for r in range(0, ring, 2):
+        order += w_blocks[r : r + 2] + w_blocks[ring + r : ring + r + 2]
+    order.append(w_blocks[-1])
+    tables = routing(cap, tokens, lines, served, order)
+    far, tables = barrier((far, tables))
+    mixed_far, x_far = mix(far_places, residual, gain, far)
+    side_word = side.astype(jnp.int32).reshape(1)
 
     def load_weights(same, other):
         arrays = mine + [kept["w0"], kept["w1"], kept["w2"]]
-        arrays, kept["slot_rows"], kept["slot_cols"] = barrier(
-            (arrays, kept["slot_rows"], kept["slot_cols"])
-        )
+        arrays, kept["tables"], same[1][1] = barrier((arrays, tables, same[1][1]))
         weights, token = fetch(arrays)
         beside_weights.extend(weights)
         return {"token": token}
@@ -585,20 +662,22 @@
     beside_weights = []
 
     def serve(first, count, blocks):
-        tables = [kept[name] for name in ("slot_rows", "slot_cols", "share_rows")]
         halves = [h for block in blocks for h in block]
-        outs = experts(
-            slots, first, count, *tables, halves, beside_weights + [kept["token"]], [half] * len(halves)
-        )
+        weights = beside_weights + [kept["token"]]
+        outs = experts(slots, first, count, side_word, gain, *kept["tables"], halves, weights)
         return [outs[i : i + 2] for i in range(0, len(outs), 2)]
 
-    def nothing(same, other):
-        return {}
-
-    def serve_four(r):
+    def serve_same(r):
         def step(same, other):
-            p0, p1, q0, q1 = serve(r, 2, same[r : r + 2] + other[r : r + 2])
-            return {("p", r): p0, ("p", r + 1): p1, ("q", r): q0, ("q", r + 1): q1}
+            p0, p1 = serve(r, 1, same[r : r + 2])
+            return {("p", r): p0, ("p", r + 1): p1}
+
+        return step
+
+    def serve_other(r):
+        def step(same, other):
+            q0, q1 = serve(r + 1, 1, other[r : r + 2])
+            return {("q", r): q0, ("q", r + 1): q1}
 
         return step
 
@@ -606,13 +685,14 @@
         p0, p1 = serve(ring - 2, 1, same[-2:])
         return {("p", ring - 2): p0, ("p", ring - 1): p1}
 
-    beside = [make_tables, load_weights]
-    for r in range(0, ring - 2, 2):
-        beside += [serve_four(r), nothing]
-    beside[ring - 1 :] = [serve_two]
-    x_same, x_other = gather_halves(normed, beside)
-    q = [kept["q", r] for r in range(ring - 2)] + serve(ring - 1, 1, x_other[-2:])
-    p = [kept["p", r] for r in range(ring)]
+    beside = [nothing, load_weights, serve_other(0)]
+    for r in range(2, ring - 2, 2):
+        beside += [serve_same(r), serve_other(r)]
+    beside.append(serve_two)
+    x_same, x_other = gather_halves([x_near, x_far], beside, [x_near_later, x_far])
+    p = [None, None] + [kept["p", r] for r in range(2, ring)]
+    q = [kept["q", r] for r in range(ring - 2)]
+    q += serve(ring - 1, 1, x_other[-2:])
 
     def add(*terms):
         return sum(t.astype(jnp.float32) for t in terms).astype(jnp.bfloat16)
@@ -622,6 +702,7 @@
     extra = send_backward(q[r][1])
     crossed = [send_across(q[r][0]), None]
     later = [send_across(q[r - 1][0]), None]
+    p[0], p[1] = serve(0, 1, x_same[:2])
     crossed[1] = send_across(add(q[r - 1][1], extra))
     came[0] = send_backward(add(p[r][0], crossed[0]))
     crossed[0] = later[0]
@@ -630,9 +711,9 @@
         for h in (1, 0):
             total = add(p[r][h], came[h], crossed[h])
             total, behind = barrier((total, q[r - 1][h]))
-            came[h] = send_backward(total)
-            crossed[h] = send_across(behind)
-    return finish(mixed, *[[p[0][h], came[h], crossed[h]] for h in range(2)])
+            came[h], crossed[h] = send_backward(total), send_across(behind)
+    mixed = [mixed_near, mixed_far]
+    return finish(side_word, *[[mixed[h], p[0][h], came[h], crossed[h]] for h in range(2)])
 
 
 def solution(mesh):

time: 169 us -> 151 us (0.89)
  starting transfers between devices: 52.8 us -> 40.2 us
  local copies, waits for them, and re-layouts: 16.4 us -> 4.96 us
  waiting for transfers between devices: 45.4 us -> 52.4 us
    ppermute x45, waiting for transfers between devices: 32.7 us -> 45.7 us  [sender(): return lambda x: lax.ppermute(x, 'wide', shift(*by))]
    ppermute x45, starting transfers between devices: 48 us -> 36.1 us  [sender(): return lambda x: lax.ppermute(x, 'wide', shift(*by))]
    unnamed x71 -> x24, local copies, waits for them, and re-layouts: 11.9 us -> 0.99 us
    ppermute x4, waiting for transfers between devices: 12.8 us -> 6.74 us  [side_sender(): return lambda x: lax.ppermute(x, ('groups', 'wide'), pairs)]
    pallas_call x3 -> x4, Pallas kernels: 18 us -> 17.5 us  [experts(): pl.pallas_call(functools.partial(experts_kernel, first_pair, pairs, n_in,...]
    pallas_call x3 -> x5, Pallas kernels: 6.27 us -> 6.67 us  [the longest x2 2.27 us: mix(): pl.pallas_call(mix_kernel, in_specs=[SMEM] + [VMEM] * (2 + len(parts)), o...]
  transfers between devices with their start and end apart: 49 -> 49, of which waited for: 17 -> 21; matrix products, arithmetic and copies ran while one was open for 7% -> 4% of each run, Pallas kernels for 21% -> 28%
where the time goes in v3:
time: 151 us; the launch traced here: 150 us
  waiting for transfers between devices  52.4 us (35%)
  Pallas kernels  49.1 us (33%)
  starting transfers between devices  40.2 us (27%)
  local copies, waits for them, and re-layouts  4.96 us (3%)
  other arithmetic  3.07 us (2%)
    ppermute x45, waiting for transfers between devices, sender(): return lambda x: lax.ppermute(x, 'wide', shift(*by))  45.7 us
    ppermute x45, starting transfers between devices, sender(): return lambda x: lax.ppermute(x, 'wide', shift(*by))  36.1 us
    pallas_call x4, Pallas kernels, experts(): pl.pallas_call(functools.partial(experts_kernel, first_pair, pairs, n_in,...  17.5 us
    pallas_call x2, Pallas kernels, attention(): pl.pallas_call(attention_kernel, grid=(1,), in_specs=[SMEM, pl.BlockSpec(...  12.9 us
    ppermute x4, waiting for transfers between devices, side_sender(): return lambda x: lax.ppermute(x, ('groups', 'wide'), pairs)  6.74 us
    pallas_call x1, Pallas kernels, fetch(): pl.pallas_call(fetch_kernel, in_specs=[ANY] * len(arrays), out_specs=[VME...  6.49 us
    pallas_call x1, Pallas kernels, projection(): pl.pallas_call(functools.partial(projection_kernel, len(pieces), n_blocks...  5.54 us
    ppermute x4, starting transfers between devices, side_sender(): return lambda x: lax.ppermute(x, ('groups', 'wide'), pairs)  4.07 us
  transfers between devices with their start and end apart: 49, of which 21 were waited for; matrix products, arithmetic and copies ran while one was open for 4% of the time, Pallas kernels for 28%

profile of v3, /device:TPU:0, one launch (start us, length us, event | category | flops | bytes accessed | tf_op | source)
XLA Modules:
  0.0 150.2 jit_solution(4875529221760752927)
XLA Ops:
  5.5 3.0 %collective-permute-start.1 = (bf16[272,512]{1,0:T(8,128)(2,1)S(1)}, bf16[272,512]{1,0:T(8,128)(2,1)S(1)}, u32[]{:S(2)}, u32[]{:S(2)}) collective-permute-start(bf16[272,512]{1,0:T(8,128)(2,1)S(1)} %pad_maximum_fusion.refs_8_.refs_0_), channel_id=1, source_target_pairs={{0,4},{1,5},{2,6},{3,7},{4,8},{5,9},{6,10},{7,11},{8,12},{9,13},{1... | collective-permute-start | bytes 835592 | tf_op jit(solution)/shard_map/ppermute | solution.py:524
  8.5 1.5 %collective-permute-start.2 = (bf16[272,512]{1,0:T(8,128)(2,1)S(1)}, bf16[272,512]{1,0:T(8,128)(2,1)S(1)}, u32[]{:S(2)}, u32[]{:S(2)}) collective-permute-start(bf16[272,512]{1,0:T(8,128)(2,1)S(1)} %pad_maximum_fusion.refs_8_.refs_0_), channel_id=1, source_target_pairs={{0,2},{1,3},{2,0},{3,1},{4,6},{5,7},{6,4},{7,5},{8,10},{9,11},{10,... | collective-permute-start | bytes 835592 | tf_op jit(solution)/shard_map/ppermute | solution.py:524
  10.1 6.5 %attention.2.refs_0_ = bf16[128,1024]{1,0:T(8,128)(2,1)} custom-call(s32[1]{0:T(128)} %dynamic_slice.9.len_ref, bf16[128,2048]{1,0:T(8,128)(2,1)} %q_ref.3, bf16[128,256]{1,0:T(8,128)(2,1)} %nk_ref.3, bf16[128,256]{1,0:T(8,128)(2,1)} %nv_ref.3, bf16[2048,256]{1,0:T(8,128)(2,1)} %bitcast.35, bf16[2048,256]{1,0:T(8,128)(2,1)} %bitcast.37), custom_call_target="tpu_custom_call" | custom-call | flops 5368709120 | bytes 1048576 | tf_op jit(solution)/shard_map/attention/pallas_call | solution.py:96
  18.5 1.5 %collective-permute-start.5 = (bf16[272,512]{1,0:T(8,128)(2,1)S(1)}, bf16[272,512]{1,0:T(8,128)(2,1)S(1)}, u32[]{:S(2)}, u32[]{:S(2)}) collective-permute-start(bf16[272,512]{1,0:T(8,128)(2,1)S(1)} %collective-permute-done.1.refs_9_.refs_1_), channel_id=1, source_target_pairs={{0,2},{1,3},{2,0},{3,1},{4,6},{5,7},{6,4},{7,5},{8,10},{9,11},{10,... | collective-permute-start | bytes 835592 | tf_op jit(solution)/shard_map/ppermute | solution.py:524
  20.0 1.5 collective-permute-start.6
  21.5 6.5 %attention.3.refs_1_ = bf16[128,1024]{1,0:T(8,128)(2,1)} custom-call(s32[1]{0:T(128)} %dynamic_slice.9.len_ref, bf16[128,2048]{1,0:T(8,128)(2,1)} %q_ref.3, bf16[128,256]{1,0:T(8,128)(2,1)} %nk_ref.3, bf16[128,256]{1,0:T(8,128)(2,1)} %nv_ref.3, bf16[2048,256]{1,0:T(8,128)(2,1)} %bitcast.36, bf16[2048,256]{1,0:T(8,128)(2,1)} %bitcast.38), custom_call_target="tpu_custom_call" | custom-call | flops 5368709120 | bytes 1048576 | tf_op jit(solution)/shard_map/attention/pallas_call | solution.py:96
  28.8 1.4 collective-permute-start.8
  31.4 5.6 %collective-permute-done.15.refs_5_ = bf16[128,1024]{1,0:T(8,128)(2,1)S(1)} collective-permute-done((bf16[128,1024]{1,0:T(8,128)(2,1)}, bf16[128,1024]{1,0:T(8,128)(2,1)S(1)}, u32[]{:S(2)}, u32[]{:S(2)}) %collective-permute-start.15) | collective-permute-done | bytes 262176 | tf_op jit(solution)/shard_map/ppermute | solution.py:532
  37.1 1.9 %collective-permute-done.8.refs_11_.refs_5_ = bf16[272,512]{1,0:T(8,128)(2,1)S(1)} collective-permute-done((bf16[272,512]{1,0:T(8,128)(2,1)S(1)}, bf16[272,512]{1,0:T(8,128)(2,1)S(1)}, u32[]{:S(2)}, u32[]{:S(2)}) %collective-permute-start.8) | collective-permute-done | bytes 278560 | tf_op jit(solution)/shard_map/ppermute | solution.py:524
  42.5 5.5 %projection.1 = (bf16[512,2048]{1,0:T(8,128)(2,1)S(1)}, f32[512,512]{1,0:T(8,128)S(1)}) custom-call(s32[16]{0:T(128)S(1)} %mul.65.base_ref, bf16[128,1024]{1,0:T(8,128)(2,1)S(1)} %copy-done.10, bf16[128,1024]{1,0:T(8,128)(2,1)S(1)} %copy-done.11, bf16[128,1024]{1,0:T(8,128)(2,1)S(1)} %collective-permute-done.10.refs_2_, ...), custom_call_target="tpu_custom_call" | custom-call | flops 1073741824 | bytes 2097152 | tf_op jit(solution)/shard_map/projection/pallas_call | solution.py:158
  52.5 1.8 %collective-permute-start.23 = (bf16[128,1024]{1,0:T(8,128)(2,1)S(1)}, bf16[128,1024]{1,0:T(8,128)(2,1)S(1)}, u32[]{:S(2)}, u32[]{:S(2)}) collective-permute-start(bf16[128,1024]{1,0:T(8,128)(2,1)S(1)} %get-tuple-element.175.refs_0_), channel_id=1, source_target_pairs={{0,4},{1,5},{2,6},{3,7},{4,8},{5,9},{6,10},{7,11},{8,12},{9,13},{1... | collective-permute-start | bytes 786440 | tf_op jit(solution)/shard_map/ppermute | solution.py:524
  54.6 1.9 %routing.1 = (s32[4,2,256]{2,1,0:T(2,128)S(1)}, s32[4,256,2]{2,1,0:T(8,128)S(1)}, f32[4,2,256]{2,1,0:T(2,128)S(1)}) custom-call(s32[2]{0:T(128)S(1)} %pad_add_fusion.2.served_ref, bf16[272,512]{1,0:T(8,128)(2,1)} %copy-done, bf16[272,512]{1,0:T(8,128)(2,1)} %copy-done.3, bf16[272,512]{1,0:T(8,128)(2,1)} %copy-done.4, bf16[272,512]{1,0:T(8,128)(2,1)} %copy-done.6, ...), custom_call_target="tpu_custom_call" | custom-call | tf_op jit(solution)/shard_map/routing/pallas_call | solution.py:337
  58.8 1.8 %collective-permute-start.21 = (bf16[128,1024]{1,0:T(8,128)(2,1)S(1)}, bf16[128,1024]{1,0:T(8,128)(2,1)S(1)}, u32[]{:S(2)}, u32[]{:S(2)}) collective-permute-start(bf16[128,1024]{1,0:T(8,128)(2,1)S(1)} %get-tuple-element.170.refs_1_), channel_id=1, source_target_pairs={{0,4},{1,5},{2,6},{3,7},{4,8},{5,9},{6,10},{7,11},{8,12},{9,13},{1... | collective-permute-start | bytes 786440 | tf_op jit(solution)/shard_map/ppermute | solution.py:524
  60.9 2.1 %collective-permute-done.23.refs_2_ = bf16[128,1024]{1,0:T(8,128)(2,1)S(1)} collective-permute-done((bf16[128,1024]{1,0:T(8,128)(2,1)S(1)}, bf16[128,1024]{1,0:T(8,128)(2,1)S(1)}, u32[]{:S(2)}, u32[]{:S(2)}) %collective-permute-start.23) | collective-permute-done | bytes 262176 | tf_op jit(solution)/shard_map/ppermute | solution.py:524
  64.9 4.9 %collective-permute-done.21.refs_3_ = bf16[128,1024]{1,0:T(8,128)(2,1)S(1)} collective-permute-done((bf16[128,1024]{1,0:T(8,128)(2,1)S(1)}, bf16[128,1024]{1,0:T(8,128)(2,1)S(1)}, u32[]{:S(2)}, u32[]{:S(2)}) %collective-permute-start.21) | collective-permute-done | bytes 262176 | tf_op jit(solution)/shard_map/ppermute | solution.py:524
  72.1 6.5 %fetch.1 = (bf16[2048,768]{1,0:T(8,128)(2,1)S(1)}, bf16[2048,768]{1,0:T(8,128)(2,1)S(1)}, bf16[768,2048]{1,0:T(8,128)(2,1)S(1)}, bf16[2048,768]{1,0:T(8,128)(2,1...) custom-call(bf16[2048,768]{1,0:T(8,128)(2,1)} %bitcast.30, ...), custom_call_target="tpu_custom_call" | custom-call | tf_op jit(solution)/shard_map/fetch/pallas_call | solution.py:372
  78.6 2.1 %collective-permute-start.29 = (bf16[128,1024]{1,0:T(8,128)(2,1)S(1)}, bf16[128,1024]{1,0:T(8,128)(2,1)S(1)}, u32[]{:S(2)}, u32[]{:S(2)}) collective-permute-start(bf16[128,1024]{1,0:T(8,128)(2,1)S(1)} %collective-permute-done.27.refs_0_), channel_id=1, source_target_pairs={{0,4},{1,5},{2,6},{3,7},{4,8},{5,9},{6,10},{7,11},{8,12},{9,13},{1... | collective-permute-start | bytes 786440 | tf_op jit(solution)/shard_map/ppermute | solution.py:524
  82.9 4.4 %experts.5 = (bf16[128,1024]{1,0:T(8,128)(2,1)S(1)}, bf16[128,1024]{1,0:T(8,128)(2,1)S(1)}, bf16[128,1024]{1,0:T(8,128)(2,1)S(1)}, bf16[128,1024]{1,0:T(8,128)(2,1)S(1)}) custom-call(s32[1]{0:T(128)} %bitcast.side_ref, f32[1,2048]{1,0:T(1,128)S(1)} %bitcast.25, s32[4,2,256]{2,1,0:T(2,128)S(1)} %get-tuple-element.172.slot_rows, ...), custom_call_target="tpu_custom_call" | custom-call | flops 2717908992 | bytes 18874368 | tf_op jit(solution)/shard_map/experts/pallas_call | solution.py:455
  87.3 1.8 %collective-permute-done.29.refs_2_ = bf16[128,1024]{1,0:T(8,128)(2,1)S(1)} collective-permute-done((bf16[128,1024]{1,0:T(8,128)(2,1)S(1)}, bf16[128,1024]{1,0:T(8,128)(2,1)S(1)}, u32[]{:S(2)}, u32[]{:S(2)}) %collective-permute-start.29) | collective-permute-done | bytes 262176 | tf_op jit(solution)/shard_map/ppermute | solution.py:524
  89.7 3.0 %collective-permute-done.32.refs_3_ = bf16[128,1024]{1,0:T(8,128)(2,1)S(1)} collective-permute-done((bf16[128,1024]{1,0:T(8,128)(2,1)S(1)}, bf16[128,1024]{1,0:T(8,128)(2,1)S(1)}, u32[]{:S(2)}, u32[]{:S(2)}) %collective-permute-start.32) | collective-permute-done | bytes 262176 | tf_op jit(solution)/shard_map/ppermute | solution.py:524
  93.9 4.4 %experts.6 = (bf16[128,1024]{1,0:T(8,128)(2,1)S(1)}, bf16[128,1024]{1,0:T(8,128)(2,1)S(1)}, bf16[128,1024]{1,0:T(8,128)(2,1)S(1)}, bf16[128,1024]{1,0:T(8,128)(2,1)S(1)}) custom-call(s32[1]{0:T(128)} %bitcast.side_ref, f32[1,2048]{1,0:T(1,128)S(1)} %bitcast.26, s32[4,2,256]{2,1,0:T(2,128)S(1)} %get-tuple-element.172.slot_rows, ...), custom_call_target="tpu_custom_call" | custom-call | flops 2717908992 | bytes 18874368 | tf_op jit(solution)/shard_map/experts/pallas_call | solution.py:455
  99.0 2.8 %collective-permute-done.34.refs_3_ = bf16[128,1024]{1,0:T(8,128)(2,1)S(1)} collective-permute-done((bf16[128,1024]{1,0:T(8,128)(2,1)S(1)}, bf16[128,1024]{1,0:T(8,128)(2,1)S(1)}, u32[]{:S(2)}, u32[]{:S(2)}) %collective-permute-start.34) | collective-permute-done | bytes 262176 | tf_op jit(solution)/shard_map/ppermute | solution.py:524
  101.9 4.4 %experts.7 = (bf16[128,1024]{1,0:T(8,128)(2,1)S(1)}, bf16[128,1024]{1,0:T(8,128)(2,1)S(1)}, bf16[128,1024]{1,0:T(8,128)(2,1)S(1)}, bf16[128,1024]{1,0:T(8,128)(2,1)S(1)}) custom-call(s32[1]{0:T(128)} %bitcast.side_ref, f32[1,2048]{1,0:T(1,128)S(1)} %bitcast.27, s32[4,2,256]{2,1,0:T(2,128)S(1)} %get-tuple-element.172.slot_rows, ...), custom_call_target="tpu_custom_call" | custom-call | flops 2717908992 | bytes 18874368 | tf_op jit(solution)/shard_map/experts/pallas_call | solution.py:455
  108.3 7.2 %collective-permute-done.35 = bf16[128,1024]{1,0:T(8,128)(2,1)S(1)} collective-permute-done((bf16[128,1024]{1,0:T(8,128)(2,1)S(1)}, bf16[128,1024]{1,0:T(8,128)(2,1)S(1)}, u32[]{:S(2)}, u32[]{:S(2)}) %collective-permute-start.35) | collective-permute-done | bytes 262176 | tf_op jit(solution)/shard_map/ppermute | solution.py:524
  115.8 1.7 %collective-permute-start.44 = (bf16[128,1024]{1,0:T(8,128)(2,1)S(1)}, bf16[128,1024]{1,0:T(8,128)(2,1)S(1)}, u32[]{:S(2)}, u32[]{:S(2)}) collective-permute-start(bf16[128,1024]{1,0:T(8,128)(2,1)S(1)} %add_convert_fusion.2), channel_id=1, source_target_pairs={{0,2},{1,3},{2,0},{3,1},{4,6},{5,7},{6,4},{7,5},{8,10},{9,11},{10,... | collective-permute-start | bytes 786440 | tf_op jit(solution)/shard_map/ppermute | solution.py:524
  117.5 3.6 %collective-permute-done.37 = bf16[128,1024]{1,0:T(8,128)(2,1)S(1)} collective-permute-done((bf16[128,1024]{1,0:T(8,128)(2,1)S(1)}, bf16[128,1024]{1,0:T(8,128)(2,1)S(1)}, u32[]{:S(2)}, u32[]{:S(2)}) %collective-permute-start.37) | collective-permute-done | bytes 262176 | tf_op jit(solution)/shard_map/ppermute | solution.py:524
  121.2 2.9 %collective-permute-done.36 = bf16[128,1024]{1,0:T(8,128)(2,1)S(1)} collective-permute-done((bf16[128,1024]{1,0:T(8,128)(2,1)S(1)}, bf16[128,1024]{1,0:T(8,128)(2,1)S(1)}, u32[]{:S(2)}, u32[]{:S(2)}) %collective-permute-start.36) | collective-permute-done | bytes 262176 | tf_op jit(solution)/shard_map/ppermute | solution.py:524
  125.5 4.2 %collective-permute-done.42 = bf16[128,1024]{1,0:T(8,128)(2,1)S(1)} collective-permute-done((bf16[128,1024]{1,0:T(8,128)(2,1)S(1)}, bf16[128,1024]{1,0:T(8,128)(2,1)S(1)}, u32[]{:S(2)}, u32[]{:S(2)}) %collective-permute-start.42) | collective-permute-done | bytes 262176 | tf_op jit(solution)/shard_map/ppermute | solution.py:524
  131.1 4.4 %experts.4 = (bf16[128,1024]{1,0:T(8,128)(2,1)S(1)}, bf16[128,1024]{1,0:T(8,128)(2,1)S(1)}, bf16[128,1024]{1,0:T(8,128)(2,1)S(1)}, bf16[128,1024]{1,0:T(8,128)(2,1)S(1)}) custom-call(s32[1]{0:T(128)} %bitcast.side_ref, f32[1,2048]{1,0:T(1,128)S(1)} %bitcast.28, s32[4,2,256]{2,1,0:T(2,128)S(1)} %get-tuple-element.172.slot_rows, ...), custom_call_target="tpu_custom_call" | custom-call | flops 2717908992 | bytes 18874368 | tf_op jit(solution)/shard_map/experts/pallas_call | solution.py:455
  138.2 2.8 %collective-permute-done.45 = bf16[128,1024]{1,0:T(8,128)(2,1)S(1)} collective-permute-done((bf16[128,1024]{1,0:T(8,128)(2,1)S(1)}, bf16[128,1024]{1,0:T(8,128)(2,1)S(1)}, u32[]{:S(2)}, u32[]{:S(2)}) %collective-permute-start.45) | collective-permute-done | bytes 262176 | tf_op jit(solution)/shard_map/ppermute | solution.py:524
  144.6 2.9 %collective-permute-done.47.refs_6_ = bf16[128,1024]{1,0:T(8,128)(2,1)S(1)} collective-permute-done((bf16[128,1024]{1,0:T(8,128)(2,1)S(1)}, bf16[128,1024]{1,0:T(8,128)(2,1)S(1)}, u32[]{:S(2)}, u32[]{:S(2)}) %collective-permute-start.47) | collective-permute-done | bytes 262176 | tf_op jit(solution)/shard_map/ppermute | solution.py:524
  148.7 1.5 %finish.1 = bf16[128,2048]{1,0:T(8,128)(2,1)} custom-call(s32[1]{0:T(128)} %bitcast.side_ref, f32[128,1024]{1,0:T(8,128)S(1)} %get-tuple-element.146.refs_0_, bf16[128,1024]{1,0:T(8,128)(2,1)S(1)} %get-tuple-element.192.refs_1_, bf16[128,1024]{1,0:T(8,128)(2,1)S(1)} %collective-permute-done.40.refs_2_, ...), custom_call_target="tpu_custom_call" | custom-call | tf_op jit(solution)/shard_map/finish/pallas_call | solution.py:271
  (127 shorter events, 41.5 us)
Async XLA Ops:
  4.9 12.6 %collective-permute-start.3 = (bf16[2048,768]{1,0:T(8,128)(2,1)}, bf16[2048,768]{1,0:T(8,128)(2,1)}, u32[]{:S(2)}, u32[]{:S(2)}) collective-permute-start(bf16[2048,768]{1,0:T(8,128)(2,1)} %bitcast.29), channel_id=1, source_target_pairs={{0,1},{1,0},{2,3},{3,2},{4,5},{5,4},{6,7},{7,6},{8,9},{9,8},{10,11... | collective-permute-start | bytes 9437192 | tf_op jit(solution)/shard_map/ppermute | solution.py:524
  5.0 23.0 %collective-permute-start.7 = (bf16[2048,768]{1,0:T(8,128)(2,1)}, bf16[2048,768]{1,0:T(8,128)(2,1)}, u32[]{:S(2)}, u32[]{:S(2)}) collective-permute-start(bf16[2048,768]{1,0:T(8,128)(2,1)} %bitcast.31), channel_id=1, source_target_pairs={{0,1},{1,0},{2,3},{3,2},{4,5},{5,4},{6,7},{7,6},{8,9},{9,8},{10,11... | collective-permute-start | bytes 9437192 | tf_op jit(solution)/shard_map/ppermute | solution.py:524
  5.5 25.3 %collective-permute-start.11 = (bf16[768,2048]{1,0:T(8,128)(2,1)}, bf16[768,2048]{1,0:T(8,128)(2,1)}, u32[]{:S(2)}, u32[]{:S(2)}) collective-permute-start(bf16[768,2048]{1,0:T(8,128)(2,1)} %bitcast.33), channel_id=1, source_target_pairs={{0,1},{1,0},{2,3},{3,2},{4,5},{5,4},{6,7},{7,6},{8,9},{9,8},{10,11... | collective-permute-start | bytes 9437192 | tf_op jit(solution)/shard_map/ppermute | solution.py:524
  5.5 11.9 %collective-permute-start.1 = (bf16[272,512]{1,0:T(8,128)(2,1)S(1)}, bf16[272,512]{1,0:T(8,128)(2,1)S(1)}, u32[]{:S(2)}, u32[]{:S(2)}) collective-permute-start(bf16[272,512]{1,0:T(8,128)(2,1)S(1)} %pad_maximum_fusion.refs_8_.refs_0_), channel_id=1, source_target_pairs={{0,4},{1,5},{2,6},{3,7},{4,8},{5,9},{6,10},{7,11},{8,12},{9,13},{1... | collective-permute-start | bytes 835592 | tf_op jit(solution)/shard_map/ppermute | solution.py:524
  8.5 8.9 %collective-permute-start.2 = (bf16[272,512]{1,0:T(8,128)(2,1)S(1)}, bf16[272,512]{1,0:T(8,128)(2,1)S(1)}, u32[]{:S(2)}, u32[]{:S(2)}) collective-permute-start(bf16[272,512]{1,0:T(8,128)(2,1)S(1)} %pad_maximum_fusion.refs_8_.refs_0_), channel_id=1, source_target_pairs={{0,2},{1,3},{2,0},{3,1},{4,6},{5,7},{6,4},{7,5},{8,10},{9,11},{10,... | collective-permute-start | bytes 835592 | tf_op jit(solution)/shard_map/ppermute | solution.py:524
  17.5 10.5 %collective-permute-start.4 = (bf16[272,512]{1,0:T(8,128)(2,1)S(1)}, bf16[272,512]{1,0:T(8,128)(2,1)S(1)}, u32[]{:S(2)}, u32[]{:S(2)}) collective-permute-start(bf16[272,512]{1,0:T(8,128)(2,1)S(1)} %collective-permute-done.1.refs_9_.refs_1_), channel_id=1, source_target_pairs={{0,4},{1,5},{2,6},{3,7},{4,8},{5,9},{6,10},{7,11},{8,12},{9,13},{1... | collective-permute-start | bytes 835592 | tf_op jit(solution)/shard_map/ppermute | solution.py:524
  18.5 9.5 %collective-permute-start.5 = (bf16[272,512]{1,0:T(8,128)(2,1)S(1)}, bf16[272,512]{1,0:T(8,128)(2,1)S(1)}, u32[]{:S(2)}, u32[]{:S(2)}) collective-permute-start(bf16[272,512]{1,0:T(8,128)(2,1)S(1)} %collective-permute-done.1.refs_9_.refs_1_), channel_id=1, source_target_pairs={{0,2},{1,3},{2,0},{3,1},{4,6},{5,7},{6,4},{7,5},{8,10},{9,11},{10,... | collective-permute-start | bytes 835592 | tf_op jit(solution)/shard_map/ppermute | solution.py:524
  28.0 9.0 %collective-permute-start.15 = (bf16[128,1024]{1,0:T(8,128)(2,1)}, bf16[128,1024]{1,0:T(8,128)(2,1)S(1)}, u32[]{:S(2)}, u32[]{:S(2)}) collective-permute-start(bf16[128,1024]{1,0:T(8,128)(2,1)} %attention.3.refs_1_), channel_id=1, source_target_pairs={{0,16},{1,17},{2,18},{3,19},{4,20},{5,21},{6,22},{7,23},{8,24},{9,... | collective-permute-start | bytes 786440 | tf_op jit(solution)/shard_map/ppermute | solution.py:532
  28.8 10.3 %collective-permute-start.8 = (bf16[272,512]{1,0:T(8,128)(2,1)S(1)}, bf16[272,512]{1,0:T(8,128)(2,1)S(1)}, u32[]{:S(2)}, u32[]{:S(2)}) collective-permute-start(bf16[272,512]{1,0:T(8,128)(2,1)S(1)} %collective-permute-done.4.refs_10_.refs_4_), channel_id=1, source_target_pairs={{0,4},{1,5},{2,6},{3,7},{4,8},{5,9},{6,10},{7,11},{8,12},{9,13},{1... | collective-permute-start | bytes 835592 | tf_op jit(solution)/shard_map/ppermute | solution.py:524
  30.2 8.8 %collective-permute-start.9 = (bf16[272,512]{1,0:T(8,128)(2,1)S(1)}, bf16[272,512]{1,0:T(8,128)(2,1)S(1)}, u32[]{:S(2)}, u32[]{:S(2)}) collective-permute-start(bf16[272,512]{1,0:T(8,128)(2,1)S(1)} %collective-permute-done.4.refs_10_.refs_4_), channel_id=1, source_target_pairs={{0,2},{1,3},{2,0},{3,1},{4,6},{5,7},{6,4},{7,5},{8,10},{9,11},{10,... | collective-permute-start | bytes 835592 | tf_op jit(solution)/shard_map/ppermute | solution.py:524
  30.8 10.7 %collective-permute-start.14 = (bf16[128,1024]{1,0:T(8,128)(2,1)}, bf16[128,1024]{1,0:T(8,128)(2,1)S(1)}, u32[]{:S(2)}, u32[]{:S(2)}) collective-permute-start(bf16[128,1024]{1,0:T(8,128)(2,1)} %attention.3.refs_1_), channel_id=1, source_target_pairs={{0,1},{1,0},{2,3},{3,2},{4,5},{5,4},{6,7},{7,6},{8,9},{9,8},{10,11... | collective-permute-start | bytes 786440 | tf_op jit(solution)/shard_map/ppermute | solution.py:524
  30.9 10.6 %collective-permute-start.16 = (bf16[128,1024]{1,0:T(8,128)(2,1)S(1)}, bf16[128,1024]{1,0:T(8,128)(2,1)}, u32[]{:S(2)}, u32[]{:S(2)}) collective-permute-start(bf16[128,1024]{1,0:T(8,128)(2,1)S(1)} %collective-permute-done.6.refs_4_), channel_id=1, source_target_pairs={{0,1},{1,0},{2,3},{3,2},{4,5},{5,4},{6,7},{7,6},{8,9},{9,8},{10,11... | collective-permute-start | bytes 786440 | tf_op jit(solution)/shard_map/ppermute | solution.py:524
  52.5 10.5 %collective-permute-start.23 = (bf16[128,1024]{1,0:T(8,128)(2,1)S(1)}, bf16[128,1024]{1,0:T(8,128)(2,1)S(1)}, u32[]{:S(2)}, u32[]{:S(2)}) collective-permute-start(bf16[128,1024]{1,0:T(8,128)(2,1)S(1)} %get-tuple-element.175.refs_0_), channel_id=1, source_target_pairs={{0,4},{1,5},{2,6},{3,7},{4,8},{5,9},{6,10},{7,11},{8,12},{9,13},{1... | collective-permute-start | bytes 786440 | tf_op jit(solution)/shard_map/ppermute | solution.py:524
  54.3 8.7 %collective-permute-start.24 = (bf16[128,1024]{1,0:T(8,128)(2,1)S(1)}, bf16[128,1024]{1,0:T(8,128)(2,1)S(1)}, u32[]{:S(2)}, u32[]{:S(2)}) collective-permute-start(bf16[128,1024]{1,0:T(8,128)(2,1)S(1)} %get-tuple-element.175.refs_0_), channel_id=1, source_target_pairs={{0,2},{1,3},{2,0},{3,1},{4,6},{5,7},{6,4},{7,5},{8,10},{9,11},{10,... | collective-permute-start | bytes 786440 | tf_op jit(solution)/shard_map/ppermute | solution.py:524
  58.8 11.0 %collective-permute-start.21 = (bf16[128,1024]{1,0:T(8,128)(2,1)S(1)}, bf16[128,1024]{1,0:T(8,128)(2,1)S(1)}, u32[]{:S(2)}, u32[]{:S(2)}) collective-permute-start(bf16[128,1024]{1,0:T(8,128)(2,1)S(1)} %get-tuple-element.170.refs_1_), channel_id=1, source_target_pairs={{0,4},{1,5},{2,6},{3,7},{4,8},{5,9},{6,10},{7,11},{8,12},{9,13},{1... | collective-permute-start | bytes 786440 | tf_op jit(solution)/shard_map/ppermute | solution.py:524
  60.6 9.2 %collective-permute-start.22 = (bf16[128,1024]{1,0:T(8,128)(2,1)S(1)}, bf16[128,1024]{1,0:T(8,128)(2,1)S(1)}, u32[]{:S(2)}, u32[]{:S(2)}) collective-permute-start(bf16[128,1024]{1,0:T(8,128)(2,1)S(1)} %get-tuple-element.170.refs_1_), channel_id=1, source_target_pairs={{0,2},{1,3},{2,0},{3,1},{4,6},{5,7},{6,4},{7,5},{8,10},{9,11},{10,... | collective-permute-start | bytes 786440 | tf_op jit(solution)/shard_map/ppermute | solution.py:524
  63.0 15.6 %collective-permute-start.27 = (bf16[128,1024]{1,0:T(8,128)(2,1)S(1)}, bf16[128,1024]{1,0:T(8,128)(2,1)S(1)}, u32[]{:S(2)}, u32[]{:S(2)}) collective-permute-start(bf16[128,1024]{1,0:T(8,128)(2,1)S(1)} %collective-permute-done.23.refs_2_), channel_id=1, source_target_pairs={{0,4},{1,5},{2,6},{3,7},{4,8},{5,9},{6,10},{7,11},{8,12},{9,13},{1... | collective-permute-start | bytes 786440 | tf_op jit(solution)/shard_map/ppermute | solution.py:524
  63.5 15.1 %collective-permute-start.28 = (bf16[128,1024]{1,0:T(8,128)(2,1)S(1)}, bf16[128,1024]{1,0:T(8,128)(2,1)S(1)}, u32[]{:S(2)}, u32[]{:S(2)}) collective-permute-start(bf16[128,1024]{1,0:T(8,128)(2,1)S(1)} %collective-permute-done.23.refs_2_), channel_id=1, source_target_pairs={{0,2},{1,3},{2,0},{3,1},{4,6},{5,7},{6,4},{7,5},{8,10},{9,11},{10,... | collective-permute-start | bytes 786440 | tf_op jit(solution)/shard_map/ppermute | solution.py:524
  69.8 11.6 %collective-permute-start.25 = (bf16[128,1024]{1,0:T(8,128)(2,1)S(1)}, bf16[128,1024]{1,0:T(8,128)(2,1)S(1)}, u32[]{:S(2)}, u32[]{:S(2)}) collective-permute-start(bf16[128,1024]{1,0:T(8,128)(2,1)S(1)} %collective-permute-done.21.refs_3_), channel_id=1, source_target_pairs={{0,4},{1,5},{2,6},{3,7},{4,8},{5,9},{6,10},{7,11},{8,12},{9,13},{1... | collective-permute-start | bytes 786440 | tf_op jit(solution)/shard_map/ppermute | solution.py:524
  71.1 10.4 %collective-permute-start.26 = (bf16[128,1024]{1,0:T(8,128)(2,1)S(1)}, bf16[128,1024]{1,0:T(8,128)(2,1)S(1)}, u32[]{:S(2)}, u32[]{:S(2)}) collective-permute-start(bf16[128,1024]{1,0:T(8,128)(2,1)S(1)} %collective-permute-done.21.refs_3_), channel_id=1, source_target_pairs={{0,2},{1,3},{2,0},{3,1},{4,6},{5,7},{6,4},{7,5},{8,10},{9,11},{10,... | collective-permute-start | bytes 786440 | tf_op jit(solution)/shard_map/ppermute | solution.py:524
  78.6 10.5 %collective-permute-start.29 = (bf16[128,1024]{1,0:T(8,128)(2,1)S(1)}, bf16[128,1024]{1,0:T(8,128)(2,1)S(1)}, u32[]{:S(2)}, u32[]{:S(2)}) collective-permute-start(bf16[128,1024]{1,0:T(8,128)(2,1)S(1)} %collective-permute-done.27.refs_0_), channel_id=1, source_target_pairs={{0,4},{1,5},{2,6},{3,7},{4,8},{5,9},{6,10},{7,11},{8,12},{9,13},{1... | collective-permute-start | bytes 786440 | tf_op jit(solution)/shard_map/ppermute | solution.py:524
  80.7 8.9 %collective-permute-start.30 = (bf16[128,1024]{1,0:T(8,128)(2,1)S(1)}, bf16[128,1024]{1,0:T(8,128)(2,1)S(1)}, u32[]{:S(2)}, u32[]{:S(2)}) collective-permute-start(bf16[128,1024]{1,0:T(8,128)(2,1)S(1)} %collective-permute-done.27.refs_0_), channel_id=1, source_target_pairs={{0,2},{1,3},{2,0},{3,1},{4,6},{5,7},{6,4},{7,5},{8,10},{9,11},{10,... | collective-permute-start | bytes 786440 | tf_op jit(solution)/shard_map/ppermute | solution.py:524
  81.4 11.2 %collective-permute-start.32 = (bf16[128,1024]{1,0:T(8,128)(2,1)S(1)}, bf16[128,1024]{1,0:T(8,128)(2,1)S(1)}, u32[]{:S(2)}, u32[]{:S(2)}) collective-permute-start(bf16[128,1024]{1,0:T(8,128)(2,1)S(1)} %collective-permute-done.25.refs_1_), channel_id=1, source_target_pairs={{0,4},{1,5},{2,6},{3,7},{4,8},{5,9},{6,10},{7,11},{8,12},{9,13},{1... | collective-permute-start | bytes 786440 | tf_op jit(solution)/shard_map/ppermute | solution.py:524
  81.5 11.2 %collective-permute-start.33 = (bf16[128,1024]{1,0:T(8,128)(2,1)S(1)}, bf16[128,1024]{1,0:T(8,128)(2,1)S(1)}, u32[]{:S(2)}, u32[]{:S(2)}) collective-permute-start(bf16[128,1024]{1,0:T(8,128)(2,1)S(1)} %collective-permute-done.25.refs_1_), channel_id=1, source_target_pairs={{0,2},{1,3},{2,0},{3,1},{4,6},{5,7},{6,4},{7,5},{8,10},{9,11},{10,... | collective-permute-start | bytes 786440 | tf_op jit(solution)/shard_map/ppermute | solution.py:524
  106.2 9.3 %collective-permute-start.35 = (bf16[128,1024]{1,0:T(8,128)(2,1)S(1)}, bf16[128,1024]{1,0:T(8,128)(2,1)S(1)}, u32[]{:S(2)}, u32[]{:S(2)}) collective-permute-start(bf16[128,1024]{1,0:T(8,128)(2,1)S(1)} %get-tuple-element.216), channel_id=1, source_target_pairs={{0,2},{1,3},{2,0},{3,1},{4,6},{5,7},{6,4},{7,5},{8,10},{9,11},{10,... | collective-permute-start | bytes 786440 | tf_op jit(solution)/shard_map/ppermute | solution.py:524
  107.4 13.8 %collective-permute-start.37 = (bf16[128,1024]{1,0:T(8,128)(2,1)S(1)}, bf16[128,1024]{1,0:T(8,128)(2,1)S(1)}, u32[]{:S(2)}, u32[]{:S(2)}) collective-permute-start(bf16[128,1024]{1,0:T(8,128)(2,1)S(1)} %get-tuple-element.217), channel_id=1, source_target_pairs={{0,2},{1,3},{2,0},{3,1},{4,6},{5,7},{6,4},{7,5},{8,10},{9,11},{10,... | collective-permute-start | bytes 786440 | tf_op jit(solution)/shard_map/ppermute | solution.py:524
  115.7 14.0 %collective-permute-start.42 = (bf16[128,1024]{1,0:T(8,128)(2,1)S(1)}, bf16[128,1024]{1,0:T(8,128)(2,1)S(1)}, u32[]{:S(2)}, u32[]{:S(2)}) collective-permute-start(bf16[128,1024]{1,0:T(8,128)(2,1)S(1)} %get-tuple-element.228), channel_id=1, source_target_pairs={{0,12},{1,13},{2,14},{3,15},{4,0},{5,1},{6,2},{7,3},{8,4},{9,5},{1... | collective-permute-start | bytes 786440 | tf_op jit(solution)/shard_map/ppermute | solution.py:524
  115.8 13.9 %collective-permute-start.44 = (bf16[128,1024]{1,0:T(8,128)(2,1)S(1)}, bf16[128,1024]{1,0:T(8,128)(2,1)S(1)}, u32[]{:S(2)}, u32[]{:S(2)}) collective-permute-start(bf16[128,1024]{1,0:T(8,128)(2,1)S(1)} %add_convert_fusion.2), channel_id=1, source_target_pairs={{0,2},{1,3},{2,0},{3,1},{4,6},{5,7},{6,4},{7,5},{8,10},{9,11},{10,... | collective-permute-start | bytes 786440 | tf_op jit(solution)/shard_map/ppermute | solution.py:524
  124.2 11.3 %collective-permute-start.39 = (bf16[128,1024]{1,0:T(8,128)(2,1)S(1)}, bf16[128,1024]{1,0:T(8,128)(2,1)S(1)}, u32[]{:S(2)}, u32[]{:S(2)}) collective-permute-start(bf16[128,1024]{1,0:T(8,128)(2,1)S(1)} %get-tuple-element.220), channel_id=1, source_target_pairs={{0,2},{1,3},{2,0},{3,1},{4,6},{5,7},{6,4},{7,5},{8,10},{9,11},{10,... | collective-permute-start | bytes 786440 | tf_op jit(solution)/shard_map/ppermute | solution.py:524
  125.3 10.2 %collective-permute-start.38 = (bf16[128,1024]{1,0:T(8,128)(2,1)S(1)}, bf16[128,1024]{1,0:T(8,128)(2,1)S(1)}, u32[]{:S(2)}, u32[]{:S(2)}) collective-permute-start(bf16[128,1024]{1,0:T(8,128)(2,1)S(1)} %add_convert_fusion.4), channel_id=1, source_target_pairs={{0,12},{1,13},{2,14},{3,15},{4,0},{5,1},{6,2},{7,3},{8,4},{9,5},{1... | collective-permute-start | bytes 786440 | tf_op jit(solution)/shard_map/ppermute | solution.py:524
  131.0 10.0 %collective-permute-start.45 = (bf16[128,1024]{1,0:T(8,128)(2,1)S(1)}, bf16[128,1024]{1,0:T(8,128)(2,1)S(1)}, u32[]{:S(2)}, u32[]{:S(2)}) collective-permute-start(bf16[128,1024]{1,0:T(8,128)(2,1)S(1)} %add_convert_fusion.1), channel_id=1, source_target_pairs={{0,12},{1,13},{2,14},{3,15},{4,0},{5,1},{6,2},{7,3},{8,4},{9,5},{1... | collective-permute-start | bytes 786440 | tf_op jit(solution)/shard_map/ppermute | solution.py:524
  135.7 8.9 %collective-permute-start.40 = (bf16[128,1024]{1,0:T(8,128)(2,1)S(1)}, bf16[128,1024]{1,0:T(8,128)(2,1)S(1)}, u32[]{:S(2)}, u32[]{:S(2)}) collective-permute-start(bf16[128,1024]{1,0:T(8,128)(2,1)S(1)} %add_convert_fusion.3), channel_id=1, source_target_pairs={{0,12},{1,13},{2,14},{3,15},{4,0},{5,1},{6,2},{7,3},{8,4},{9,5},{1... | collective-permute-start | bytes 786440 | tf_op jit(solution)/shard_map/ppermute | solution.py:524
  (29 other events, 294.3 us)

commit v4 on v3

--- a/solution.py
+++ b/solution.py
@@ -18,18 +18,31 @@
 ANY = pl.BlockSpec(memory_space=pl.ANY)
 
 
+def place_of(ring):
+    me = lax.axis_index("wide")
+    return me // 4 % ring, me // 2 % 2, me % 2
+
+
 def dot(a, b):
     return jnp.dot(a, b, preferred_element_type=jnp.float32)
 
 
-def attention_kernel(len_ref, q_ref, nk_ref, nv_ref, k_ref, v_ref, o_ref, q_all, scores, top, acc, total):
+def attention_kernel(
+    part, len_ref, q_ref, nk_ref, nv_ref, k_any, v_any, o_ref, q_all, scores, top, acc, total, k_ref, v_ref, sems
+):
     tokens = q_ref.shape[0]
     heads = q_ref.shape[1] // HEAD
-    cache = k_ref.shape[0]
-    length = len_ref[0]
+    cache = k_any.shape[0]
+    length = len_ref[lax.axis_index("wide")]
     blocks = (length + KEY_BLOCK - 1) // KEY_BLOCK
     scale = jnp.float32(HEAD**-0.5 * LOG2E)
-    rows = heads * tokens
+    at = pl.ds(part * HEAD, HEAD)
+    copies = [
+        pltpu.make_async_copy(any_ref.at[:, at], ref, sems.at[i])
+        for i, (any_ref, ref) in enumerate(((k_any, k_ref), (v_any, v_ref)))
+    ]
+    for copy in copies:
+        copy.start()
 
     for h in range(heads):
         q_all[h * tokens : (h + 1) * tokens, :] = q_ref[:, h * HEAD : (h + 1) * HEAD]
@@ -61,6 +74,7 @@
         top[...] = jnp.maximum(top[...], fold(s, jnp.maximum))
         return carry
 
+    copies[0].wait()
     lax.fori_loop(0, blocks, score, 0)
     best = jnp.max(top[...], axis=1, keepdims=True) * scale
     top[...] = jnp.broadcast_to(best, top.shape)
@@ -80,6 +94,7 @@
         acc[...] += dot(w.astype(jnp.bfloat16), v_ref[at, :])
         return carry
 
+    copies[1].wait()
     lax.fori_loop(0, blocks, add_block, 0)
     out = (acc[...] / jnp.sum(total[...], axis=1, keepdims=True)).astype(jnp.bfloat16)
     for h in range(heads):
@@ -93,16 +108,17 @@
     group = width // parts
     cache = keys.shape[0]
     rows = group // HEAD * tokens
+    keys, values = [pltpu.with_memory_space_constraint(a, pltpu.HBM) for a in (keys, values)]
     return pl.pallas_call(
-        attention_kernel,
+        functools.partial(attention_kernel, g),
         grid=(1,),
         in_specs=[
             SMEM,
             pl.BlockSpec((tokens, group), lambda i: (0, part)),
             pl.BlockSpec((tokens, HEAD), lambda i: (0, g)),
             pl.BlockSpec((tokens, HEAD), lambda i: (0, g)),
-            pl.BlockSpec((cache, HEAD), lambda i: (0, g)),
-            pl.BlockSpec((cache, HEAD), lambda i: (0, g)),
+            ANY,
+            ANY,
         ],
         out_specs=pl.BlockSpec((tokens, group), lambda i: (0, 0)),
         out_shape=jax.ShapeDtypeStruct((tokens, group), jnp.bfloat16),
@@ -112,6 +128,9 @@
             pltpu.VMEM((rows, HEAD), jnp.float32),
             pltpu.VMEM((rows, HEAD), jnp.float32),
             pltpu.VMEM((rows, HEAD), jnp.float32),
+            pltpu.VMEM((cache, HEAD), jnp.bfloat16),
+            pltpu.VMEM((cache, HEAD), jnp.bfloat16),
+            pltpu.SemaphoreType.DMA((2,)),
         ],
         compiler_params=pltpu.CompilerParams(vmem_limit_bytes=58 * MIB),
         cost_estimate=pl.CostEstimate(
@@ -123,13 +142,21 @@
     )(length, queries, new_keys, new_values, keys, values)
 
 
-def projection_kernel(n_pieces, n_blocks, base_ref, *refs):
+def projection_kernel(n_pieces, n_blocks, *refs):
     pieces, w_refs = refs[:n_pieces], refs[n_pieces : n_pieces + n_blocks - 1]
-    left_out, sum_out, weight, sems = refs[n_pieces + n_blocks - 1 :]
+    sum_out, left_out, left, weight, sems = refs[n_pieces + n_blocks - 1 :]
     tokens, group = pieces[0].shape
     rows = weight.shape[0] // n_blocks // 2
-    each = left_out.shape[1] // group
+    each = left.shape[1] // group
+    ring = n_blocks // 2
+    place, row, core = place_of(ring)
     copies = []
+
+    def first_row(b, part):
+        z = lax.rem(place + ring - b % ring, ring)
+        y = row if b < ring else 1 - row
+        c = core if part == 0 else 1 - core
+        return pl.multiple_of(((z * 2 + y) * 2 + c) * rows, rows)
 
     def begin(src, dst):
         copies.append(pltpu.make_async_copy(src, dst, sems.at[len(copies)]))
@@ -137,110 +164,109 @@
 
     for b in range(n_blocks - 1):
         for part in range(2):
-            at = pl.multiple_of(base_ref[2 * b + part], rows)
+            at = first_row(b, part)
             begin(w_refs[b].at[pl.ds(part * rows, rows)], weight.at[pl.ds(at, rows)])
     for i, piece in enumerate(pieces):
-        dst = left_out.at[pl.ds(i // each * tokens, tokens), pl.ds(i % each * group, group)]
+        dst = left.at[pl.ds(i // each * tokens, tokens), pl.ds(i % each * group, group)]
         begin(piece, dst)
     for part in range(2):
-        at = pl.multiple_of(base_ref[2 * n_blocks - 2 + part], rows)
+        at = first_row(n_blocks - 1, part)
         weight[pl.ds(at, rows), :] = jnp.zeros((rows, weight.shape[1]), weight.dtype)
     for copy in copies:
         copy.wait()
-    sum_out[...] = dot(left_out[...], weight[...])
-
-
-def projection(bases, pieces, count, blocks):
+    sum_out[...] = dot(left[...], weight[...])
+    if left_out.shape == left.shape:
+        left_out[...] = left[...]
+    else:
+        for part in range(2):
+            at = first_row(n_blocks - 1, part)
+            left_out[:, part * rows : (part + 1) * rows] = left[:, pl.ds(at, rows)]
+
+
+def projection(rows, pieces, count, blocks):
     tokens, group = pieces[0].shape
     width = len(pieces) // count * group
     n_blocks = len(blocks) + 1
     cols = blocks[0].shape[1]
-    return pl.pallas_call(
+    whole_tiles = rows % HEAD == 0
+    pieces, blocks = [
+        [pltpu.with_memory_space_constraint(a, pltpu.HBM) for a in arrays] for arrays in (pieces, blocks)
+    ]
+    total, left = pl.pallas_call(
         functools.partial(projection_kernel, len(pieces), n_blocks),
-        in_specs=[SMEM] + [ANY] * (len(pieces) + len(blocks)),
+        in_specs=[ANY] * (len(pieces) + len(blocks)),
         out_specs=[VMEM] * 2,
         out_shape=[
-            jax.ShapeDtypeStruct((count * tokens, width), jnp.bfloat16),
             jax.ShapeDtypeStruct((count * tokens, cols), jnp.float32),
+            jax.ShapeDtypeStruct((count * tokens, 2 * rows), jnp.bfloat16)
+            if whole_tiles
+            else jax.ShapeDtypeStruct((count * tokens, width), jnp.bfloat16),
         ],
         scratch_shapes=[
+            pltpu.VMEM((count * tokens, width), jnp.bfloat16),
             pltpu.VMEM((width, cols), jnp.bfloat16),
             pltpu.SemaphoreType.DMA((2 * n_blocks - 2 + len(pieces),)),
         ],
-        compiler_params=pltpu.CompilerParams(vmem_limit_bytes=24 * MIB),
+        compiler_params=pltpu.CompilerParams(vmem_limit_bytes=20 * MIB),
         cost_estimate=pl.CostEstimate(
             flops=8 * tokens * width * cols, bytes_accessed=2 * width * cols, transcendentals=0
         ),
         name="projection",
-    )(bases, *pieces, *blocks)
-
-
-def complete_kernel(whole_tiles, base_ref, left_ref, sum_ref, first_ref, second_ref, *refs):
-    outs, (piece, sems) = refs[:-2], refs[-2:]
+    )(*pieces, *blocks)
+    if not whole_tiles:
+        ring = n_blocks // 2
+        place, row, core = place_of(ring)
+        source = ((place + 1) % ring * 2 + 1 - row) * 2
+        parts = [
+            lax.dynamic_slice_in_dim(left, (source + c) * rows, rows, 1) for c in (core, 1 - core)
+        ]
+        left = jnp.concatenate(parts, axis=1)
+    return total, left
+
+
+def complete_kernel(sum_ref, left_ref, first_ref, second_ref, *outs):
     tokens = outs[0].shape[0]
-    half = first_ref.shape[1]
-    copies = []
-    if whole_tiles:
-        rows = piece.shape[1] // 2
-        for part in range(2):
-            at = pl.multiple_of(base_ref[part], rows)
-            src = left_ref.at[:, pl.ds(at, rows)]
-            dst = piece.at[:, pl.ds(part * rows, rows)]
-            copies.append(pltpu.make_async_copy(src, dst, sems.at[part]))
-    else:
-        copies.append(pltpu.make_async_copy(left_ref, piece, sems.at[0]))
-    for copy in copies:
-        copy.start()
-    for copy in copies:
-        copy.wait()
+    half, rows = first_ref.shape[1], left_ref.shape[1]
     for h, w_ref in enumerate((first_ref, second_ref)):
         cols = slice(h * half, (h + 1) * half)
-        whole = sum_ref[:, cols] + dot(piece[...], w_ref[...])
+        whole = sum_ref[:, cols] + dot(left_ref[...], w_ref[:rows, :])
         for i, out in enumerate(outs):
             out[:, cols] = whole[i * tokens : (i + 1) * tokens].astype(out.dtype)
 
 
-def complete(bases, rows, left, total, last, types):
+def complete(total, left, last, types):
     tokens = left.shape[0] // len(types)
-    whole_tiles = rows % HEAD == 0
-    if not whole_tiles:
-        parts = [lax.dynamic_slice_in_dim(left, bases[i], rows, 1) for i in range(2)]
-        left = jnp.concatenate(parts, axis=1)
-    w_spec = pl.BlockSpec((2 * rows, last[0].shape[1]), lambda i: (0, 0))
-    full = pl.BlockSpec(total.shape, lambda i: (0, 0))
-    out = pl.BlockSpec((tokens, total.shape[1]), lambda i: (0, 0))
     return pl.pallas_call(
-        functools.partial(complete_kernel, whole_tiles),
-        grid=(1,),
-        in_specs=[SMEM, ANY, full, w_spec, w_spec],
-        out_specs=[out] * len(types),
+        complete_kernel,
+        in_specs=[VMEM] * 4,
+        out_specs=[VMEM] * len(types),
         out_shape=[jax.ShapeDtypeStruct((tokens, total.shape[1]), t) for t in types],
-        scratch_shapes=[
-            pltpu.VMEM((left.shape[0], 2 * rows), jnp.bfloat16),
-            pltpu.SemaphoreType.DMA((2,)),
-        ],
-        compiler_params=pltpu.CompilerParams(vmem_limit_bytes=24 * MIB),
+        compiler_params=pltpu.CompilerParams(vmem_limit_bytes=16 * MIB),
         name="complete",
-    )(bases, left, total, *last)
-
-
-def mix_kernel(place_ref, residual_ref, gain_ref, *refs):
+    )(total, left, *last)
+
+
+def mix_kernel(far, residual_ref, gain_ref, *refs):
     parts, (mixed_ref, sent_ref) = refs[:-2], refs[-2:]
     cols = parts[0].shape[1]
     for i, part in enumerate(parts):
-        here = pl.ds(pl.multiple_of(place_ref[i], cols), cols)
-        there = pl.ds(pl.multiple_of(place_ref[len(parts)] + place_ref[i], cols), cols)
+        core = lax.axis_index("wide") % 2
+        side = lax.axis_index("groups") % 2
+        at = (1 - core if i else core) * cols
+        base = (1 - side if far else side) * 2 * cols
+        here = pl.ds(pl.multiple_of(at, cols), cols)
+        there = pl.ds(pl.multiple_of(base + at, cols), cols)
         mixed = residual_ref[:, there].astype(jnp.float32) + part[...].astype(jnp.float32)
         mixed_ref[:, here] = mixed
         sent_ref[:, here] = (mixed * gain_ref[:, there]).astype(jnp.bfloat16)
 
 
-def mix(places, residual, gain, parts):
+def mix(far, residual, gain, parts):
     shape = (residual.shape[0], residual.shape[1] // 2)
     residual = pltpu.with_memory_space_constraint(residual, pltpu.HBM)
     return pl.pallas_call(
-        mix_kernel,
-        in_specs=[SMEM] + [VMEM] * (2 + len(parts)),
+        functools.partial(mix_kernel, far),
+        in_specs=[VMEM] * (2 + len(parts)),
         out_specs=[VMEM] * 2,
         out_shape=[
             jax.ShapeDtypeStruct(shape, jnp.float32),
@@ -249,37 +275,38 @@
         compiler_params=pltpu.CompilerParams(vmem_limit_bytes=24 * MIB),
         cost_estimate=pl.CostEstimate(flops=0, bytes_accessed=0, transcendentals=0),
         name="mix",
-    )(places, residual, gain, *parts)
-
-
-def finish_kernel(side_ref, *refs):
+    )(residual, gain, *parts)
+
+
+def finish_kernel(*refs):
     out_ref = refs[-1]
     terms = (len(refs) - 1) // 2
     half = refs[0].shape[1]
+    side = lax.axis_index("groups") % 2
     for h in range(2):
         total = refs[h * terms][...]
         for ref in refs[h * terms + 1 : (h + 1) * terms]:
             total = total + ref[...].astype(jnp.float32)
-        at = side_ref[0] if h == 0 else 1 - side_ref[0]
+        at = side if h == 0 else 1 - side
         out_ref[:, pl.ds(pl.multiple_of(at * half, half), half)] = total.astype(out_ref.dtype)
 
 
-def finish(side, first, second):
+def finish(first, second):
     tokens, half = first[0].shape
     rows = max(16, tokens // 4)
     part = pl.BlockSpec((rows, half), lambda i: (i, 0))
     return pl.pallas_call(
         finish_kernel,
         grid=(tokens // rows,),
-        in_specs=[SMEM] + [part] * (len(first) + len(second)),
+        in_specs=[part] * (len(first) + len(second)),
         out_specs=pl.BlockSpec((rows, 2 * half), lambda i: (i, 0)),
         out_shape=jax.ShapeDtypeStruct((tokens, 2 * half), jnp.bfloat16),
         compiler_params=pltpu.CompilerParams(vmem_limit_bytes=24 * MIB),
         name="finish",
-    )(side, *first, *second)
-
-
-def routing_kernel(cap, n_blocks, served_ref, *refs):
+    )(*first, *second)
+
+
+def routing_kernel(cap, n_blocks, *refs):
     sources, refs = refs[: n_blocks + 1], refs[n_blocks + 1 :]
     rows_ref, cols_ref, shares_ref, table_ref, mask, sems = refs
     tokens = mask.shape[1]
@@ -296,15 +323,18 @@
         copies[-1].start()
     for copy in copies:
         copy.wait()
+    me = lax.axis_index("wide")
+    served = [me.astype(jnp.float32), (me + 1 - 2 * (me % 2)).astype(jnp.float32)]
     for b in range(n_blocks):
         parts = [
             table_ref[b, :, i * tokens : (i + 1) * tokens].astype(jnp.float32)[:top]
             for i in range(3)
         ]
-        ids, share = parts[0], parts[1] + parts[2]
+        ids, score = parts[0], parts[1] + parts[2]
+        share = score / jnp.sum(score, axis=0, keepdims=True)
         at = slice(b % 2 * tokens, (b % 2 + 1) * tokens)
         for e in range(2):
-            hit = ids == served_ref[e].astype(jnp.float32)
+            hit = ids == served[e]
             mask[2 * b + e : 2 * b + e + 1, :] = jnp.max(
                 jnp.where(hit, 1.0, 0.0), axis=0, keepdims=True
             )
@@ -329,14 +359,14 @@
         cols_ref[b // 2, at, :] = columns[:, pair].astype(jnp.int32)
 
 
-def routing(cap, tokens, lines, served, blocks):
+def routing(cap, tokens, lines, blocks):
     blocks = [pltpu.with_memory_space_constraint(b, pltpu.HBM) for b in blocks]
     n_blocks = len(blocks) - 1
     pairs = n_blocks // 2
     rows = jax.ShapeDtypeStruct((pairs, 2, 2 * tokens), jnp.int32)
     return pl.pallas_call(
         functools.partial(routing_kernel, cap, n_blocks),
-        in_specs=[SMEM] + [ANY] * len(blocks),
+        in_specs=[ANY] * len(blocks),
         out_specs=[VMEM] * 3,
         out_shape=[
             rows,
@@ -351,7 +381,7 @@
         compiler_params=pltpu.CompilerParams(vmem_limit_bytes=16 * MIB),
         cost_estimate=pl.CostEstimate(flops=0, bytes_accessed=0, transcendentals=0),
         name="routing",
-    )(served, *blocks)
+    )(*blocks)
 
 
 def fetch_kernel(*refs):
@@ -383,18 +413,19 @@
     return there, token
 
 
-def experts_kernel(first_pair, pairs, n_in, n_out, slots, side_ref, gain_ref, slot_rows, slot_cols, share_rows, *refs):
+def experts_kernel(first_pair, pairs, n_in, n_out, slots, gain_ref, slot_rows, slot_cols, share_rows, *refs):
     x_refs = refs[:n_in]
     w_refs = refs[n_in : n_in + 6]
-    out_refs = refs[n_in + 7 : n_in + 7 + n_out]
-    xs, rows_in, act, scaled, x_sem = refs[n_in + 7 + n_out :]
+    out_refs = refs[n_in + 8 : n_in + 8 + n_out]
+    xs, rows_in, act, scaled, x_sem = refs[n_in + 8 + n_out :]
     depth = xs.shape[1]
     pair_tokens = xs.shape[0] // pairs
     block = pair_tokens // 2
     hidden = act.shape[1]
 
     half = depth // 2
-    starts = [pl.multiple_of(side_ref[0] * half, half), pl.multiple_of((1 - side_ref[0]) * half, half)]
+    side = lax.axis_index("groups") % 2
+    starts = [pl.multiple_of(side * half, half), pl.multiple_of((1 - side) * half, half)]
     x_copies = []
     for i in range(n_in):
         dst = xs.at[pl.ds(i // 2 * block, block), pl.ds(starts[i % 2], half)]
@@ -447,14 +478,14 @@
                 out_refs[4 * p + 2 * b + h][...] = got[b * block : (b + 1) * block]
 
 
-def experts(slots, first_pair, pairs, side, gain, slot_rows, slot_cols, share_rows, x_parts, weights):
+def experts(slots, first_pair, pairs, gain, slot_rows, slot_cols, share_rows, x_parts, weights):
     pair_tokens = slot_rows.shape[2]
     block = pair_tokens // 2
     depth, hidden = weights[0].shape
     n_in = n_out = len(x_parts)
     return pl.pallas_call(
         functools.partial(experts_kernel, first_pair, pairs, n_in, n_out, slots),
-        in_specs=[SMEM] + [VMEM] * 4 + [ANY] * n_in + [VMEM] * 6 + [ANY],
+        in_specs=[VMEM] * 4 + [ANY] * n_in + [VMEM] * 6 + [ANY] * 2,
         out_specs=[VMEM] * n_out,
         out_shape=[jax.ShapeDtypeStruct((block, depth // 2), jnp.bfloat16)] * n_out,
         scratch_shapes=[
@@ -471,7 +502,7 @@
             transcendentals=0,
         ),
         name="experts",
-    )(side, gain, slot_rows, slot_cols, share_rows, *x_parts, *weights)
+    )(gain, slot_rows, slot_cols, share_rows, *x_parts, *weights)
 
 
 def permutations(devices):
@@ -516,8 +547,6 @@
     half = depth // 2
     ring, shift = permutations(devices)
     core = me % 2
-    row = me // 2 % 2
-    place = me // 4
     side = lax.axis_index("groups") % 2
 
     def sender(*by):
@@ -565,7 +594,7 @@
             kept.update(new)
             same.append(moved)
             other.append(crossed)
-        last = [send_across(same[-1][0]), send_forward(other[-1][1])]
+        last = [send_forward(other[-1][0]), send_across(same[-1][1])]
         for step in beside[ring - 1 :]:
             last, new = barrier((last, step(same, other)))
             kept.update(new)
@@ -581,19 +610,19 @@
     quarter = 2 * side + core
     keep = lax.dynamic_slice_in_dim(o_weight, quarter * cols, cols, 1)
     give = lax.dynamic_slice_in_dim(o_weight, (quarter ^ 1) * cols, cols, 1)
-    shares = gate_raw / jnp.sum(gate_raw, axis=-1, keepdims=True)
-    high = shares.astype(jnp.bfloat16)
-    low = (shares - high.astype(jnp.float32)).astype(jnp.bfloat16)
+    high = gate_raw.astype(jnp.bfloat16)
+    low = (gate_raw - high.astype(jnp.float32)).astype(jnp.bfloat16)
     table = jnp.concatenate([expert_ids.astype(jnp.bfloat16).T, high.T, low.T], axis=1)
     lines = 16
     table = jnp.pad(table, ((0, lines - top), (0, cols - 3 * tokens)))
     own_block = jnp.concatenate([keep, send_core(give), table], axis=0)
-    length = lax.dynamic_slice_in_dim(cache_len, me, 1, 0)
+    length = cache_len
     mine = [w_gate[0], w_up[0], w_down[0]]
     length, own_block, mine = barrier((length, own_block, mine))
     operands = (queries, new_keys, new_values, cache_keys[0], cache_values[0])
 
     late = {}
+    beside_weights = []
 
     def attend_first(same, other):
         return {"a0": attention(0, 2, length, *operands), "w0": send_core(mine[0])}
@@ -610,61 +639,56 @@
         late["side1"] = send_side(kept["a1"])
         return {"core0": send_core(kept["a0"]), "w2": send_core(mine[2])}
 
-    offsets = jnp.arange(ring, dtype=jnp.int32)
-    rings = (place - offsets) % ring
-    first_of = jnp.concatenate([rings * 2 + row, rings * 2 + 1 - row]) * 2
-    bases = jnp.stack([first_of + core, first_of + 1 - core], axis=1).reshape(-1)
-    bases = bases * o_weight.shape[0]
-
     def project(same, other):
         kept["core1"] = send_core(kept["a1"])
         kept["corner0"] = send_core(kept["side0"])
         kept["corner1"] = send_core(late["side1"])
         kept.update(late)
         pieces = [kept[name + str(g)] for name in ("a", "core", "side", "corner") for g in range(2)]
-        left, total = projection(bases, pieces, 4, same + other)
-        return {"left": left, "sum": total}
+        return {"sum": projection(o_weight.shape[0], pieces, 4, same + other)}
 
     w_same, w_other, w_last = gather_whole(
         own_block, [attend_first, attend_second, swap_first] + [nothing] * (ring - 4) + [project]
     )
     types = [jnp.float32, jnp.float32, jnp.bfloat16, jnp.bfloat16]
     own_part, core_part, side_part, corner_part = complete(
-        bases[-2:], o_weight.shape[0], kept["left"], kept["sum"], w_last, types
+        *kept["sum"], w_last, types
     )
 
     gain = norm_gain.reshape(1, -1)
     near = [own_part, send_core(core_part)]
     far = [send_side(side_part), send_corner(corner_part)]
-    here = [core * cols, (1 - core) * cols]
-    mixed_near, x_near = mix(jnp.stack(here + [side * half]).astype(jnp.int32), residual, gain, near)
-    far_places = jnp.stack(here + [(1 - side) * half]).astype(jnp.int32)
+    mixed_near, x_near = mix(False, residual, gain, near)
     cap = tokens * top // devices + max(2, tokens * top // (8 * devices))
     slots = -(-2 * cap // 16) * 16
-    served = jnp.stack([me, me ^ 1])
     w_blocks, x_near_later = barrier((w_same + w_other + w_last, x_near))
     order = []
-    for r in range(0, ring, 2):
+    for r in range(0, ring - 2, 2):
         order += w_blocks[r : r + 2] + w_blocks[ring + r : ring + r + 2]
-    order.append(w_blocks[-1])
-    tables = routing(cap, tokens, lines, served, order)
+    order += [w_blocks[ring - 2], w_blocks[-3], w_blocks[ring - 1]] + w_blocks[-2:]
+    tables = routing(cap, tokens, lines, order)
     far, tables = barrier((far, tables))
-    mixed_far, x_far = mix(far_places, residual, gain, far)
-    side_word = side.astype(jnp.int32).reshape(1)
-
-    def load_weights(same, other):
-        arrays = mine + [kept["w0"], kept["w1"], kept["w2"]]
-        arrays, kept["tables"], same[1][1] = barrier((arrays, tables, same[1][1]))
+    mixed_far, x_far = mix(True, residual, gain, far)
+
+    def load_mine(same, other):
+        arrays, kept["tables"], same[0][1] = barrier((mine, tables, same[0][1]))
         weights, token = fetch(arrays)
         beside_weights.extend(weights)
         return {"token": token}
 
-    beside_weights = []
+    def load_other(same, other):
+        arrays = [kept["w0"], kept["w1"], kept["w2"]]
+        arrays, same[1][1] = barrier((arrays, same[1][1]))
+        weights, token = fetch(arrays)
+        beside_weights.extend(weights)
+        kept["token2"] = token
+        p0, p1 = serve(0, 1, same[:2])
+        return {("p", 0): p0, ("p", 1): p1}
 
     def serve(first, count, blocks):
         halves = [h for block in blocks for h in block]
-        weights = beside_weights + [kept["token"]]
-        outs = experts(slots, first, count, side_word, gain, *kept["tables"], halves, weights)
+        weights = beside_weights + [kept["token"], kept["token2"]]
+        outs = experts(slots, first, count, gain, *kept["tables"], halves, weights)
         return [outs[i : i + 2] for i in range(0, len(outs), 2)]
 
     def serve_same(r):
@@ -682,38 +706,44 @@
         return step
 
     def serve_two(same, other):
-        p0, p1 = serve(ring - 2, 1, same[-2:])
-        return {("p", ring - 2): p0, ("p", ring - 1): p1}
-
-    beside = [nothing, load_weights, serve_other(0)]
+        p, q = serve(ring - 2, 1, [same[ring - 2], other[ring - 2]])
+        return {("p", ring - 2): p, ("q", ring - 2): q}
+
+    beside = [load_mine, load_other, serve_other(0)]
     for r in range(2, ring - 2, 2):
         beside += [serve_same(r), serve_other(r)]
     beside.append(serve_two)
     x_same, x_other = gather_halves([x_near, x_far], beside, [x_near_later, x_far])
-    p = [None, None] + [kept["p", r] for r in range(2, ring)]
-    q = [kept["q", r] for r in range(ring - 2)]
-    q += serve(ring - 1, 1, x_other[-2:])
+    p = [kept["p", r] for r in range(ring - 1)]
+    q = [kept["q", r] for r in range(ring - 1)]
+    for parts, part in zip((p, q), serve(ring - 1, 1, [x_same[-1], x_other[-1]])):
+        parts.append(part)
 
     def add(*terms):
         return sum(t.astype(jnp.float32) for t in terms).astype(jnp.bfloat16)
 
-    r = ring - 1
-    came = [None, send_backward(p[r][1])]
-    extra = send_backward(q[r][1])
-    crossed = [send_across(q[r][0]), None]
-    later = [send_across(q[r - 1][0]), None]
-    p[0], p[1] = serve(0, 1, x_same[:2])
-    crossed[1] = send_across(add(q[r - 1][1], extra))
-    came[0] = send_backward(add(p[r][0], crossed[0]))
-    crossed[0] = later[0]
-    for r in range(ring - 2, 0, -1):
-        moving = [None, None]
-        for h in (1, 0):
-            total = add(p[r][h], came[h], crossed[h])
-            total, behind = barrier((total, q[r - 1][h]))
-            came[h], crossed[h] = send_backward(total), send_across(behind)
+    extra = send_forward(q[1][1])
+    came = [None, None]
+    own_q = list(q[0])
+    for r in range(1, ring):
+        crossed = [send_across(q[r][0]), None]
+        if r == 2:
+            crossed[1] = send_across(add(q[r][1], extra))
+        elif r > 2:
+            crossed[1] = send_across(q[r][1])
+        second = p[r][1]
+        for h in range(2):
+            terms = [(p[r][0], second)[h], came[h], crossed[h]]
+            terms = [t for t in terms if t is not None]
+            total = add(*terms) if len(terms) > 1 else terms[0]
+            if h == 0:
+                total, second = barrier((total, second))
+            if r == ring - 2:
+                total, own_q[h] = barrier((total, own_q[h]))
+            came[h] = send_forward(total)
+    crossed = [send_across(h) for h in own_q]
     mixed = [mixed_near, mixed_far]
-    return finish(side_word, *[[mixed[h], p[0][h], came[h], crossed[h]] for h in range(2)])
+    return finish(*[[mixed[h], p[0][h], came[h], crossed[h]] for h in range(2)])
 
 
 def solution(mesh):

time: 151 us -> 142 us (0.940)
  starting transfers between devices: 40.2 us -> 46.1 us
  waiting for transfers between devices: 52.4 us -> 46.5 us
  Pallas kernels: 49.1 us -> 44.1 us
  local copies, waits for them, and re-layouts: 4.96 us -> 2.43 us
    ppermute x45, waiting for transfers between devices: 45.7 us -> 39.7 us  [sender(): return lambda x: lax.ppermute(x, 'wide', shift(*by))]
    ppermute x45, starting transfers between devices: 36.1 us -> 41.4 us  [sender(): return lambda x: lax.ppermute(x, 'wide', shift(*by))]
    pallas_call x6, Pallas kernels: 17.7 us -> 13.9 us  [the longest x2 9.85 us: attention(): pl.pallas_call(functools.partial(attention_kernel, g), grid=(1,), in_spec...]
    pallas_call x1, Pallas kernels: 5.54 us -> 3.67 us  [projection(): pl.pallas_call(functools.partial(projection_kernel, len(pieces), n_blocks...]
    pallas_call x1 -> x2, Pallas kernels: 6.49 us -> 7.56 us  [fetch(): pl.pallas_call(fetch_kernel, in_specs=[ANY] * len(arrays), out_specs=[VME...]
  transfers between devices with their start and end apart: 49 -> 49, of which waited for: 21 -> 22; matrix products, arithmetic and copies ran while one was open for 4% -> 1% of each run, Pallas kernels for 28% -> 30%
where the time goes in v4:
time: 142 us
  waiting for transfers between devices  46.5 us (33%)
  starting transfers between devices  46.1 us (32%)
  Pallas kernels  44.1 us (31%)
  local copies, waits for them, and re-layouts  2.43 us (2%)
  other arithmetic  2.1 us (1%)
    ppermute x45, starting transfers between devices, sender(): return lambda x: lax.ppermute(x, 'wide', shift(*by))  41.4 us
    ppermute x45, waiting for transfers between devices, sender(): return lambda x: lax.ppermute(x, 'wide', shift(*by))  39.7 us
    pallas_call x4, Pallas kernels, experts(): pl.pallas_call(functools.partial(experts_kernel, first_pair, pairs, n_in,...  17.6 us
    pallas_call x2, Pallas kernels, attention(): pl.pallas_call(functools.partial(attention_kernel, g), grid=(1,), in_spec...  9.85 us
    pallas_call x2, Pallas kernels, fetch(): pl.pallas_call(fetch_kernel, in_specs=[ANY] * len(arrays), out_specs=[VME...  7.56 us
    ppermute x4, waiting for transfers between devices, side_sender(): return lambda x: lax.ppermute(x, ('groups', 'wide'), pairs)  6.84 us
    ppermute x4, starting transfers between devices, side_sender(): return lambda x: lax.ppermute(x, ('groups', 'wide'), pairs)  4.66 us
    pallas_call x1, Pallas kernels, projection(): pl.pallas_call(functools.partial(projection_kernel, len(pieces), n_blocks...  3.67 us
  transfers between devices with their start and end apart: 49, of which 22 were waited for; matrix products, arithmetic and copies ran while one was open for 1% of the time, Pallas kernels for 30%

profile of v4, /device:TPU:0, one launch (start us, length us, event | category | flops | bytes accessed | tf_op | source)
XLA Modules:
  0.0 141.7 jit_solution(11315562817333483487)
XLA Ops:
  3.7 3.0 %collective-permute-start.1 = (bf16[272,512]{1,0:T(8,128)(2,1)S(1)}, bf16[272,512]{1,0:T(8,128)(2,1)S(1)}, u32[]{:S(2)}, u32[]{:S(2)}) collective-permute-start(bf16[272,512]{1,0:T(8,128)(2,1)S(1)} %pad_maximum_fusion.refs_8_.refs_0_), channel_id=1, source_target_pairs={{0,4},{1,5},{2,6},{3,7},{4,8},{5,9},{6,10},{7,11},{8,12},{9,13},{1... | collective-permute-start | bytes 835592 | tf_op jit(solution)/shard_map/ppermute | solution.py:553
  8.2 4.9 %attention.2.refs_0_ = bf16[128,1024]{1,0:T(8,128)(2,1)} custom-call(s32[16]{0:T(128)} %len_ref.1, bf16[128,2048]{1,0:T(8,128)(2,1)} %q_ref.3, bf16[128,256]{1,0:T(8,128)(2,1)} %nk_ref.3, bf16[128,256]{1,0:T(8,128)(2,1)} %nv_ref.3, bf16[2048,256]{1,0:T(8,128)(2,1)} %bitcast.24, bf16[2048,256]{1,0:T(8,128)(2,1)} %bitcast.26), custom_call_target="tpu_custom_call" | custom-call | flops 5368709120 | bytes 1048576 | tf_op jit(solution)/shard_map/attention/pallas_call | solution.py:112
  13.1 2.5 %collective-permute-done.1.refs_9_.refs_1_ = bf16[272,512]{1,0:T(8,128)(2,1)S(1)} collective-permute-done((bf16[272,512]{1,0:T(8,128)(2,1)S(1)}, bf16[272,512]{1,0:T(8,128)(2,1)S(1)}, u32[]{:S(2)}, u32[]{:S(2)}) %collective-permute-start.1) | collective-permute-done | bytes 278560 | tf_op jit(solution)/shard_map/ppermute | solution.py:553
  19.7 4.9 %attention.3.refs_1_ = bf16[128,1024]{1,0:T(8,128)(2,1)} custom-call(s32[16]{0:T(128)} %len_ref.1, bf16[128,2048]{1,0:T(8,128)(2,1)} %q_ref.3, bf16[128,256]{1,0:T(8,128)(2,1)} %nk_ref.3, bf16[128,256]{1,0:T(8,128)(2,1)} %nv_ref.3, bf16[2048,256]{1,0:T(8,128)(2,1)} %bitcast.25, bf16[2048,256]{1,0:T(8,128)(2,1)} %bitcast.27), custom_call_target="tpu_custom_call" | custom-call | flops 5368709120 | bytes 1048576 | tf_op jit(solution)/shard_map/attention/pallas_call | solution.py:112
  26.9 1.7 %collective-permute-start.8 = (bf16[272,512]{1,0:T(8,128)(2,1)S(1)}, bf16[272,512]{1,0:T(8,128)(2,1)S(1)}, u32[]{:S(2)}, u32[]{:S(2)}) collective-permute-start(bf16[272,512]{1,0:T(8,128)(2,1)S(1)} %collective-permute-done.4.refs_10_.refs_4_), channel_id=1, source_target_pairs={{0,4},{1,5},{2,6},{3,7},{4,8},{5,9},{6,10},{7,11},{8,12},{9,13},{1... | collective-permute-start | bytes 835592 | tf_op jit(solution)/shard_map/ppermute | solution.py:553
  29.6 4.2 %collective-permute-done.15.refs_5_ = bf16[128,1024]{1,0:T(8,128)(2,1)S(1)} collective-permute-done((bf16[128,1024]{1,0:T(8,128)(2,1)}, bf16[128,1024]{1,0:T(8,128)(2,1)S(1)}, u32[]{:S(2)}, u32[]{:S(2)}) %collective-permute-start.15) | collective-permute-done | bytes 262176 | tf_op jit(solution)/shard_map/ppermute | solution.py:561
  33.8 2.8 %collective-permute-done.8.refs_11_.refs_6_ = bf16[272,512]{1,0:T(8,128)(2,1)S(1)} collective-permute-done((bf16[272,512]{1,0:T(8,128)(2,1)S(1)}, bf16[272,512]{1,0:T(8,128)(2,1)S(1)}, u32[]{:S(2)}, u32[]{:S(2)}) %collective-permute-start.8) | collective-permute-done | bytes 278560 | tf_op jit(solution)/shard_map/ppermute | solution.py:553
  39.7 3.7 %projection.1 = (f32[512,512]{1,0:T(8,128)S(1)}, bf16[512,256]{1,0:T(8,128)(2,1)S(1)}) custom-call(bf16[128,1024]{1,0:T(8,128)(2,1)} %attention.2.refs_0_, bf16[128,1024]{1,0:T(8,128)(2,1)} %attention.3.refs_1_, bf16[128,1024]{1,0:T(8,128)(2,1)} %copy-done.13, bf16[128,1024]{1,0:T(8,128)(2,1)} %copy-done.15, bf16[128,1024]{1,0:T(8,128)(2,1)} %copy-done.12, ...), custom_call_target="tpu_custom_call" | custom-call | flops 1073741824 | bytes 2097152 | tf_op jit(solution)/shard_map/projection/pallas_call | solution.py:195
  43.4 1.7 %collective-permute-done.13.second_ref.refs_8_ = bf16[272,256]{1,0:T(8,128)(2,1)S(1)} collective-permute-done((bf16[272,256]{1,0:T(8,128)(2,1)S(1)}, bf16[272,256]{1,0:T(8,128)(2,1)S(1)}, u32[]{:S(2)}, u32[]{:S(2)}) %collective-permute-start.13) | collective-permute-done | bytes 139296 | tf_op jit(solution)/shard_map/ppermute | solution.py:553
  48.5 1.5 %collective-permute-start.26 = (bf16[128,1024]{1,0:T(8,128)(2,1)S(1)}, bf16[128,1024]{1,0:T(8,128)(2,1)S(1)}, u32[]{:S(2)}, u32[]{:S(2)}) collective-permute-start(bf16[128,1024]{1,0:T(8,128)(2,1)S(1)} %get-tuple-element.184.refs_0_), channel_id=1, source_target_pairs={{0,2},{1,3},{2,0},{3,1},{4,6},{5,7},{6,4},{7,5},{8,10},{9,11},{10,... | collective-permute-start | bytes 786440 | tf_op jit(solution)/shard_map/ppermute | solution.py:553
  51.8 1.9 %collective-permute-done.20.refs_1_ = bf16[128,512]{1,0:T(8,128)(2,1)S(1)} collective-permute-done((bf16[128,512]{1,0:T(8,128)(2,1)S(1)}, bf16[128,512]{1,0:T(8,128)(2,1)S(1)}, u32[]{:S(2)}, u32[]{:S(2)}) %collective-permute-start.20) | collective-permute-done | bytes 131104 | tf_op jit(solution)/shard_map/ppermute | solution.py:561
  54.9 1.5 %collective-permute-start.22 = (bf16[128,1024]{1,0:T(8,128)(2,1)S(1)}, bf16[128,1024]{1,0:T(8,128)(2,1)S(1)}, u32[]{:S(2)}, u32[]{:S(2)}) collective-permute-start(bf16[128,1024]{1,0:T(8,128)(2,1)S(1)} %get-tuple-element.185.refs_1_), channel_id=1, source_target_pairs={{0,2},{1,3},{2,0},{3,1},{4,6},{5,7},{6,4},{7,5},{8,10},{9,11},{10,... | collective-permute-start | bytes 786440 | tf_op jit(solution)/shard_map/ppermute | solution.py:553
  56.4 3.8 %fetch.2 = (bf16[2048,768]{1,0:T(8,128)(2,1)S(1)}, bf16[2048,768]{1,0:T(8,128)(2,1)S(1)}, bf16[768,2048]{1,0:T(8,128)(2,1)S(1)}, f32[8,128]{1,0:T(8,128)S(1)}) custom-call(bf16[2048,768]{1,0:T(8,128)(2,1)} %bitcast.19, bf16[2048,768]{1,0:T(8,128)(2,1)} %bitcast.21, bf16[768,2048]{1,0:T(8,128)(2,1)} %bitcast.23), custom_call_target="tpu_custom_call" | custom-call | tf_op jit(solution)/shard_map/fetch/pallas_call | solution.py:402
  62.0 3.8 %collective-permute-done.21.refs_3_ = bf16[128,1024]{1,0:T(8,128)(2,1)S(1)} collective-permute-done((bf16[128,1024]{1,0:T(8,128)(2,1)S(1)}, bf16[128,1024]{1,0:T(8,128)(2,1)S(1)}, u32[]{:S(2)}, u32[]{:S(2)}) %collective-permute-start.21) | collective-permute-done | bytes 262176 | tf_op jit(solution)/shard_map/ppermute | solution.py:553
  66.8 3.8 %fetch.3 = (bf16[2048,768]{1,0:T(8,128)(2,1)S(1)}, bf16[2048,768]{1,0:T(8,128)(2,1)S(1)}, bf16[768,2048]{1,0:T(8,128)(2,1)S(1)}, f32[8,128]{1,0:T(8,128)S(1)}) custom-call(bf16[2048,768]{1,0:T(8,128)(2,1)} %copy-done.3, bf16[2048,768]{1,0:T(8,128)(2,1)} %collective-permute-done.7.refs_1_, bf16[768,2048]{1,0:T(8,128)(2,1)} %collective-permute-done.11.refs_2_), custom_call_target="tpu_custom_call" | custom-call | tf_op jit(solution)/shard_map/fetch/pallas_call | solution.py:402
  70.6 4.4 %experts.4 = (bf16[128,1024]{1,0:T(8,128)(2,1)S(1)}, bf16[128,1024]{1,0:T(8,128)(2,1)S(1)}, bf16[128,1024]{1,0:T(8,128)(2,1)S(1)}, bf16[128,1024]{1,0:T(8,128)(2,1)S(1)}) custom-call(f32[1,2048]{1,0:T(1,128)S(1)} %bitcast.14, s32[4,2,256]{2,1,0:T(2,128)S(1)} %get-tuple-element.181.slot_rows, s32[4,256,2]{2,1,0:T(8,128)S(1)} %get-tuple-element.182.slot_cols, ...), custom_call_target="tpu_custom_call" | custom-call | flops 2717908992 | bytes 18874368 | tf_op jit(solution)/shard_map/experts/pallas_call | solution.py:486
  77.0 2.3 %collective-permute-start.31 = (bf16[128,1024]{1,0:T(8,128)(2,1)S(1)}, bf16[128,1024]{1,0:T(8,128)(2,1)S(1)}, u32[]{:S(2)}, u32[]{:S(2)}) collective-permute-start(bf16[128,1024]{1,0:T(8,128)(2,1)S(1)} %collective-permute-done.23.refs_1_), channel_id=1, source_target_pairs={{0,4},{1,5},{2,6},{3,7},{4,8},{5,9},{6,10},{7,11},{8,12},{9,13},{1... | collective-permute-start | bytes 786440 | tf_op jit(solution)/shard_map/ppermute | solution.py:553
  80.3 4.4 %experts.5 = (bf16[128,1024]{1,0:T(8,128)(2,1)S(1)}, bf16[128,1024]{1,0:T(8,128)(2,1)S(1)}, bf16[128,1024]{1,0:T(8,128)(2,1)S(1)}, bf16[128,1024]{1,0:T(8,128)(2,1)S(1)}) custom-call(f32[1,2048]{1,0:T(1,128)S(1)} %bitcast.15, s32[4,2,256]{2,1,0:T(2,128)S(1)} %get-tuple-element.181.slot_rows, s32[4,256,2]{2,1,0:T(8,128)S(1)} %get-tuple-element.182.slot_cols, ...), custom_call_target="tpu_custom_call" | custom-call | flops 2717908992 | bytes 18874368 | tf_op jit(solution)/shard_map/experts/pallas_call | solution.py:486
  86.1 3.8 %collective-permute-done.31.refs_1_ = bf16[128,1024]{1,0:T(8,128)(2,1)S(1)} collective-permute-done((bf16[128,1024]{1,0:T(8,128)(2,1)S(1)}, bf16[128,1024]{1,0:T(8,128)(2,1)S(1)}, u32[]{:S(2)}, u32[]{:S(2)}) %collective-permute-start.31) | collective-permute-done | bytes 262176 | tf_op jit(solution)/shard_map/ppermute | solution.py:553
  92.2 2.3 %collective-permute-start.43 = (bf16[128,1024]{1,0:T(8,128)(2,1)S(1)}, bf16[128,1024]{1,0:T(8,128)(2,1)S(1)}, u32[]{:S(2)}, u32[]{:S(2)}) collective-permute-start(bf16[128,1024]{1,0:T(8,128)(2,1)S(1)} %get-tuple-element.248), channel_id=1, source_target_pairs={{0,4},{1,5},{2,6},{3,7},{4,8},{5,9},{6,10},{7,11},{8,12},{9,13},{1... | collective-permute-start | bytes 786440 | tf_op jit(solution)/shard_map/ppermute | solution.py:553
  94.5 4.4 %experts.6 = (bf16[128,1024]{1,0:T(8,128)(2,1)S(1)}, bf16[128,1024]{1,0:T(8,128)(2,1)S(1)}, bf16[128,1024]{1,0:T(8,128)(2,1)S(1)}, bf16[128,1024]{1,0:T(8,128)(2,1)S(1)}) custom-call(f32[1,2048]{1,0:T(1,128)S(1)} %bitcast.16, s32[4,2,256]{2,1,0:T(2,128)S(1)} %get-tuple-element.181.slot_rows, s32[4,256,2]{2,1,0:T(8,128)S(1)} %get-tuple-element.182.slot_cols, ...), custom_call_target="tpu_custom_call" | custom-call | flops 2717908992 | bytes 18874368 | tf_op jit(solution)/shard_map/experts/pallas_call | solution.py:486
  98.9 2.0 %collective-permute-done.33.refs_2_ = bf16[128,1024]{1,0:T(8,128)(2,1)S(1)} collective-permute-done((bf16[128,1024]{1,0:T(8,128)(2,1)S(1)}, bf16[128,1024]{1,0:T(8,128)(2,1)S(1)}, u32[]{:S(2)}, u32[]{:S(2)}) %collective-permute-start.33) | collective-permute-done | bytes 262176 | tf_op jit(solution)/shard_map/ppermute | solution.py:553
  102.0 3.0 %collective-permute-done.35 = bf16[128,1024]{1,0:T(8,128)(2,1)S(1)} collective-permute-done((bf16[128,1024]{1,0:T(8,128)(2,1)S(1)}, bf16[128,1024]{1,0:T(8,128)(2,1)S(1)}, u32[]{:S(2)}, u32[]{:S(2)}) %collective-permute-start.35) | collective-permute-done | bytes 262176 | tf_op jit(solution)/shard_map/ppermute | solution.py:553
  105.1 2.4 %collective-permute-start.36 = (bf16[128,1024]{1,0:T(8,128)(2,1)S(1)}, bf16[128,1024]{1,0:T(8,128)(2,1)S(1)}, u32[]{:S(2)}, u32[]{:S(2)}) collective-permute-start(bf16[128,1024]{1,0:T(8,128)(2,1)S(1)} %add_convert_fusion.5), channel_id=1, source_target_pairs={{0,4},{1,5},{2,6},{3,7},{4,8},{5,9},{6,10},{7,11},{8,12},{9,13},{1... | collective-permute-start | bytes 786440 | tf_op jit(solution)/shard_map/ppermute | solution.py:553
  108.9 4.4 %experts.7 = (bf16[128,1024]{1,0:T(8,128)(2,1)S(1)}, bf16[128,1024]{1,0:T(8,128)(2,1)S(1)}, bf16[128,1024]{1,0:T(8,128)(2,1)S(1)}, bf16[128,1024]{1,0:T(8,128)(2,1)S(1)}) custom-call(f32[1,2048]{1,0:T(1,128)S(1)} %bitcast.17, s32[4,2,256]{2,1,0:T(2,128)S(1)} %get-tuple-element.181.slot_rows, s32[4,256,2]{2,1,0:T(8,128)S(1)} %get-tuple-element.182.slot_cols, ...), custom_call_target="tpu_custom_call" | custom-call | flops 2717908992 | bytes 18874368 | tf_op jit(solution)/shard_map/experts/pallas_call | solution.py:486
  115.5 2.2 %collective-permute-start.38 = (bf16[128,1024]{1,0:T(8,128)(2,1)S(1)}, bf16[128,1024]{1,0:T(8,128)(2,1)S(1)}, u32[]{:S(2)}, u32[]{:S(2)}) collective-permute-start(bf16[128,1024]{1,0:T(8,128)(2,1)S(1)} %add_convert_fusion.4), channel_id=1, source_target_pairs={{0,4},{1,5},{2,6},{3,7},{4,8},{5,9},{6,10},{7,11},{8,12},{9,13},{1... | collective-permute-start | bytes 786440 | tf_op jit(solution)/shard_map/ppermute | solution.py:553
  117.7 2.0 %collective-permute-done.42 = bf16[128,1024]{1,0:T(8,128)(2,1)S(1)} collective-permute-done((bf16[128,1024]{1,0:T(8,128)(2,1)S(1)}, bf16[128,1024]{1,0:T(8,128)(2,1)S(1)}, u32[]{:S(2)}, u32[]{:S(2)}) %collective-permute-start.42) | collective-permute-done | bytes 262176 | tf_op jit(solution)/shard_map/ppermute | solution.py:553
  123.6 2.5 %collective-permute-done.38 = bf16[128,1024]{1,0:T(8,128)(2,1)S(1)} collective-permute-done((bf16[128,1024]{1,0:T(8,128)(2,1)S(1)}, bf16[128,1024]{1,0:T(8,128)(2,1)S(1)}, u32[]{:S(2)}, u32[]{:S(2)}) %collective-permute-start.38) | collective-permute-done | bytes 262176 | tf_op jit(solution)/shard_map/ppermute | solution.py:553
  128.2 3.5 %collective-permute-done.45 = bf16[128,1024]{1,0:T(8,128)(2,1)S(1)} collective-permute-done((bf16[128,1024]{1,0:T(8,128)(2,1)S(1)}, bf16[128,1024]{1,0:T(8,128)(2,1)S(1)}, u32[]{:S(2)}, u32[]{:S(2)}) %collective-permute-start.45) | collective-permute-done | bytes 262176 | tf_op jit(solution)/shard_map/ppermute | solution.py:553
  133.0 2.8 %collective-permute-done.48.refs_7_ = bf16[128,1024]{1,0:T(8,128)(2,1)S(1)} collective-permute-done((bf16[128,1024]{1,0:T(8,128)(2,1)S(1)}, bf16[128,1024]{1,0:T(8,128)(2,1)S(1)}, u32[]{:S(2)}, u32[]{:S(2)}) %collective-permute-start.48) | collective-permute-done | bytes 262176 | tf_op jit(solution)/shard_map/ppermute | solution.py:553
  135.8 4.3 %collective-permute-done.47.refs_6_ = bf16[128,1024]{1,0:T(8,128)(2,1)S(1)} collective-permute-done((bf16[128,1024]{1,0:T(8,128)(2,1)S(1)}, bf16[128,1024]{1,0:T(8,128)(2,1)S(1)}, u32[]{:S(2)}, u32[]{:S(2)}) %collective-permute-start.47) | collective-permute-done | bytes 262176 | tf_op jit(solution)/shard_map/ppermute | solution.py:553
  140.1 1.5 %finish.1 = bf16[128,2048]{1,0:T(8,128)(2,1)} custom-call(f32[128,1024]{1,0:T(8,128)S(1)} %get-tuple-element.154.refs_0_, bf16[128,1024]{1,0:T(8,128)(2,1)S(1)} %get-tuple-element.206.refs_1_, bf16[128,1024]{1,0:T(8,128)(2,1)S(1)} %collective-permute-done.40.refs_2_, bf16[128,1024]{1,0:T(8,128)(2,1)S(1)} %collective-permute-done.41.refs_3_, ...), custom_call_target="tpu_custom_call" | custom-call | tf_op jit(solution)/shard_map/finish/pallas_call | solution.py:298
  (129 shorter events, 43.2 us)
Async XLA Ops:
  3.0 12.6 %collective-permute-start.3 = (bf16[2048,768]{1,0:T(8,128)(2,1)}, bf16[2048,768]{1,0:T(8,128)(2,1)S(1)}, u32[]{:S(2)}, u32[]{:S(2)}) collective-permute-start(bf16[2048,768]{1,0:T(8,128)(2,1)} %bitcast.18), channel_id=1, source_target_pairs={{0,1},{1,0},{2,3},{3,2},{4,5},{5,4},{6,7},{7,6},{8,9},{9,8},{10,11... | collective-permute-start | bytes 9437192 | tf_op jit(solution)/shard_map/ppermute | solution.py:553
  3.1 21.5 %collective-permute-start.7 = (bf16[2048,768]{1,0:T(8,128)(2,1)}, bf16[2048,768]{1,0:T(8,128)(2,1)}, u32[]{:S(2)}, u32[]{:S(2)}) collective-permute-start(bf16[2048,768]{1,0:T(8,128)(2,1)} %bitcast.20), channel_id=1, source_target_pairs={{0,1},{1,0},{2,3},{3,2},{4,5},{5,4},{6,7},{7,6},{8,9},{9,8},{10,11... | collective-permute-start | bytes 9437192 | tf_op jit(solution)/shard_map/ppermute | solution.py:553
  3.6 25.5 %collective-permute-start.11 = (bf16[768,2048]{1,0:T(8,128)(2,1)}, bf16[768,2048]{1,0:T(8,128)(2,1)}, u32[]{:S(2)}, u32[]{:S(2)}) collective-permute-start(bf16[768,2048]{1,0:T(8,128)(2,1)} %bitcast.22), channel_id=1, source_target_pairs={{0,1},{1,0},{2,3},{3,2},{4,5},{5,4},{6,7},{7,6},{8,9},{9,8},{10,11... | collective-permute-start | bytes 9437192 | tf_op jit(solution)/shard_map/ppermute | solution.py:553
  3.7 11.9 %collective-permute-start.1 = (bf16[272,512]{1,0:T(8,128)(2,1)S(1)}, bf16[272,512]{1,0:T(8,128)(2,1)S(1)}, u32[]{:S(2)}, u32[]{:S(2)}) collective-permute-start(bf16[272,512]{1,0:T(8,128)(2,1)S(1)} %pad_maximum_fusion.refs_8_.refs_0_), channel_id=1, source_target_pairs={{0,4},{1,5},{2,6},{3,7},{4,8},{5,9},{6,10},{7,11},{8,12},{9,13},{1... | collective-permute-start | bytes 835592 | tf_op jit(solution)/shard_map/ppermute | solution.py:553
  15.6 10.0 %collective-permute-start.4 = (bf16[272,512]{1,0:T(8,128)(2,1)S(1)}, bf16[272,512]{1,0:T(8,128)(2,1)S(1)}, u32[]{:S(2)}, u32[]{:S(2)}) collective-permute-start(bf16[272,512]{1,0:T(8,128)(2,1)S(1)} %collective-permute-done.1.refs_9_.refs_1_), channel_id=1, source_target_pairs={{0,4},{1,5},{2,6},{3,7},{4,8},{5,9},{6,10},{7,11},{8,12},{9,13},{1... | collective-permute-start | bytes 835592 | tf_op jit(solution)/shard_map/ppermute | solution.py:553
  26.9 9.7 %collective-permute-start.8 = (bf16[272,512]{1,0:T(8,128)(2,1)S(1)}, bf16[272,512]{1,0:T(8,128)(2,1)S(1)}, u32[]{:S(2)}, u32[]{:S(2)}) collective-permute-start(bf16[272,512]{1,0:T(8,128)(2,1)S(1)} %collective-permute-done.4.refs_10_.refs_4_), channel_id=1, source_target_pairs={{0,4},{1,5},{2,6},{3,7},{4,8},{5,9},{6,10},{7,11},{8,12},{9,13},{1... | collective-permute-start | bytes 835592 | tf_op jit(solution)/shard_map/ppermute | solution.py:553
  48.4 11.8 %collective-permute-start.25 = (bf16[128,1024]{1,0:T(8,128)(2,1)S(1)}, bf16[128,1024]{1,0:T(8,128)(2,1)S(1)}, u32[]{:S(2)}, u32[]{:S(2)}) collective-permute-start(bf16[128,1024]{1,0:T(8,128)(2,1)S(1)} %get-tuple-element.184.refs_0_), channel_id=1, source_target_pairs={{0,4},{1,5},{2,6},{3,7},{4,8},{5,9},{6,10},{7,11},{8,12},{9,13},{1... | collective-permute-start | bytes 786440 | tf_op jit(solution)/shard_map/ppermute | solution.py:553
  48.5 11.8 %collective-permute-start.26 = (bf16[128,1024]{1,0:T(8,128)(2,1)S(1)}, bf16[128,1024]{1,0:T(8,128)(2,1)S(1)}, u32[]{:S(2)}, u32[]{:S(2)}) collective-permute-start(bf16[128,1024]{1,0:T(8,128)(2,1)S(1)} %get-tuple-element.184.refs_0_), channel_id=1, source_target_pairs={{0,2},{1,3},{2,0},{3,1},{4,6},{5,7},{6,4},{7,5},{8,10},{9,11},{10,... | collective-permute-start | bytes 786440 | tf_op jit(solution)/shard_map/ppermute | solution.py:553
  54.8 10.9 %collective-permute-start.21 = (bf16[128,1024]{1,0:T(8,128)(2,1)S(1)}, bf16[128,1024]{1,0:T(8,128)(2,1)S(1)}, u32[]{:S(2)}, u32[]{:S(2)}) collective-permute-start(bf16[128,1024]{1,0:T(8,128)(2,1)S(1)} %get-tuple-element.185.refs_1_), channel_id=1, source_target_pairs={{0,4},{1,5},{2,6},{3,7},{4,8},{5,9},{6,10},{7,11},{8,12},{9,13},{1... | collective-permute-start | bytes 786440 | tf_op jit(solution)/shard_map/ppermute | solution.py:553
  54.9 10.9 %collective-permute-start.22 = (bf16[128,1024]{1,0:T(8,128)(2,1)S(1)}, bf16[128,1024]{1,0:T(8,128)(2,1)S(1)}, u32[]{:S(2)}, u32[]{:S(2)}) collective-permute-start(bf16[128,1024]{1,0:T(8,128)(2,1)S(1)} %get-tuple-element.185.refs_1_), channel_id=1, source_target_pairs={{0,2},{1,3},{2,0},{3,1},{4,6},{5,7},{6,4},{7,5},{8,10},{9,11},{10,... | collective-permute-start | bytes 786440 | tf_op jit(solution)/shard_map/ppermute | solution.py:553
  60.2 14.8 %collective-permute-start.27 = (bf16[128,1024]{1,0:T(8,128)(2,1)S(1)}, bf16[128,1024]{1,0:T(8,128)(2,1)S(1)}, u32[]{:S(2)}, u32[]{:S(2)}) collective-permute-start(bf16[128,1024]{1,0:T(8,128)(2,1)S(1)} %collective-permute-done.25.refs_2_), channel_id=1, source_target_pairs={{0,4},{1,5},{2,6},{3,7},{4,8},{5,9},{6,10},{7,11},{8,12},{9,13},{1... | collective-permute-start | bytes 786440 | tf_op jit(solution)/shard_map/ppermute | solution.py:553
  60.7 14.4 %collective-permute-start.28 = (bf16[128,1024]{1,0:T(8,128)(2,1)S(1)}, bf16[128,1024]{1,0:T(8,128)(2,1)S(1)}, u32[]{:S(2)}, u32[]{:S(2)}) collective-permute-start(bf16[128,1024]{1,0:T(8,128)(2,1)S(1)} %collective-permute-done.25.refs_2_), channel_id=1, source_target_pairs={{0,2},{1,3},{2,0},{3,1},{4,6},{5,7},{6,4},{7,5},{8,10},{9,11},{10,... | collective-permute-start | bytes 786440 | tf_op jit(solution)/shard_map/ppermute | solution.py:553
  65.8 11.2 %collective-permute-start.23 = (bf16[128,1024]{1,0:T(8,128)(2,1)S(1)}, bf16[128,1024]{1,0:T(8,128)(2,1)S(1)}, u32[]{:S(2)}, u32[]{:S(2)}) collective-permute-start(bf16[128,1024]{1,0:T(8,128)(2,1)S(1)} %collective-permute-done.21.refs_3_), channel_id=1, source_target_pairs={{0,4},{1,5},{2,6},{3,7},{4,8},{5,9},{6,10},{7,11},{8,12},{9,13},{1... | collective-permute-start | bytes 786440 | tf_op jit(solution)/shard_map/ppermute | solution.py:553
  65.8 11.2 %collective-permute-start.24 = (bf16[128,1024]{1,0:T(8,128)(2,1)S(1)}, bf16[128,1024]{1,0:T(8,128)(2,1)S(1)}, u32[]{:S(2)}, u32[]{:S(2)}) collective-permute-start(bf16[128,1024]{1,0:T(8,128)(2,1)S(1)} %collective-permute-done.21.refs_3_), channel_id=1, source_target_pairs={{0,2},{1,3},{2,0},{3,1},{4,6},{5,7},{6,4},{7,5},{8,10},{9,11},{10,... | collective-permute-start | bytes 786440 | tf_op jit(solution)/shard_map/ppermute | solution.py:553
  75.0 11.1 %collective-permute-start.29 = (bf16[128,1024]{1,0:T(8,128)(2,1)S(1)}, bf16[128,1024]{1,0:T(8,128)(2,1)S(1)}, u32[]{:S(2)}, u32[]{:S(2)}) collective-permute-start(bf16[128,1024]{1,0:T(8,128)(2,1)S(1)} %collective-permute-done.27.refs_0_), channel_id=1, source_target_pairs={{0,4},{1,5},{2,6},{3,7},{4,8},{5,9},{6,10},{7,11},{8,12},{9,13},{1... | collective-permute-start | bytes 786440 | tf_op jit(solution)/shard_map/ppermute | solution.py:553
  76.0 10.1 %collective-permute-start.30 = (bf16[128,1024]{1,0:T(8,128)(2,1)S(1)}, bf16[128,1024]{1,0:T(8,128)(2,1)S(1)}, u32[]{:S(2)}, u32[]{:S(2)}) collective-permute-start(bf16[128,1024]{1,0:T(8,128)(2,1)S(1)} %collective-permute-done.27.refs_0_), channel_id=1, source_target_pairs={{0,2},{1,3},{2,0},{3,1},{4,6},{5,7},{6,4},{7,5},{8,10},{9,11},{10,... | collective-permute-start | bytes 786440 | tf_op jit(solution)/shard_map/ppermute | solution.py:553
  77.0 12.9 %collective-permute-start.31 = (bf16[128,1024]{1,0:T(8,128)(2,1)S(1)}, bf16[128,1024]{1,0:T(8,128)(2,1)S(1)}, u32[]{:S(2)}, u32[]{:S(2)}) collective-permute-start(bf16[128,1024]{1,0:T(8,128)(2,1)S(1)} %collective-permute-done.23.refs_1_), channel_id=1, source_target_pairs={{0,4},{1,5},{2,6},{3,7},{4,8},{5,9},{6,10},{7,11},{8,12},{9,13},{1... | collective-permute-start | bytes 786440 | tf_op jit(solution)/shard_map/ppermute | solution.py:553
  79.3 10.6 %collective-permute-start.32 = (bf16[128,1024]{1,0:T(8,128)(2,1)S(1)}, bf16[128,1024]{1,0:T(8,128)(2,1)S(1)}, u32[]{:S(2)}, u32[]{:S(2)}) collective-permute-start(bf16[128,1024]{1,0:T(8,128)(2,1)S(1)} %collective-permute-done.23.refs_1_), channel_id=1, source_target_pairs={{0,2},{1,3},{2,0},{3,1},{4,6},{5,7},{6,4},{7,5},{8,10},{9,11},{10,... | collective-permute-start | bytes 786440 | tf_op jit(solution)/shard_map/ppermute | solution.py:553
  89.9 11.0 %collective-permute-start.33 = (bf16[128,1024]{1,0:T(8,128)(2,1)S(1)}, bf16[128,1024]{1,0:T(8,128)(2,1)S(1)}, u32[]{:S(2)}, u32[]{:S(2)}) collective-permute-start(bf16[128,1024]{1,0:T(8,128)(2,1)S(1)} %collective-permute-done.30.refs_2_), channel_id=1, source_target_pairs={{0,4},{1,5},{2,6},{3,7},{4,8},{5,9},{6,10},{7,11},{8,12},{9,13},{1... | collective-permute-start | bytes 786440 | tf_op jit(solution)/shard_map/ppermute | solution.py:553
  90.2 10.8 %collective-permute-start.34 = (bf16[128,1024]{1,0:T(8,128)(2,1)S(1)}, bf16[128,1024]{1,0:T(8,128)(2,1)S(1)}, u32[]{:S(2)}, u32[]{:S(2)}) collective-permute-start(bf16[128,1024]{1,0:T(8,128)(2,1)S(1)} %collective-permute-done.31.refs_1_), channel_id=1, source_target_pairs={{0,2},{1,3},{2,0},{3,1},{4,6},{5,7},{6,4},{7,5},{8,10},{9,11},{10,... | collective-permute-start | bytes 786440 | tf_op jit(solution)/shard_map/ppermute | solution.py:553
  91.2 13.8 %collective-permute-start.35 = (bf16[128,1024]{1,0:T(8,128)(2,1)S(1)}, bf16[128,1024]{1,0:T(8,128)(2,1)S(1)}, u32[]{:S(2)}, u32[]{:S(2)}) collective-permute-start(bf16[128,1024]{1,0:T(8,128)(2,1)S(1)} %get-tuple-element.230), channel_id=1, source_target_pairs={{0,2},{1,3},{2,0},{3,1},{4,6},{5,7},{6,4},{7,5},{8,10},{9,11},{10,... | collective-permute-start | bytes 786440 | tf_op jit(solution)/shard_map/ppermute | solution.py:553
  92.2 15.3 %collective-permute-start.43 = (bf16[128,1024]{1,0:T(8,128)(2,1)S(1)}, bf16[128,1024]{1,0:T(8,128)(2,1)S(1)}, u32[]{:S(2)}, u32[]{:S(2)}) collective-permute-start(bf16[128,1024]{1,0:T(8,128)(2,1)S(1)} %get-tuple-element.248), channel_id=1, source_target_pairs={{0,4},{1,5},{2,6},{3,7},{4,8},{5,9},{6,10},{7,11},{8,12},{9,13},{1... | collective-permute-start | bytes 786440 | tf_op jit(solution)/shard_map/ppermute | solution.py:553
  101.0 13.4 %collective-permute-start.37 = (bf16[128,1024]{1,0:T(8,128)(2,1)S(1)}, bf16[128,1024]{1,0:T(8,128)(2,1)S(1)}, u32[]{:S(2)}, u32[]{:S(2)}) collective-permute-start(bf16[128,1024]{1,0:T(8,128)(2,1)S(1)} %get-tuple-element.233), channel_id=1, source_target_pairs={{0,2},{1,3},{2,0},{3,1},{4,6},{5,7},{6,4},{7,5},{8,10},{9,11},{10,... | collective-permute-start | bytes 786440 | tf_op jit(solution)/shard_map/ppermute | solution.py:553
  105.1 10.3 %collective-permute-start.36 = (bf16[128,1024]{1,0:T(8,128)(2,1)S(1)}, bf16[128,1024]{1,0:T(8,128)(2,1)S(1)}, u32[]{:S(2)}, u32[]{:S(2)}) collective-permute-start(bf16[128,1024]{1,0:T(8,128)(2,1)S(1)} %add_convert_fusion.5), channel_id=1, source_target_pairs={{0,4},{1,5},{2,6},{3,7},{4,8},{5,9},{6,10},{7,11},{8,12},{9,13},{1... | collective-permute-start | bytes 786440 | tf_op jit(solution)/shard_map/ppermute | solution.py:553
  107.6 10.1 %collective-permute-start.44 = (bf16[128,1024]{1,0:T(8,128)(2,1)S(1)}, bf16[128,1024]{1,0:T(8,128)(2,1)S(1)}, u32[]{:S(2)}, u32[]{:S(2)}) collective-permute-start(bf16[128,1024]{1,0:T(8,128)(2,1)S(1)} %add_convert_fusion.2), channel_id=1, source_target_pairs={{0,2},{1,3},{2,0},{3,1},{4,6},{5,7},{6,4},{7,5},{8,10},{9,11},{10,... | collective-permute-start | bytes 786440 | tf_op jit(solution)/shard_map/ppermute | solution.py:553
  108.7 11.0 %collective-permute-start.42 = (bf16[128,1024]{1,0:T(8,128)(2,1)S(1)}, bf16[128,1024]{1,0:T(8,128)(2,1)S(1)}, u32[]{:S(2)}, u32[]{:S(2)}) collective-permute-start(bf16[128,1024]{1,0:T(8,128)(2,1)S(1)} %get-tuple-element.246), channel_id=1, source_target_pairs={{0,4},{1,5},{2,6},{3,7},{4,8},{5,9},{6,10},{7,11},{8,12},{9,13},{1... | collective-permute-start | bytes 786440 | tf_op jit(solution)/shard_map/ppermute | solution.py:553
  114.4 13.8 %collective-permute-start.46 = (bf16[128,1024]{1,0:T(8,128)(2,1)S(1)}, bf16[128,1024]{1,0:T(8,128)(2,1)S(1)}, u32[]{:S(2)}, u32[]{:S(2)}) collective-permute-start(bf16[128,1024]{1,0:T(8,128)(2,1)S(1)} %get-tuple-element.251), channel_id=1, source_target_pairs={{0,2},{1,3},{2,0},{3,1},{4,6},{5,7},{6,4},{7,5},{8,10},{9,11},{10,... | collective-permute-start | bytes 786440 | tf_op jit(solution)/shard_map/ppermute | solution.py:553
  115.5 10.6 %collective-permute-start.38 = (bf16[128,1024]{1,0:T(8,128)(2,1)S(1)}, bf16[128,1024]{1,0:T(8,128)(2,1)S(1)}, u32[]{:S(2)}, u32[]{:S(2)}) collective-permute-start(bf16[128,1024]{1,0:T(8,128)(2,1)S(1)} %add_convert_fusion.4), channel_id=1, source_target_pairs={{0,4},{1,5},{2,6},{3,7},{4,8},{5,9},{6,10},{7,11},{8,12},{9,13},{1... | collective-permute-start | bytes 786440 | tf_op jit(solution)/shard_map/ppermute | solution.py:553
  119.8 12.0 %collective-permute-start.45 = (bf16[128,1024]{1,0:T(8,128)(2,1)S(1)}, bf16[128,1024]{1,0:T(8,128)(2,1)S(1)}, u32[]{:S(2)}, u32[]{:S(2)}) collective-permute-start(bf16[128,1024]{1,0:T(8,128)(2,1)S(1)} %add_convert_fusion.1), channel_id=1, source_target_pairs={{0,4},{1,5},{2,6},{3,7},{4,8},{5,9},{6,10},{7,11},{8,12},{9,13},{1... | collective-permute-start | bytes 786440 | tf_op jit(solution)/shard_map/ppermute | solution.py:553
  120.5 12.4 %collective-permute-start.41 = (bf16[128,1024]{1,0:T(8,128)(2,1)S(1)}, bf16[128,1024]{1,0:T(8,128)(2,1)S(1)}, u32[]{:S(2)}, u32[]{:S(2)}) collective-permute-start(bf16[128,1024]{1,0:T(8,128)(2,1)S(1)} %get-tuple-element.241), channel_id=1, source_target_pairs={{0,2},{1,3},{2,0},{3,1},{4,6},{5,7},{6,4},{7,5},{8,10},{9,11},{10,... | collective-permute-start | bytes 786440 | tf_op jit(solution)/shard_map/ppermute | solution.py:553
  122.6 13.1 %collective-permute-start.48 = (bf16[128,1024]{1,0:T(8,128)(2,1)S(1)}, bf16[128,1024]{1,0:T(8,128)(2,1)S(1)}, u32[]{:S(2)}, u32[]{:S(2)}) collective-permute-start(bf16[128,1024]{1,0:T(8,128)(2,1)S(1)} %get-tuple-element.252), channel_id=1, source_target_pairs={{0,2},{1,3},{2,0},{3,1},{4,6},{5,7},{6,4},{7,5},{8,10},{9,11},{10,... | collective-permute-start | bytes 786440 | tf_op jit(solution)/shard_map/ppermute | solution.py:553
  126.3 9.5 %collective-permute-start.40 = (bf16[128,1024]{1,0:T(8,128)(2,1)S(1)}, bf16[128,1024]{1,0:T(8,128)(2,1)S(1)}, u32[]{:S(2)}, u32[]{:S(2)}) collective-permute-start(bf16[128,1024]{1,0:T(8,128)(2,1)S(1)} %add_convert_fusion.3), channel_id=1, source_target_pairs={{0,4},{1,5},{2,6},{3,7},{4,8},{5,9},{6,10},{7,11},{8,12},{9,13},{1... | collective-permute-start | bytes 786440 | tf_op jit(solution)/shard_map/ppermute | solution.py:553
  (35 other events, 257.2 us)

commit v5 on v4

--- a/solution.py
+++ b/solution.py
@@ -683,7 +683,8 @@
         beside_weights.extend(weights)
         kept["token2"] = token
         p0, p1 = serve(0, 1, same[:2])
-        return {("p", 0): p0, ("p", 1): p1}
+        kept["p", 0], kept["p", 1] = p0, p1
+        return {}
 
     def serve(first, count, blocks):
         halves = [h for block in blocks for h in block]
@@ -700,14 +701,15 @@
 
     def serve_other(r):
         def step(same, other):
-            q0, q1 = serve(r + 1, 1, other[r : r + 2])
-            return {("q", r): q0, ("q", r + 1): q1}
+            kept["q", r], kept["q", r + 1] = serve(r + 1, 1, other[r : r + 2])
+            return {}
 
         return step
 
     def serve_two(same, other):
         p, q = serve(ring - 2, 1, [same[ring - 2], other[ring - 2]])
-        return {("p", ring - 2): p, ("q", ring - 2): q}
+        kept["p", ring - 2], kept["q", ring - 2] = p, q
+        return {}
 
     beside = [load_mine, load_other, serve_other(0)]
     for r in range(2, ring - 2, 2):

time: 142 us -> 138 us (0.972)
  starting transfers between devices: 46.1 us -> 40.4 us
  waiting for transfers between devices: 46.5 us -> 48.1 us
    ppermute x45, starting transfers between devices: 41.4 us -> 35.7 us  [sender(): return lambda x: lax.ppermute(x, 'wide', shift(*by))]
    ppermute x45, waiting for transfers between devices: 39.7 us -> 41.1 us  [sender(): return lambda x: lax.ppermute(x, 'wide', shift(*by))]
  transfers between devices with their start and end apart: 49 -> 49, of which waited for: 22 -> 22; matrix products, arithmetic and copies ran while one was open for 1% -> 2% of each run, Pallas kernels for 30% -> 31%
where the time goes in v5:
time: 138 us
  waiting for transfers between devices  48.1 us (35%)
  Pallas kernels  44.1 us (32%)
  starting transfers between devices  40.4 us (29%)
  local copies, waits for them, and re-layouts  2.45 us (2%)
  other arithmetic  2.1 us (2%)
    ppermute x45, waiting for transfers between devices, sender(): return lambda x: lax.ppermute(x, 'wide', shift(*by))  41.1 us
    ppermute x45, starting transfers between devices, sender(): return lambda x: lax.ppermute(x, 'wide', shift(*by))  35.7 us
    pallas_call x4, Pallas kernels, experts(): pl.pallas_call(functools.partial(experts_kernel, first_pair, pairs, n_in,...  17.5 us
    pallas_call x2, Pallas kernels, attention(): pl.pallas_call(functools.partial(attention_kernel, g), grid=(1,), in_spec...  9.85 us
    pallas_call x2, Pallas kernels, fetch(): pl.pallas_call(fetch_kernel, in_specs=[ANY] * len(arrays), out_specs=[VME...  7.56 us
    ppermute x4, waiting for transfers between devices, side_sender(): return lambda x: lax.ppermute(x, ('groups', 'wide'), pairs)  6.93 us
    ppermute x4, starting transfers between devices, side_sender(): return lambda x: lax.ppermute(x, ('groups', 'wide'), pairs)  4.73 us
    pallas_call x1, Pallas kernels, projection(): pl.pallas_call(functools.partial(projection_kernel, len(pieces), n_blocks...  3.67 us
  transfers between devices with their start and end apart: 49, of which 22 were waited for; matrix products, arithmetic and copies ran while one was open for 2% of the time, Pallas kernels for 31%

profile of v5, /device:TPU:0, one launch (start us, length us, event | category | flops | bytes accessed | tf_op | source)
XLA Modules:
  0.0 137.6 jit_solution(3365430679362716309)
XLA Ops:
  3.7 3.0 %collective-permute-start.1 = (bf16[272,512]{1,0:T(8,128)(2,1)S(1)}, bf16[272,512]{1,0:T(8,128)(2,1)S(1)}, u32[]{:S(2)}, u32[]{:S(2)}) collective-permute-start(bf16[272,512]{1,0:T(8,128)(2,1)S(1)} %pad_maximum_fusion.refs_8_.refs_0_), channel_id=1, source_target_pairs={{0,4},{1,5},{2,6},{3,7},{4,8},{5,9},{6,10},{7,11},{8,12},{9,13},{1... | collective-permute-start | bytes 835592 | tf_op jit(solution)/shard_map/ppermute | solution.py:553
  8.2 4.9 %attention.2.refs_0_ = bf16[128,1024]{1,0:T(8,128)(2,1)} custom-call(s32[16]{0:T(128)} %len_ref.1, bf16[128,2048]{1,0:T(8,128)(2,1)} %q_ref.3, bf16[128,256]{1,0:T(8,128)(2,1)} %nk_ref.3, bf16[128,256]{1,0:T(8,128)(2,1)} %nv_ref.3, bf16[2048,256]{1,0:T(8,128)(2,1)} %bitcast.24, bf16[2048,256]{1,0:T(8,128)(2,1)} %bitcast.26), custom_call_target="tpu_custom_call" | custom-call | flops 5368709120 | bytes 1048576 | tf_op jit(solution)/shard_map/attention/pallas_call | solution.py:112
  13.1 2.5 %collective-permute-done.1.refs_9_.refs_1_ = bf16[272,512]{1,0:T(8,128)(2,1)S(1)} collective-permute-done((bf16[272,512]{1,0:T(8,128)(2,1)S(1)}, bf16[272,512]{1,0:T(8,128)(2,1)S(1)}, u32[]{:S(2)}, u32[]{:S(2)}) %collective-permute-start.1) | collective-permute-done | bytes 278560 | tf_op jit(solution)/shard_map/ppermute | solution.py:553
  19.7 4.9 %attention.3.refs_1_ = bf16[128,1024]{1,0:T(8,128)(2,1)} custom-call(s32[16]{0:T(128)} %len_ref.1, bf16[128,2048]{1,0:T(8,128)(2,1)} %q_ref.3, bf16[128,256]{1,0:T(8,128)(2,1)} %nk_ref.3, bf16[128,256]{1,0:T(8,128)(2,1)} %nv_ref.3, bf16[2048,256]{1,0:T(8,128)(2,1)} %bitcast.25, bf16[2048,256]{1,0:T(8,128)(2,1)} %bitcast.27), custom_call_target="tpu_custom_call" | custom-call | flops 5368709120 | bytes 1048576 | tf_op jit(solution)/shard_map/attention/pallas_call | solution.py:112
  27.0 1.6 %collective-permute-start.8 = (bf16[272,512]{1,0:T(8,128)(2,1)S(1)}, bf16[272,512]{1,0:T(8,128)(2,1)S(1)}, u32[]{:S(2)}, u32[]{:S(2)}) collective-permute-start(bf16[272,512]{1,0:T(8,128)(2,1)S(1)} %collective-permute-done.4.refs_10_.refs_4_), channel_id=1, source_target_pairs={{0,4},{1,5},{2,6},{3,7},{4,8},{5,9},{6,10},{7,11},{8,12},{9,13},{1... | collective-permute-start | bytes 835592 | tf_op jit(solution)/shard_map/ppermute | solution.py:553
  29.6 4.6 %collective-permute-done.15.refs_5_ = bf16[128,1024]{1,0:T(8,128)(2,1)S(1)} collective-permute-done((bf16[128,1024]{1,0:T(8,128)(2,1)}, bf16[128,1024]{1,0:T(8,128)(2,1)S(1)}, u32[]{:S(2)}, u32[]{:S(2)}) %collective-permute-start.15) | collective-permute-done | bytes 262176 | tf_op jit(solution)/shard_map/ppermute | solution.py:561
  34.1 3.4 %collective-permute-done.8.refs_11_.refs_6_ = bf16[272,512]{1,0:T(8,128)(2,1)S(1)} collective-permute-done((bf16[272,512]{1,0:T(8,128)(2,1)S(1)}, bf16[272,512]{1,0:T(8,128)(2,1)S(1)}, u32[]{:S(2)}, u32[]{:S(2)}) %collective-permute-start.8) | collective-permute-done | bytes 278560 | tf_op jit(solution)/shard_map/ppermute | solution.py:553
  39.5 3.7 %projection.1 = (f32[512,512]{1,0:T(8,128)S(1)}, bf16[512,256]{1,0:T(8,128)(2,1)S(1)}) custom-call(bf16[128,1024]{1,0:T(8,128)(2,1)} %attention.2.refs_0_, bf16[128,1024]{1,0:T(8,128)(2,1)} %attention.3.refs_1_, bf16[128,1024]{1,0:T(8,128)(2,1)} %copy-done.13, bf16[128,1024]{1,0:T(8,128)(2,1)} %copy-done.15, bf16[128,1024]{1,0:T(8,128)(2,1)} %copy-done.12, ...), custom_call_target="tpu_custom_call" | custom-call | flops 1073741824 | bytes 2097152 | tf_op jit(solution)/shard_map/projection/pallas_call | solution.py:195
  43.2 1.7 %collective-permute-done.13.second_ref.refs_8_ = bf16[272,256]{1,0:T(8,128)(2,1)S(1)} collective-permute-done((bf16[272,256]{1,0:T(8,128)(2,1)S(1)}, bf16[272,256]{1,0:T(8,128)(2,1)S(1)}, u32[]{:S(2)}, u32[]{:S(2)}) %collective-permute-start.13) | collective-permute-done | bytes 139296 | tf_op jit(solution)/shard_map/ppermute | solution.py:553
  45.2 1.7 %collective-permute-start.19 = (bf16[128,512]{1,0:T(8,128)(2,1)S(1)}, bf16[128,512]{1,0:T(8,128)(2,1)S(1)}, u32[]{:S(2)}, u32[]{:S(2)}) collective-permute-start(bf16[128,512]{1,0:T(8,128)(2,1)S(1)} %get-tuple-element.143), channel_id=1, source_target_pairs={{0,16},{1,17},{2,18},{3,19},{4,20},{5,21},{6,22},{7,23},{8,24},{9,... | collective-permute-start | bytes 393224 | tf_op jit(solution)/shard_map/ppermute | solution.py:561
  51.6 1.9 %collective-permute-done.20.refs_1_ = bf16[128,512]{1,0:T(8,128)(2,1)S(1)} collective-permute-done((bf16[128,512]{1,0:T(8,128)(2,1)S(1)}, bf16[128,512]{1,0:T(8,128)(2,1)S(1)}, u32[]{:S(2)}, u32[]{:S(2)}) %collective-permute-start.20) | collective-permute-done | bytes 131104 | tf_op jit(solution)/shard_map/ppermute | solution.py:561
  56.5 3.8 %fetch.2 = (bf16[2048,768]{1,0:T(8,128)(2,1)S(1)}, bf16[2048,768]{1,0:T(8,128)(2,1)S(1)}, bf16[768,2048]{1,0:T(8,128)(2,1)S(1)}, f32[8,128]{1,0:T(8,128)S(1)}) custom-call(bf16[2048,768]{1,0:T(8,128)(2,1)} %bitcast.19, bf16[2048,768]{1,0:T(8,128)(2,1)} %bitcast.21, bf16[768,2048]{1,0:T(8,128)(2,1)} %bitcast.23), custom_call_target="tpu_custom_call" | custom-call | tf_op jit(solution)/shard_map/fetch/pallas_call | solution.py:402
  61.8 3.7 %collective-permute-done.23.refs_3_ = bf16[128,1024]{1,0:T(8,128)(2,1)S(1)} collective-permute-done((bf16[128,1024]{1,0:T(8,128)(2,1)S(1)}, bf16[128,1024]{1,0:T(8,128)(2,1)S(1)}, u32[]{:S(2)}, u32[]{:S(2)}) %collective-permute-start.23) | collective-permute-done | bytes 262176 | tf_op jit(solution)/shard_map/ppermute | solution.py:553
  65.5 1.8 %collective-permute-start.30 = (bf16[128,1024]{1,0:T(8,128)(2,1)S(1)}, bf16[128,1024]{1,0:T(8,128)(2,1)S(1)}, u32[]{:S(2)}, u32[]{:S(2)}) collective-permute-start(bf16[128,1024]{1,0:T(8,128)(2,1)S(1)} %collective-permute-done.23.refs_3_), channel_id=1, source_target_pairs={{0,2},{1,3},{2,0},{3,1},{4,6},{5,7},{6,4},{7,5},{8,10},{9,11},{10,... | collective-permute-start | bytes 786440 | tf_op jit(solution)/shard_map/ppermute | solution.py:553
  67.3 3.8 %fetch.3 = (bf16[2048,768]{1,0:T(8,128)(2,1)S(1)}, bf16[2048,768]{1,0:T(8,128)(2,1)S(1)}, bf16[768,2048]{1,0:T(8,128)(2,1)S(1)}, f32[8,128]{1,0:T(8,128)S(1)}) custom-call(bf16[2048,768]{1,0:T(8,128)(2,1)} %copy-done.3, bf16[2048,768]{1,0:T(8,128)(2,1)} %collective-permute-done.7.refs_1_, bf16[768,2048]{1,0:T(8,128)(2,1)} %collective-permute-done.11.refs_2_), custom_call_target="tpu_custom_call" | custom-call | tf_op jit(solution)/shard_map/fetch/pallas_call | solution.py:402
  73.1 3.8 %collective-permute-done.29.refs_1_ = bf16[128,1024]{1,0:T(8,128)(2,1)S(1)} collective-permute-done((bf16[128,1024]{1,0:T(8,128)(2,1)S(1)}, bf16[128,1024]{1,0:T(8,128)(2,1)S(1)}, u32[]{:S(2)}, u32[]{:S(2)}) %collective-permute-start.29) | collective-permute-done | bytes 262176 | tf_op jit(solution)/shard_map/ppermute | solution.py:553
  78.7 4.4 %experts.7 = (bf16[128,1024]{1,0:T(8,128)(2,1)S(1)}, bf16[128,1024]{1,0:T(8,128)(2,1)S(1)}, bf16[128,1024]{1,0:T(8,128)(2,1)S(1)}, bf16[128,1024]{1,0:T(8,128)(2,1)S(1)}) custom-call(f32[1,2048]{1,0:T(1,128)S(1)} %bitcast.14, s32[4,2,256]{2,1,0:T(2,128)S(1)} %get-tuple-element.164.slot_rows, s32[4,256,2]{2,1,0:T(8,128)S(1)} %get-tuple-element.165.slot_cols, ...), custom_call_target="tpu_custom_call" | custom-call | flops 2717908992 | bytes 18874368 | tf_op jit(solution)/shard_map/experts/pallas_call | solution.py:486
  83.1 1.8 %collective-permute-start.35 = (bf16[128,1024]{1,0:T(8,128)(2,1)S(1)}, bf16[128,1024]{1,0:T(8,128)(2,1)S(1)}, u32[]{:S(2)}, u32[]{:S(2)}) collective-permute-start(bf16[128,1024]{1,0:T(8,128)(2,1)S(1)} %get-tuple-element.206), channel_id=1, source_target_pairs={{0,2},{1,3},{2,0},{3,1},{4,6},{5,7},{6,4},{7,5},{8,10},{9,11},{10,... | collective-permute-start | bytes 786440 | tf_op jit(solution)/shard_map/ppermute | solution.py:553
  84.9 4.4 %experts.4 = (bf16[128,1024]{1,0:T(8,128)(2,1)S(1)}, bf16[128,1024]{1,0:T(8,128)(2,1)S(1)}, bf16[128,1024]{1,0:T(8,128)(2,1)S(1)}, bf16[128,1024]{1,0:T(8,128)(2,1)S(1)}) custom-call(f32[1,2048]{1,0:T(1,128)S(1)} %bitcast.15, s32[4,2,256]{2,1,0:T(2,128)S(1)} %get-tuple-element.164.slot_rows, s32[4,256,2]{2,1,0:T(8,128)S(1)} %get-tuple-element.165.slot_cols, ...), custom_call_target="tpu_custom_call" | custom-call | flops 2717908992 | bytes 18874368 | tf_op jit(solution)/shard_map/experts/pallas_call | solution.py:486
  89.3 1.7 %collective-permute-start.43 = (bf16[128,1024]{1,0:T(8,128)(2,1)S(1)}, bf16[128,1024]{1,0:T(8,128)(2,1)S(1)}, u32[]{:S(2)}, u32[]{:S(2)}) collective-permute-start(bf16[128,1024]{1,0:T(8,128)(2,1)S(1)} %get-tuple-element.224), channel_id=1, source_target_pairs={{0,4},{1,5},{2,6},{3,7},{4,8},{5,9},{6,10},{7,11},{8,12},{9,13},{1... | collective-permute-start | bytes 786440 | tf_op jit(solution)/shard_map/ppermute | solution.py:553
  91.3 1.6 %collective-permute-start.34 = (bf16[128,1024]{1,0:T(8,128)(2,1)S(1)}, bf16[128,1024]{1,0:T(8,128)(2,1)S(1)}, u32[]{:S(2)}, u32[]{:S(2)}) collective-permute-start(bf16[128,1024]{1,0:T(8,128)(2,1)S(1)} %collective-permute-done.31.refs_1_), channel_id=1, source_target_pairs={{0,2},{1,3},{2,0},{3,1},{4,6},{5,7},{6,4},{7,5},{8,10},{9,11},{10,... | collective-permute-start | bytes 786440 | tf_op jit(solution)/shard_map/ppermute | solution.py:553
  93.0 4.4 %experts.6 = (bf16[128,1024]{1,0:T(8,128)(2,1)S(1)}, bf16[128,1024]{1,0:T(8,128)(2,1)S(1)}, bf16[128,1024]{1,0:T(8,128)(2,1)S(1)}, bf16[128,1024]{1,0:T(8,128)(2,1)S(1)}) custom-call(f32[1,2048]{1,0:T(1,128)S(1)} %bitcast.16, s32[4,2,256]{2,1,0:T(2,128)S(1)} %get-tuple-element.164.slot_rows, s32[4,256,2]{2,1,0:T(8,128)S(1)} %get-tuple-element.165.slot_cols, ...), custom_call_target="tpu_custom_call" | custom-call | flops 2717908992 | bytes 18874368 | tf_op jit(solution)/shard_map/experts/pallas_call | solution.py:486
  97.9 1.8 %collective-permute-start.36 = (bf16[128,1024]{1,0:T(8,128)(2,1)S(1)}, bf16[128,1024]{1,0:T(8,128)(2,1)S(1)}, u32[]{:S(2)}, u32[]{:S(2)}) collective-permute-start(bf16[128,1024]{1,0:T(8,128)(2,1)S(1)} %add_convert_fusion.5), channel_id=1, source_target_pairs={{0,4},{1,5},{2,6},{3,7},{4,8},{5,9},{6,10},{7,11},{8,12},{9,13},{1... | collective-permute-start | bytes 786440 | tf_op jit(solution)/shard_map/ppermute | solution.py:553
  101.5 4.0 %collective-permute-done.33.refs_2_ = bf16[128,1024]{1,0:T(8,128)(2,1)S(1)} collective-permute-done((bf16[128,1024]{1,0:T(8,128)(2,1)S(1)}, bf16[128,1024]{1,0:T(8,128)(2,1)S(1)}, u32[]{:S(2)}, u32[]{:S(2)}) %collective-permute-start.33) | collective-permute-done | bytes 262176 | tf_op jit(solution)/shard_map/ppermute | solution.py:553
  105.5 4.4 %experts.5 = (bf16[128,1024]{1,0:T(8,128)(2,1)S(1)}, bf16[128,1024]{1,0:T(8,128)(2,1)S(1)}, bf16[128,1024]{1,0:T(8,128)(2,1)S(1)}, bf16[128,1024]{1,0:T(8,128)(2,1)S(1)}) custom-call(f32[1,2048]{1,0:T(1,128)S(1)} %bitcast.17, s32[4,2,256]{2,1,0:T(2,128)S(1)} %get-tuple-element.164.slot_rows, s32[4,256,2]{2,1,0:T(8,128)S(1)} %get-tuple-element.165.slot_cols, ...), custom_call_target="tpu_custom_call" | custom-call | flops 2717908992 | bytes 18874368 | tf_op jit(solution)/shard_map/experts/pallas_call | solution.py:486
  112.2 4.2 %collective-permute-done.42 = bf16[128,1024]{1,0:T(8,128)(2,1)S(1)} collective-permute-done((bf16[128,1024]{1,0:T(8,128)(2,1)S(1)}, bf16[128,1024]{1,0:T(8,128)(2,1)S(1)}, u32[]{:S(2)}, u32[]{:S(2)}) %collective-permute-start.42) | collective-permute-done | bytes 262176 | tf_op jit(solution)/shard_map/ppermute | solution.py:553
  120.0 2.1 %collective-permute-done.38 = bf16[128,1024]{1,0:T(8,128)(2,1)S(1)} collective-permute-done((bf16[128,1024]{1,0:T(8,128)(2,1)S(1)}, bf16[128,1024]{1,0:T(8,128)(2,1)S(1)}, u32[]{:S(2)}, u32[]{:S(2)}) %collective-permute-start.38) | collective-permute-done | bytes 262176 | tf_op jit(solution)/shard_map/ppermute | solution.py:553
  122.3 2.5 %collective-permute-done.46 = bf16[128,1024]{1,0:T(8,128)(2,1)S(1)} collective-permute-done((bf16[128,1024]{1,0:T(8,128)(2,1)S(1)}, bf16[128,1024]{1,0:T(8,128)(2,1)S(1)}, u32[]{:S(2)}, u32[]{:S(2)}) %collective-permute-start.46) | collective-permute-done | bytes 262176 | tf_op jit(solution)/shard_map/ppermute | solution.py:553
  124.8 2.9 %collective-permute-done.45 = bf16[128,1024]{1,0:T(8,128)(2,1)S(1)} collective-permute-done((bf16[128,1024]{1,0:T(8,128)(2,1)S(1)}, bf16[128,1024]{1,0:T(8,128)(2,1)S(1)}, u32[]{:S(2)}, u32[]{:S(2)}) %collective-permute-start.45) | collective-permute-done | bytes 262176 | tf_op jit(solution)/shard_map/ppermute | solution.py:553
  128.6 2.8 %collective-permute-done.48.refs_7_ = bf16[128,1024]{1,0:T(8,128)(2,1)S(1)} collective-permute-done((bf16[128,1024]{1,0:T(8,128)(2,1)S(1)}, bf16[128,1024]{1,0:T(8,128)(2,1)S(1)}, u32[]{:S(2)}, u32[]{:S(2)}) %collective-permute-start.48) | collective-permute-done | bytes 262176 | tf_op jit(solution)/shard_map/ppermute | solution.py:553
  131.4 1.8 %collective-permute-done.40.refs_2_ = bf16[128,1024]{1,0:T(8,128)(2,1)S(1)} collective-permute-done((bf16[128,1024]{1,0:T(8,128)(2,1)S(1)}, bf16[128,1024]{1,0:T(8,128)(2,1)S(1)}, u32[]{:S(2)}, u32[]{:S(2)}) %collective-permute-start.40) | collective-permute-done | bytes 262176 | tf_op jit(solution)/shard_map/ppermute | solution.py:553
  133.3 2.8 %collective-permute-done.47.refs_6_ = bf16[128,1024]{1,0:T(8,128)(2,1)S(1)} collective-permute-done((bf16[128,1024]{1,0:T(8,128)(2,1)S(1)}, bf16[128,1024]{1,0:T(8,128)(2,1)S(1)}, u32[]{:S(2)}, u32[]{:S(2)}) %collective-permute-start.47) | collective-permute-done | bytes 262176 | tf_op jit(solution)/shard_map/ppermute | solution.py:553
  (129 shorter events, 38.9 us)
Async XLA Ops:
  3.0 12.6 %collective-permute-start.3 = (bf16[2048,768]{1,0:T(8,128)(2,1)}, bf16[2048,768]{1,0:T(8,128)(2,1)S(1)}, u32[]{:S(2)}, u32[]{:S(2)}) collective-permute-start(bf16[2048,768]{1,0:T(8,128)(2,1)} %bitcast.18), channel_id=1, source_target_pairs={{0,1},{1,0},{2,3},{3,2},{4,5},{5,4},{6,7},{7,6},{8,9},{9,8},{10,11... | collective-permute-start | bytes 9437192 | tf_op jit(solution)/shard_map/ppermute | solution.py:553
  3.1 21.5 %collective-permute-start.7 = (bf16[2048,768]{1,0:T(8,128)(2,1)}, bf16[2048,768]{1,0:T(8,128)(2,1)}, u32[]{:S(2)}, u32[]{:S(2)}) collective-permute-start(bf16[2048,768]{1,0:T(8,128)(2,1)} %bitcast.20), channel_id=1, source_target_pairs={{0,1},{1,0},{2,3},{3,2},{4,5},{5,4},{6,7},{7,6},{8,9},{9,8},{10,11... | collective-permute-start | bytes 9437192 | tf_op jit(solution)/shard_map/ppermute | solution.py:553
  3.6 25.5 %collective-permute-start.11 = (bf16[768,2048]{1,0:T(8,128)(2,1)}, bf16[768,2048]{1,0:T(8,128)(2,1)}, u32[]{:S(2)}, u32[]{:S(2)}) collective-permute-start(bf16[768,2048]{1,0:T(8,128)(2,1)} %bitcast.22), channel_id=1, source_target_pairs={{0,1},{1,0},{2,3},{3,2},{4,5},{5,4},{6,7},{7,6},{8,9},{9,8},{10,11... | collective-permute-start | bytes 9437192 | tf_op jit(solution)/shard_map/ppermute | solution.py:553
  3.7 11.9 %collective-permute-start.1 = (bf16[272,512]{1,0:T(8,128)(2,1)S(1)}, bf16[272,512]{1,0:T(8,128)(2,1)S(1)}, u32[]{:S(2)}, u32[]{:S(2)}) collective-permute-start(bf16[272,512]{1,0:T(8,128)(2,1)S(1)} %pad_maximum_fusion.refs_8_.refs_0_), channel_id=1, source_target_pairs={{0,4},{1,5},{2,6},{3,7},{4,8},{5,9},{6,10},{7,11},{8,12},{9,13},{1... | collective-permute-start | bytes 835592 | tf_op jit(solution)/shard_map/ppermute | solution.py:553
  15.6 10.0 %collective-permute-start.4 = (bf16[272,512]{1,0:T(8,128)(2,1)S(1)}, bf16[272,512]{1,0:T(8,128)(2,1)S(1)}, u32[]{:S(2)}, u32[]{:S(2)}) collective-permute-start(bf16[272,512]{1,0:T(8,128)(2,1)S(1)} %collective-permute-done.1.refs_9_.refs_1_), channel_id=1, source_target_pairs={{0,4},{1,5},{2,6},{3,7},{4,8},{5,9},{6,10},{7,11},{8,12},{9,13},{1... | collective-permute-start | bytes 835592 | tf_op jit(solution)/shard_map/ppermute | solution.py:553
  27.0 10.6 %collective-permute-start.8 = (bf16[272,512]{1,0:T(8,128)(2,1)S(1)}, bf16[272,512]{1,0:T(8,128)(2,1)S(1)}, u32[]{:S(2)}, u32[]{:S(2)}) collective-permute-start(bf16[272,512]{1,0:T(8,128)(2,1)S(1)} %collective-permute-done.4.refs_10_.refs_4_), channel_id=1, source_target_pairs={{0,4},{1,5},{2,6},{3,7},{4,8},{5,9},{6,10},{7,11},{8,12},{9,13},{1... | collective-permute-start | bytes 835592 | tf_op jit(solution)/shard_map/ppermute | solution.py:553
  48.2 12.1 %collective-permute-start.21 = (bf16[128,1024]{1,0:T(8,128)(2,1)S(1)}, bf16[128,1024]{1,0:T(8,128)(2,1)S(1)}, u32[]{:S(2)}, u32[]{:S(2)}) collective-permute-start(bf16[128,1024]{1,0:T(8,128)(2,1)S(1)} %get-tuple-element.167.refs_0_), channel_id=1, source_target_pairs={{0,4},{1,5},{2,6},{3,7},{4,8},{5,9},{6,10},{7,11},{8,12},{9,13},{1... | collective-permute-start | bytes 786440 | tf_op jit(solution)/shard_map/ppermute | solution.py:553
  48.7 11.6 %collective-permute-start.22 = (bf16[128,1024]{1,0:T(8,128)(2,1)S(1)}, bf16[128,1024]{1,0:T(8,128)(2,1)S(1)}, u32[]{:S(2)}, u32[]{:S(2)}) collective-permute-start(bf16[128,1024]{1,0:T(8,128)(2,1)S(1)} %get-tuple-element.167.refs_0_), channel_id=1, source_target_pairs={{0,2},{1,3},{2,0},{3,1},{4,6},{5,7},{6,4},{7,5},{8,10},{9,11},{10,... | collective-permute-start | bytes 786440 | tf_op jit(solution)/shard_map/ppermute | solution.py:553
  54.6 10.8 %collective-permute-start.23 = (bf16[128,1024]{1,0:T(8,128)(2,1)S(1)}, bf16[128,1024]{1,0:T(8,128)(2,1)S(1)}, u32[]{:S(2)}, u32[]{:S(2)}) collective-permute-start(bf16[128,1024]{1,0:T(8,128)(2,1)S(1)} %get-tuple-element.168.refs_1_), channel_id=1, source_target_pairs={{0,4},{1,5},{2,6},{3,7},{4,8},{5,9},{6,10},{7,11},{8,12},{9,13},{1... | collective-permute-start | bytes 786440 | tf_op jit(solution)/shard_map/ppermute | solution.py:553
  55.1 10.4 %collective-permute-start.24 = (bf16[128,1024]{1,0:T(8,128)(2,1)S(1)}, bf16[128,1024]{1,0:T(8,128)(2,1)S(1)}, u32[]{:S(2)}, u32[]{:S(2)}) collective-permute-start(bf16[128,1024]{1,0:T(8,128)(2,1)S(1)} %get-tuple-element.168.refs_1_), channel_id=1, source_target_pairs={{0,2},{1,3},{2,0},{3,1},{4,6},{5,7},{6,4},{7,5},{8,10},{9,11},{10,... | collective-permute-start | bytes 786440 | tf_op jit(solution)/shard_map/ppermute | solution.py:553
  60.3 11.0 %collective-permute-start.25 = (bf16[128,1024]{1,0:T(8,128)(2,1)S(1)}, bf16[128,1024]{1,0:T(8,128)(2,1)S(1)}, u32[]{:S(2)}, u32[]{:S(2)}) collective-permute-start(bf16[128,1024]{1,0:T(8,128)(2,1)S(1)} %collective-permute-done.21.refs_2_), channel_id=1, source_target_pairs={{0,4},{1,5},{2,6},{3,7},{4,8},{5,9},{6,10},{7,11},{8,12},{9,13},{1... | collective-permute-start | bytes 786440 | tf_op jit(solution)/shard_map/ppermute | solution.py:553
  61.5 9.8 %collective-permute-start.26 = (bf16[128,1024]{1,0:T(8,128)(2,1)S(1)}, bf16[128,1024]{1,0:T(8,128)(2,1)S(1)}, u32[]{:S(2)}, u32[]{:S(2)}) collective-permute-start(bf16[128,1024]{1,0:T(8,128)(2,1)S(1)} %collective-permute-done.21.refs_2_), channel_id=1, source_target_pairs={{0,2},{1,3},{2,0},{3,1},{4,6},{5,7},{6,4},{7,5},{8,10},{9,11},{10,... | collective-permute-start | bytes 786440 | tf_op jit(solution)/shard_map/ppermute | solution.py:553
  65.5 11.4 %collective-permute-start.29 = (bf16[128,1024]{1,0:T(8,128)(2,1)S(1)}, bf16[128,1024]{1,0:T(8,128)(2,1)S(1)}, u32[]{:S(2)}, u32[]{:S(2)}) collective-permute-start(bf16[128,1024]{1,0:T(8,128)(2,1)S(1)} %collective-permute-done.23.refs_3_), channel_id=1, source_target_pairs={{0,4},{1,5},{2,6},{3,7},{4,8},{5,9},{6,10},{7,11},{8,12},{9,13},{1... | collective-permute-start | bytes 786440 | tf_op jit(solution)/shard_map/ppermute | solution.py:553
  65.5 11.4 %collective-permute-start.30 = (bf16[128,1024]{1,0:T(8,128)(2,1)S(1)}, bf16[128,1024]{1,0:T(8,128)(2,1)S(1)}, u32[]{:S(2)}, u32[]{:S(2)}) collective-permute-start(bf16[128,1024]{1,0:T(8,128)(2,1)S(1)} %collective-permute-done.23.refs_3_), channel_id=1, source_target_pairs={{0,2},{1,3},{2,0},{3,1},{4,6},{5,7},{6,4},{7,5},{8,10},{9,11},{10,... | collective-permute-start | bytes 786440 | tf_op jit(solution)/shard_map/ppermute | solution.py:553
  71.3 18.0 %collective-permute-start.27 = (bf16[128,1024]{1,0:T(8,128)(2,1)S(1)}, bf16[128,1024]{1,0:T(8,128)(2,1)S(1)}, u32[]{:S(2)}, u32[]{:S(2)}) collective-permute-start(bf16[128,1024]{1,0:T(8,128)(2,1)S(1)} %collective-permute-done.25.refs_0_), channel_id=1, source_target_pairs={{0,4},{1,5},{2,6},{3,7},{4,8},{5,9},{6,10},{7,11},{8,12},{9,13},{1... | collective-permute-start | bytes 786440 | tf_op jit(solution)/shard_map/ppermute | solution.py:553
  72.8 18.2 %collective-permute-start.28 = (bf16[128,1024]{1,0:T(8,128)(2,1)S(1)}, bf16[128,1024]{1,0:T(8,128)(2,1)S(1)}, u32[]{:S(2)}, u32[]{:S(2)}) collective-permute-start(bf16[128,1024]{1,0:T(8,128)(2,1)S(1)} %collective-permute-done.25.refs_0_), channel_id=1, source_target_pairs={{0,2},{1,3},{2,0},{3,1},{4,6},{5,7},{6,4},{7,5},{8,10},{9,11},{10,... | collective-permute-start | bytes 786440 | tf_op jit(solution)/shard_map/ppermute | solution.py:553
  76.9 14.1 %collective-permute-start.31 = (bf16[128,1024]{1,0:T(8,128)(2,1)S(1)}, bf16[128,1024]{1,0:T(8,128)(2,1)S(1)}, u32[]{:S(2)}, u32[]{:S(2)}) collective-permute-start(bf16[128,1024]{1,0:T(8,128)(2,1)S(1)} %collective-permute-done.29.refs_1_), channel_id=1, source_target_pairs={{0,4},{1,5},{2,6},{3,7},{4,8},{5,9},{6,10},{7,11},{8,12},{9,13},{1... | collective-permute-start | bytes 786440 | tf_op jit(solution)/shard_map/ppermute | solution.py:553
  78.4 12.6 %collective-permute-start.32 = (bf16[128,1024]{1,0:T(8,128)(2,1)S(1)}, bf16[128,1024]{1,0:T(8,128)(2,1)S(1)}, u32[]{:S(2)}, u32[]{:S(2)}) collective-permute-start(bf16[128,1024]{1,0:T(8,128)(2,1)S(1)} %collective-permute-done.29.refs_1_), channel_id=1, source_target_pairs={{0,2},{1,3},{2,0},{3,1},{4,6},{5,7},{6,4},{7,5},{8,10},{9,11},{10,... | collective-permute-start | bytes 786440 | tf_op jit(solution)/shard_map/ppermute | solution.py:553
  83.1 14.8 %collective-permute-start.35 = (bf16[128,1024]{1,0:T(8,128)(2,1)S(1)}, bf16[128,1024]{1,0:T(8,128)(2,1)S(1)}, u32[]{:S(2)}, u32[]{:S(2)}) collective-permute-start(bf16[128,1024]{1,0:T(8,128)(2,1)S(1)} %get-tuple-element.206), channel_id=1, source_target_pairs={{0,2},{1,3},{2,0},{3,1},{4,6},{5,7},{6,4},{7,5},{8,10},{9,11},{10,... | collective-permute-start | bytes 786440 | tf_op jit(solution)/shard_map/ppermute | solution.py:553
  89.3 10.6 %collective-permute-start.43 = (bf16[128,1024]{1,0:T(8,128)(2,1)S(1)}, bf16[128,1024]{1,0:T(8,128)(2,1)S(1)}, u32[]{:S(2)}, u32[]{:S(2)}) collective-permute-start(bf16[128,1024]{1,0:T(8,128)(2,1)S(1)} %get-tuple-element.224), channel_id=1, source_target_pairs={{0,4},{1,5},{2,6},{3,7},{4,8},{5,9},{6,10},{7,11},{8,12},{9,13},{1... | collective-permute-start | bytes 786440 | tf_op jit(solution)/shard_map/ppermute | solution.py:553
  91.0 14.5 %collective-permute-start.33 = (bf16[128,1024]{1,0:T(8,128)(2,1)S(1)}, bf16[128,1024]{1,0:T(8,128)(2,1)S(1)}, u32[]{:S(2)}, u32[]{:S(2)}) collective-permute-start(bf16[128,1024]{1,0:T(8,128)(2,1)S(1)} %collective-permute-done.28.refs_2_), channel_id=1, source_target_pairs={{0,4},{1,5},{2,6},{3,7},{4,8},{5,9},{6,10},{7,11},{8,12},{9,13},{1... | collective-permute-start | bytes 786440 | tf_op jit(solution)/shard_map/ppermute | solution.py:553
  91.3 14.1 %collective-permute-start.34 = (bf16[128,1024]{1,0:T(8,128)(2,1)S(1)}, bf16[128,1024]{1,0:T(8,128)(2,1)S(1)}, u32[]{:S(2)}, u32[]{:S(2)}) collective-permute-start(bf16[128,1024]{1,0:T(8,128)(2,1)S(1)} %collective-permute-done.31.refs_1_), channel_id=1, source_target_pairs={{0,2},{1,3},{2,0},{3,1},{4,6},{5,7},{6,4},{7,5},{8,10},{9,11},{10,... | collective-permute-start | bytes 786440 | tf_op jit(solution)/shard_map/ppermute | solution.py:553
  97.4 13.4 %collective-permute-start.37 = (bf16[128,1024]{1,0:T(8,128)(2,1)S(1)}, bf16[128,1024]{1,0:T(8,128)(2,1)S(1)}, u32[]{:S(2)}, u32[]{:S(2)}) collective-permute-start(bf16[128,1024]{1,0:T(8,128)(2,1)S(1)} %get-tuple-element.209), channel_id=1, source_target_pairs={{0,2},{1,3},{2,0},{3,1},{4,6},{5,7},{6,4},{7,5},{8,10},{9,11},{10,... | collective-permute-start | bytes 786440 | tf_op jit(solution)/shard_map/ppermute | solution.py:553
  97.9 12.9 %collective-permute-start.36 = (bf16[128,1024]{1,0:T(8,128)(2,1)S(1)}, bf16[128,1024]{1,0:T(8,128)(2,1)S(1)}, u32[]{:S(2)}, u32[]{:S(2)}) collective-permute-start(bf16[128,1024]{1,0:T(8,128)(2,1)S(1)} %add_convert_fusion.5), channel_id=1, source_target_pairs={{0,4},{1,5},{2,6},{3,7},{4,8},{5,9},{6,10},{7,11},{8,12},{9,13},{1... | collective-permute-start | bytes 786440 | tf_op jit(solution)/shard_map/ppermute | solution.py:553
  99.9 12.3 %collective-permute-start.44 = (bf16[128,1024]{1,0:T(8,128)(2,1)S(1)}, bf16[128,1024]{1,0:T(8,128)(2,1)S(1)}, u32[]{:S(2)}, u32[]{:S(2)}) collective-permute-start(bf16[128,1024]{1,0:T(8,128)(2,1)S(1)} %add_convert_fusion.2), channel_id=1, source_target_pairs={{0,2},{1,3},{2,0},{3,1},{4,6},{5,7},{6,4},{7,5},{8,10},{9,11},{10,... | collective-permute-start | bytes 786440 | tf_op jit(solution)/shard_map/ppermute | solution.py:553
  105.5 11.0 %collective-permute-start.42 = (bf16[128,1024]{1,0:T(8,128)(2,1)S(1)}, bf16[128,1024]{1,0:T(8,128)(2,1)S(1)}, u32[]{:S(2)}, u32[]{:S(2)}) collective-permute-start(bf16[128,1024]{1,0:T(8,128)(2,1)S(1)} %get-tuple-element.222), channel_id=1, source_target_pairs={{0,4},{1,5},{2,6},{3,7},{4,8},{5,9},{6,10},{7,11},{8,12},{9,13},{1... | collective-permute-start | bytes 786440 | tf_op jit(solution)/shard_map/ppermute | solution.py:553
  110.9 11.1 %collective-permute-start.38 = (bf16[128,1024]{1,0:T(8,128)(2,1)S(1)}, bf16[128,1024]{1,0:T(8,128)(2,1)S(1)}, u32[]{:S(2)}, u32[]{:S(2)}) collective-permute-start(bf16[128,1024]{1,0:T(8,128)(2,1)S(1)} %add_convert_fusion.4), channel_id=1, source_target_pairs={{0,4},{1,5},{2,6},{3,7},{4,8},{5,9},{6,10},{7,11},{8,12},{9,13},{1... | collective-permute-start | bytes 786440 | tf_op jit(solution)/shard_map/ppermute | solution.py:553
  111.8 13.0 %collective-permute-start.46 = (bf16[128,1024]{1,0:T(8,128)(2,1)S(1)}, bf16[128,1024]{1,0:T(8,128)(2,1)S(1)}, u32[]{:S(2)}, u32[]{:S(2)}) collective-permute-start(bf16[128,1024]{1,0:T(8,128)(2,1)S(1)} %get-tuple-element.227), channel_id=1, source_target_pairs={{0,2},{1,3},{2,0},{3,1},{4,6},{5,7},{6,4},{7,5},{8,10},{9,11},{10,... | collective-permute-start | bytes 786440 | tf_op jit(solution)/shard_map/ppermute | solution.py:553
  116.6 11.1 %collective-permute-start.45 = (bf16[128,1024]{1,0:T(8,128)(2,1)S(1)}, bf16[128,1024]{1,0:T(8,128)(2,1)S(1)}, u32[]{:S(2)}, u32[]{:S(2)}) collective-permute-start(bf16[128,1024]{1,0:T(8,128)(2,1)S(1)} %add_convert_fusion.1), channel_id=1, source_target_pairs={{0,4},{1,5},{2,6},{3,7},{4,8},{5,9},{6,10},{7,11},{8,12},{9,13},{1... | collective-permute-start | bytes 786440 | tf_op jit(solution)/shard_map/ppermute | solution.py:553
  116.7 12.0 %collective-permute-start.41 = (bf16[128,1024]{1,0:T(8,128)(2,1)S(1)}, bf16[128,1024]{1,0:T(8,128)(2,1)S(1)}, u32[]{:S(2)}, u32[]{:S(2)}) collective-permute-start(bf16[128,1024]{1,0:T(8,128)(2,1)S(1)} %get-tuple-element.217), channel_id=1, source_target_pairs={{0,2},{1,3},{2,0},{3,1},{4,6},{5,7},{6,4},{7,5},{8,10},{9,11},{10,... | collective-permute-start | bytes 786440 | tf_op jit(solution)/shard_map/ppermute | solution.py:553
  119.2 12.2 %collective-permute-start.48 = (bf16[128,1024]{1,0:T(8,128)(2,1)S(1)}, bf16[128,1024]{1,0:T(8,128)(2,1)S(1)}, u32[]{:S(2)}, u32[]{:S(2)}) collective-permute-start(bf16[128,1024]{1,0:T(8,128)(2,1)S(1)} %get-tuple-element.228), channel_id=1, source_target_pairs={{0,2},{1,3},{2,0},{3,1},{4,6},{5,7},{6,4},{7,5},{8,10},{9,11},{10,... | collective-permute-start | bytes 786440 | tf_op jit(solution)/shard_map/ppermute | solution.py:553
  122.2 11.1 %collective-permute-start.40 = (bf16[128,1024]{1,0:T(8,128)(2,1)S(1)}, bf16[128,1024]{1,0:T(8,128)(2,1)S(1)}, u32[]{:S(2)}, u32[]{:S(2)}) collective-permute-start(bf16[128,1024]{1,0:T(8,128)(2,1)S(1)} %add_convert_fusion.3), channel_id=1, source_target_pairs={{0,4},{1,5},{2,6},{3,7},{4,8},{5,9},{6,10},{7,11},{8,12},{9,13},{1... | collective-permute-start | bytes 786440 | tf_op jit(solution)/shard_map/ppermute | solution.py:553
  (35 other events, 253.3 us)
